TPU v7x, 32 devices: a whole 2x2x4 slice. The times are simulated.
32 devices in a mesh: member: 2 (over y), tile: 4 (over z), sub: 2 (over x), comp: 2 (over core).
Axes of the slice: x: 2, y: 2, z: 4, core: 2. Of those that a mesh axis runs over, the one named last changes fastest.
Arguments:
- air_exchanges: bfloat16 [4, 8, 131072], P(('member', 'comp'), None, ('tile', 'sub')), parts along dimension 0, may hold values from -6 to 6
- air_destination: int32 [2, 131072, 1], P('comp', ('tile', 'sub')), may hold values from 0 to 7, as said below
- diagonal_group_pointer: int32 [2, 4, 2, 64, 2], P('comp', 'tile', 'sub'), may hold values from 0 to 319
- interpolation_factors: bfloat16 [2, 4, 2, 64, 2, 128, 128], P('comp', 'tile', 'sub'), may hold values from -0.375 to 0.375
- marine_fields: float32 [4, 3, 256, 256], P(('member', 'comp'), None, 'tile', 'sub'), parts along dimension 0, may hold values from -6 to 6
- skin_warmth_anomaly: float32 [4, 256, 256], P(('member', 'comp'), 'tile', 'sub'), parts along dimension 0, may hold values from -6 to 6
- gravity_bathymetry: float32 [2, 256, 256], P('comp', 'tile', 'sub'), may hold values from 0.1 to 0.9
- marine_indicator: int32 [2, 256, 256], P('comp', 'tile', 'sub'), may hold values 0 or 1
Outputs:
- ocean_out: float32 [4, 3, 256, 256], P(('member', 'comp'), None, 'tile', 'sub'), parts along dimension 0
- atm_sst: float32 [4, 131072], P(('member', 'comp'), ('tile', 'sub')), parts along dimension 0
There are 2 independent parts, one for each index of `member`. A program takes and returns all parts, laid end to end along the dimension named above; an argument that names none is the same for every part. Nothing has to cross between parts.
Inputs may be any that keep to these rules, and one draw needn't show every extreme that they name: `air_destination`: the ocean tile t * 2 + s that atmosphere column i intersects; with source = i // 16384, it is (source + o) mod 8 for some o with |o| <= 2. Among the 16384 columns of one device no tile is named more than 8192 times, and in every basin some device's columns name one tile exactly 8192 times.
All inputs are finite; a program needn't handle non-finite values. No bound on the sum of `marine_indicator` on one device may be relied on, other than what follows from the above.
Results may differ from a plain program's by a relative error of at most 0.0028.
Values may be sent and summed in bfloat16 or wider, within the bound.
No kernel may reach another device: no remote copies, remote signals or barrier semaphores. Data moves between devices by JAX's collectives and lax.ppermute only.
A program may use at most 128 MiB of HBM per device.

v0:
```python
import jax
import jax.numpy as jnp
from jax import lax
from jax.sharding import PartitionSpec as P

NEIGHBOR_TILES = 5
SUBS = 8


def passed_along(block, axis, distance):
    devices = range(lax.axis_size(axis))
    route = [((i - distance) % len(devices), i) for i in devices]
    return lax.ppermute(block, axis, route)


def padded_2(block, sides, width):
    for axis, dim in sides:
        count = lax.axis_size(axis)
        forward = [(i, i + 1) for i in range(count - 1)]
        backward = [(target, source) for source, target in forward]
        low = lax.ppermute(
            lax.slice_in_dim(block, block.shape[dim] - width, None, axis=dim), axis, forward
        )
        high = lax.ppermute(lax.slice_in_dim(block, 0, width, axis=dim), axis, backward)
        block = jnp.concatenate([low, block, high], axis=dim)
    return block


def column_ranks(offsets, slot_kinds):
    column_count = offsets.shape[0]
    breadth = 128
    onehot = (offsets[:, None] == jnp.arange(slot_kinds, dtype=jnp.int32)[None, :]).astype(
        jnp.float32
    )
    blocked = onehot.reshape(column_count // breadth, breadth, slot_kinds)
    lower_mask = (jnp.arange(breadth)[:, None] > jnp.arange(breadth)[None, :]).astype(jnp.float32)
    inside_count = jnp.einsum("ij,bjo->bio", lower_mask, blocked, precision=lax.Precision.HIGHEST)
    totals = jnp.sum(blocked, axis=1)
    block_count = totals.shape[0]
    earlier = (jnp.arange(block_count)[:, None] > jnp.arange(block_count)[None, :]).astype(
        jnp.float32
    )
    carried = jnp.dot(earlier, totals, precision=lax.Precision.HIGHEST)
    before = inside_count + carried[:, None, :]
    return jnp.sum(before * blocked, axis=2).reshape(column_count).astype(jnp.int32)


def difference_x(values):
    padded = jnp.pad(values, ((0, 0), (1, 1)))
    return 0.5 * (padded[:, 2:] - padded[:, :-2])


def difference_y(values):
    padded = jnp.pad(values, ((1, 1), (0, 0)))
    return 0.5 * (padded[2:, :] - padded[:-2, :])


def surface_forcing(fields):
    wind_speed = jnp.sqrt(fields[0] * fields[0] + fields[1] * fields[1] + 1.0)
    stress_x = 0.2 * wind_speed * fields[0]
    stress_y = 0.2 * wind_speed * fields[1]
    freshwater = 0.5 * (fields[3] - fields[2])
    thermal_forcing = fields[7] + fields[6] - fields[4] - fields[5]
    return (stress_x, stress_y, freshwater, thermal_forcing)


def barotropic_step(ocean_now, statics, coriolis):
    height, east_flow, north_flow = ocean_now
    liquid_indicator, depth_map, stress_x, stress_y, freshwater = statics
    height = liquid_indicator * (
        height - (difference_x(east_flow) + difference_y(north_flow)) + freshwater
    )
    slope_x = difference_x(height)
    slope_y = difference_y(height)
    new_east = liquid_indicator * (
        east_flow + coriolis * north_flow - depth_map * slope_x + stress_x
    )
    new_north = liquid_indicator * (
        north_flow - coriolis * east_flow - depth_map * slope_y + stress_y
    )
    return (height, new_east, new_north)


def remap_forward(received, narrow_longitudes, intersect_factor):
    field_count = received.shape[0]
    grouped = received.reshape(field_count, -1, intersect_factor.shape[2]).transpose(1, 0, 2)
    blocks = grouped[narrow_longitudes]
    result = jnp.einsum(
        "kwab,kwfb->fka", intersect_factor, blocks, preferred_element_type=jnp.float32
    )
    return result.reshape(field_count, -1)


def backward_interpolation(departing_warmth, narrow_longitudes, intersect_factor, group_total):
    group_breadth = intersect_factor.shape[2]
    exchange_shares = jnp.einsum(
        "ylub,yu->ylb",
        intersect_factor,
        departing_warmth.reshape(-1, group_breadth),
        preferred_element_type=jnp.float32,
    )
    select = (
        narrow_longitudes[:, :, None] == jnp.arange(group_total, dtype=jnp.int32)[None, None, :]
    ).astype(jnp.float32)
    return jnp.einsum(
        "kwc,kwb->cb", select, exchange_shares, precision=lax.Precision.HIGHEST
    ).reshape(-1)


def shards(
    air_exchanges,
    air_destination,
    diagonal_group_pointer,
    interpolation_factors,
    marine_fields,
    skin_warmth_anomaly,
    gravity_bathymetry,
    marine_indicator,
):
    latitudes_each_parcel = lax.axis_size("tile")
    longitudes_each_parcel = lax.axis_size("sub")
    parcel_total = latitudes_each_parcel * longitudes_each_parcel
    column_count = air_destination.shape[1]
    slot_limit = column_count // 2
    middle = NEIGHBOR_TILES // 2
    my_tile = lax.axis_index("tile") * longitudes_each_parcel + lax.axis_index("sub")
    destination_listing = air_destination[0, :, 0]
    offsets = jnp.mod(destination_listing - my_tile + middle, parcel_total)
    ranking = column_ranks(offsets, NEIGHBOR_TILES)
    flat_slot = offsets * slot_limit + ranking
    fluxes = air_exchanges[0]
    field_count = fluxes.shape[0]
    slot_source = (
        jnp.full((NEIGHBOR_TILES * slot_limit,), column_count, jnp.int32)
        .at[flat_slot]
        .set(jnp.arange(column_count, dtype=jnp.int32))
    )
    padded_fields = jnp.concatenate([fluxes, jnp.zeros((field_count, 1), jnp.bfloat16)], axis=1)
    outbound = padded_fields[:, slot_source].reshape(field_count, NEIGHBOR_TILES, slot_limit)
    arrived = [None] * NEIGHBOR_TILES
    arrived[middle] = outbound[:, middle]
    for slot in range(NEIGHBOR_TILES):
        if slot != middle:
            arrived[slot] = passed_along(outbound[:, slot], ("tile", "sub"), slot - middle)
    received = jnp.stack(arrived, axis=1).reshape(field_count, NEIGHBOR_TILES * slot_limit)
    narrow_longitudes = diagonal_group_pointer[0, 0, 0]
    intersect_factor = interpolation_factors[0, 0, 0]
    group_breadth = intersect_factor.shape[2]
    parcel_latitudes = skin_warmth_anomaly.shape[1]
    parcel_longitudes = skin_warmth_anomaly.shape[2]
    remapped = remap_forward(received, narrow_longitudes, intersect_factor).reshape(
        field_count, parcel_latitudes, parcel_longitudes
    )
    stress_x, stress_y, freshwater, thermal_forcing = surface_forcing(remapped)
    liquid_indicator = marine_indicator[0].astype(jnp.float32)
    depth_map = gravity_bathymetry[0]
    departing_warmth = (skin_warmth_anomaly[0] + 0.25 * liquid_indicator * thermal_forcing).astype(
        jnp.bfloat16
    )
    sent_back_results = backward_interpolation(
        departing_warmth.reshape(-1),
        narrow_longitudes,
        intersect_factor,
        NEIGHBOR_TILES * slot_limit // group_breadth,
    ).reshape(NEIGHBOR_TILES, slot_limit)
    homeward = [None] * NEIGHBOR_TILES
    homeward[middle] = sent_back_results[middle]
    for slot in range(NEIGHBOR_TILES):
        if slot != middle:
            homeward[slot] = passed_along(sent_back_results[slot], ("tile", "sub"), middle - slot)
    backward = jnp.stack(homeward).reshape(-1)
    atm_temp = backward[flat_slot][None, :]
    total_rows = parcel_latitudes * latitudes_each_parcel
    first_row = lax.axis_index("tile") * parcel_latitudes
    height = marine_fields[0, 0]
    east_flow = marine_fields[0, 1]
    north_flow = marine_fields[0, 2]
    margin_steps = 4
    reach = 2 * margin_steps
    stacked = padded_2(
        jnp.stack([liquid_indicator, depth_map, stress_x, stress_y, freshwater]),
        (("tile", 1), ("sub", 2)),
        reach,
    )
    statics = (stacked[0], stacked[1], stacked[2], stacked[3], stacked[4])
    wide_rows = first_row - reach + jnp.arange(parcel_latitudes + 2 * reach, dtype=jnp.int32)
    coriolis = (0.1 + 0.2 * (wide_rows.astype(jnp.float32) + 0.5) / total_rows)[:, None]
    for start in range(0, SUBS, margin_steps):
        widened = padded_2(
            jnp.stack([height, east_flow, north_flow]), (("tile", 1), ("sub", 2)), reach
        )
        ocean_now = (widened[0], widened[1], widened[2])
        for counter in range(min(margin_steps, SUBS - start)):
            ocean_now = barotropic_step(ocean_now, statics, coriolis)
        height = ocean_now[0][reach:-reach, reach:-reach]
        east_flow = ocean_now[1][reach:-reach, reach:-reach]
        north_flow = ocean_now[2][reach:-reach, reach:-reach]
    ocean_out = jnp.stack([height, east_flow, north_flow])[None]
    return (ocean_out, atm_temp)


def solution(mesh):
    return jax.shard_map(
        shards,
        mesh=mesh,
        in_specs=(
            P(("member", "comp"), None, ("tile", "sub")),
            P("comp", ("tile", "sub"), None),
            P("comp", "tile", "sub", None, None),
            P("comp", "tile", "sub", None, None, None, None),
            P(("member", "comp"), None, "tile", "sub"),
            P(("member", "comp"), "tile", "sub"),
            P("comp", "tile", "sub"),
            P("comp", "tile", "sub"),
        ),
        out_specs=(
            P(("member", "comp"), None, "tile", "sub"),
            P(("member", "comp"), ("tile", "sub")),
        ),
        check_vma=False,
    )
```

profile of v0, /device:TPU:0, one launch (start us, length us, event | category | flops | bytes accessed | tf_op | source)
XLA Modules:
  0.0 465.4 jit_solution(15447866363872143955)
XLA Ops:
  0.6 0.9 subtract_add_fusion
  1.6 0.1 convert_reduce_fusion
  1.7 0.1 fusion.129
  1.8 0.3 fusion.9
  2.2 1.2 compare_select_fusion.1
  3.3 60.4 %scatter_custom_fusion = s32[40960]{0:T(1024)S(1)} fusion(s32[16384]{0:T(1024)S(1)} %bitcast.208, s32[16384]{0:T(1024)S(1)} %iota.33, s32[]{:T(128)} %constant.23.clone.1), kind=kCustom, calls=%fused_computation.40 | custom fusion | bytes 163844 | tf_op jit(solution)/shard_map/scatter | solution.py:136
  63.8 4.0 copy.213
  67.8 5.4 %concatenate.21 = bf16[8,16385]{0,1:T(8,128)(2,1)} pad(bf16[8,16384]{0,1:T(8,128)(2,1)} %bitcast.187, bf16[]{:T(256)} %constant.22.clone.1), padding=0_0x0_1 | pad | bytes 524306 | tf_op jit(solution)/shard_map/concatenate | solution.py:138
  73.2 139.3 %gather_fusion = bf16[40960,8]{1,0:T(8,128)(2,1)} fusion(bf16[8,16385]{0,1:T(8,128)(2,1)} %concatenate.21, s32[40960]{0:T(1024)S(1)} %fusion.10), kind=kCustom, calls=%fused_computation | custom fusion | bytes 1474560 | tf_op jit(solution)/shard_map/gather | solution.py:139
  212.5 7.4 %fusion.139 = (bf16[8,1,8192]{0,2,1:T(8,128)(2,1)S(1)}, bf16[8,1,8192]{0,2,1:T(8,128)(2,1)}, bf16[8,1,8192]{0,2,1:T(8,128)(2,1)}, bf16[8,1,8192]{0,2,1:T(8,128)(2,1)}, bf16[8,1,8192]{0,2,1:T(8,128)(2,1)}) fusion(bf16[8,5,8192]{0,2,1:T(8,128)(2,1)} %bitcast.188), kind=kLoop, calls=%fused_computation.249 | loop fusion | bytes 1310720 | tf_op jit(solution)/shard_map/slice | solution.py:144
  219.9 2.5 copy.235
  222.4 5.0 %collective-permute-start = (bf16[8,8192]{1,0:T(8,128)(2,1)}, bf16[8,8192]{1,0:T(8,128)(2,1)}, u32[]{:S(2)}, u32[]{:S(2)}) collective-permute-start(bf16[8,8192]{1,0:T(8,128)(2,1)} %bitcast.9), channel_id=1, source_target_pairs={{4,0},{6,2},{8,4},{10,6},{12,8},{14,10},{0,12},{2,14},{5,1},{7,3},... | collective-permute-start | bytes 393224 | tf_op jit(solution)/shard_map/ppermute | solution.py:13
  227.5 2.5 copy.236
  230.0 1.4 collective-permute-start.1
  231.3 2.5 copy.238
  233.8 0.6 collective-permute-start.2
  234.9 2.8 collective-permute-start.8
  237.8 1.3 collective-permute-start.9
  239.2 0.1 reshape.179
  239.4 2.0 collective-permute-done.8
  241.3 4.1 collective-permute-done.9
  245.6 2.9 collective-permute-start.10
  248.5 1.3 collective-permute-start.11
  249.8 1.8 copy.237
  251.6 0.8 copy.239
  252.5 1.8 collective-permute-start.3
  254.3 0.2 pad_maximum_fusion.1
  254.5 0.9 bitcast_dynamic-update-slice_fusion.3
  255.4 0.9 bitcast_dynamic-update-slice_fusion.2
  256.4 0.9 bitcast_dynamic-update-slice_fusion.1
  257.3 1.9 collective-permute-done.3
  259.3 0.7 gather_fusion.1
  260.0 3.5 fusion.6
  263.7 1.9 collective-permute-start.4
  265.6 1.3 collective-permute-start.5
  266.9 0.7 fusion
  267.6 3.7 collective-permute-done.5
  271.4 4.6 collective-permute-start.6
  276.0 1.3 collective-permute-start.7
  277.3 0.4 convolution_bitcast_fusion
  277.7 1.5 collective-permute-done.6
  279.2 4.4 collective-permute-done.7
  283.6 0.2 pad_maximum_fusion
  284.4 0.1 fusion.20
  284.5 0.1 add_multiply_fusion.5
  284.7 0.1 add_multiply_fusion.4
  284.9 0.1 fusion.44
  285.0 0.1 add_multiply_fusion.3
  285.1 0.1 fusion.56
  285.3 0.3 fusion.126
  285.7 3.8 collective-permute-start.12
  289.6 1.3 collective-permute-start.13
  290.9 2.7 collective-permute-start.16
  293.6 4.7 %collective-permute-start.18 = (f32[8192]{0:T(1024)S(1)}, f32[8192]{0:T(1024)S(1)}, u32[]{:S(2)}, u32[]{:S(2)}) collective-permute-start(f32[8192]{0:T(1024)S(1)} %get-tuple-element.51), channel_id=1, source_target_pairs={{2,0},{4,2},{6,4},{8,6},{10,8},{12,10},{14,12},{0,14},{3,1},{5,3},... | collective-permute-start | bytes 98312 | tf_op jit(solution)/shard_map/ppermute | solution.py:13
  298.4 2.5 collective-permute-start.14
  300.9 1.3 collective-permute-start.15
  302.2 0.2 stack.83
  302.6 160.6 %gather_fusion.2 = f32[16384]{0:T(1024)} fusion(f32[40960]{0:T(1024)S(1)} %reshape.166, s32[16384]{0:T(1024)S(1)} %broadcast_clamp_fusion), kind=kCustom, calls=%fused_computation.2 | custom fusion | bytes 196608 | tf_op jit(solution)/shard_map/gather | solution.py:172
  463.2 0.2 pad_maximum_fusion.2
  463.5 0.1 add_multiply_fusion.2
  463.7 0.1 add_multiply_fusion.1
  464.0 0.1 add_multiply_fusion
  464.4 0.3 fusion.114
  464.7 0.8 copy.231
  (78 shorter events, 2.9 us)
Async XLA Ops:
  219.9 14.6 %copy-start.2 = (f32[1,3,64,128]{3,2,1,0:T(8,128)S(1)}, f32[1,3,64,128]{3,2,1,0:T(8,128)}, u32[]{:S(2)}) copy-start(f32[1,3,64,128]{3,2,1,0:T(8,128)} %param.12) | copy-start | bytes 294916
  219.9 19.2 %copy-start.5 = (s32[1,1,1,64,2]{3,4,2,1,0:T(2,128)S(1)}, s32[1,1,1,64,2]{3,4,2,1,0:T(2,128)}, u32[]{:S(2)}) copy-start(s32[1,1,1,64,2]{3,4,2,1,0:T(2,128)} %param.10) | copy-start | bytes 1540
  219.9 19.4 %copy-start.1 = (s32[1,64,128]{2,1,0:T(8,128)S(1)}, s32[1,64,128]{2,1,0:T(8,128)}, u32[]{:S(2)}) copy-start(s32[1,64,128]{2,1,0:T(8,128)} %param.15) | copy-start | bytes 98308
  219.9 19.4 %copy-start.4 = (f32[1,64,128]{2,1,0:T(8,128)S(1)}, f32[1,64,128]{2,1,0:T(8,128)}, u32[]{:S(2)}) copy-start(f32[1,64,128]{2,1,0:T(8,128)} %param.14) | copy-start | bytes 98308
  222.4 32.1 %collective-permute-start = (bf16[8,8192]{1,0:T(8,128)(2,1)}, bf16[8,8192]{1,0:T(8,128)(2,1)}, u32[]{:S(2)}, u32[]{:S(2)}) collective-permute-start(bf16[8,8192]{1,0:T(8,128)(2,1)} %bitcast.9), channel_id=1, source_target_pairs={{4,0},{6,2},{8,4},{10,6},{12,8},{14,10},{0,12},{2,14},{5,1},{7,3},... | collective-permute-start | bytes 393224 | tf_op jit(solution)/shard_map/ppermute | solution.py:13
  230.0 25.5 %collective-permute-start.1 = (bf16[8,8192]{1,0:T(8,128)(2,1)}, bf16[8,8192]{1,0:T(8,128)(2,1)}, u32[]{:S(2)}, u32[]{:S(2)}) collective-permute-start(bf16[8,8192]{1,0:T(8,128)(2,1)} %bitcast.12), channel_id=1, source_target_pairs={{2,0},{4,2},{6,4},{8,6},{10,8},{12,10},{14,12},{0,14},{3,1},{5,3},... | collective-permute-start | bytes 393224 | tf_op jit(solution)/shard_map/ppermute | solution.py:13
  233.8 22.6 %collective-permute-start.2 = (bf16[8,8192]{1,0:T(8,128)(2,1)}, bf16[8,8192]{1,0:T(8,128)(2,1)}, u32[]{:S(2)}, u32[]{:S(2)}) collective-permute-start(bf16[8,8192]{1,0:T(8,128)(2,1)} %bitcast.14), channel_id=1, source_target_pairs={{14,0},{0,2},{2,4},{4,6},{6,8},{8,10},{10,12},{12,14},{15,1},{1,3}... | collective-permute-start | bytes 393224 | tf_op jit(solution)/shard_map/ppermute | solution.py:13
  234.9 6.4 %collective-permute-start.8 = (f32[3,8,128]{1,2,0:T(8,128)S(1)}, f32[3,8,128]{1,2,0:T(8,128)S(1)}, u32[]{:S(2)}, u32[]{:S(2)}) collective-permute-start(f32[3,8,128]{1,2,0:T(8,128)S(1)} %get-tuple-element.48), channel_id=1, source_target_pairs={{0,4},{4,8},{8,12},{1,5},{5,9},{9,13},{2,6},{6,10},{10,14},{3,7},{... | collective-permute-start | bytes 36872 | tf_op jit(solution)/shard_map/ppermute | solution.py:21
  237.8 7.7 %collective-permute-start.9 = (f32[3,8,128]{1,2,0:T(8,128)S(1)}, f32[3,8,128]{1,2,0:T(8,128)S(1)}, u32[]{:S(2)}, u32[]{:S(2)}) collective-permute-start(f32[3,8,128]{1,2,0:T(8,128)S(1)} %get-tuple-element.49), channel_id=1, source_target_pairs={{4,0},{8,4},{12,8},{5,1},{9,5},{13,9},{6,2},{10,6},{14,10},{7,3},{... | collective-permute-start | bytes 36872 | tf_op jit(solution)/shard_map/ppermute | solution.py:24
  245.6 6.9 %collective-permute-start.10 = (f32[3,80,8]{1,2,0:T(8,128)S(1)}, f32[3,80,8]{1,2,0:T(8,128)S(1)}, u32[]{:S(2)}, u32[]{:S(2)}) collective-permute-start(f32[3,80,8]{1,2,0:T(8,128)S(1)} %get-tuple-element.15), channel_id=1, source_target_pairs={{0,2},{1,3},{4,6},{5,7},{8,10},{9,11},{12,14},{13,15},{16,18},{17,... | collective-permute-start | bytes 23048 | tf_op jit(solution)/shard_map/ppermute | solution.py:21
  248.5 5.8 %collective-permute-start.11 = (f32[3,80,8]{1,2,0:T(8,128)S(1)}, f32[3,80,8]{1,2,0:T(8,128)S(1)}, u32[]{:S(2)}, u32[]{:S(2)}) collective-permute-start(f32[3,80,8]{1,2,0:T(8,128)S(1)} %get-tuple-element.16), channel_id=1, source_target_pairs={{2,0},{3,1},{6,4},{7,5},{10,8},{11,9},{14,12},{15,13},{18,16},{19,... | collective-permute-start | bytes 23048 | tf_op jit(solution)/shard_map/ppermute | solution.py:24
  252.5 11.1 %copy-start.3 = (f32[1,64,128]{2,1,0:T(8,128)S(1)}, f32[1,64,128]{2,1,0:T(8,128)}, u32[]{:S(2)}) copy-start(f32[1,64,128]{2,1,0:T(8,128)} %param.13) | copy-start | bytes 98308
  252.5 6.8 %collective-permute-start.3 = (bf16[8,8192]{1,0:T(8,128)(2,1)S(1)}, bf16[8,8192]{1,0:T(8,128)(2,1)S(1)}, u32[]{:S(2)}, u32[]{:S(2)}) collective-permute-start(bf16[8,8192]{1,0:T(8,128)(2,1)S(1)} %bitcast.213), channel_id=1, source_target_pairs={{12,0},{14,2},{0,4},{2,6},{4,8},{6,10},{8,12},{10,14},{13,1},{15,3... | collective-permute-start | bytes 393224 | tf_op jit(solution)/shard_map/ppermute | solution.py:13
  260.0 6.9 %copy-start = (bf16[1,1,1,64,2,128,128]{6,5,4,3,2,1,0:T(8,128)(2,1)S(1)}, bf16[1,1,1,64,2,128,128]{6,5,4,3,2,1,0:T(8,128)(2,1)}, u32[]{:S(2)}) copy-start(bf16[1,1,1,64,2,128,128]{6,5,4,3,2,1,0:T(8,128)(2,1)} %param.11) | copy-start | bytes 12582916
  263.7 3.9 collective-permute-start.4
  265.6 5.7 %collective-permute-start.5 = (f32[5,8,128]{2,1,0:T(8,128)S(1)}, f32[5,8,128]{2,1,0:T(8,128)S(1)}, u32[]{:S(2)}, u32[]{:S(2)}) collective-permute-start(f32[5,8,128]{2,1,0:T(8,128)S(1)} %get-tuple-element.56), channel_id=1, source_target_pairs={{4,0},{8,4},{12,8},{5,1},{9,5},{13,9},{6,2},{10,6},{14,10},{7,3},{... | collective-permute-start | bytes 61448 | tf_op jit(solution)/shard_map/ppermute | solution.py:24
  271.4 7.8 %collective-permute-start.6 = (f32[5,80,8]{2,1,0:T(8,128)S(1)}, f32[5,80,8]{2,1,0:T(8,128)S(1)}, u32[]{:S(2)}, u32[]{:S(2)}) collective-permute-start(f32[5,80,8]{2,1,0:T(8,128)S(1)} %get-tuple-element.44), channel_id=1, source_target_pairs={{0,2},{1,3},{4,6},{5,7},{8,10},{9,11},{12,14},{13,15},{16,18},{17,... | collective-permute-start | bytes 38408 | tf_op jit(solution)/shard_map/ppermute | solution.py:21
  276.0 7.7 %collective-permute-start.7 = (f32[5,80,8]{2,1,0:T(8,128)S(1)}, f32[5,80,8]{2,1,0:T(8,128)S(1)}, u32[]{:S(2)}, u32[]{:S(2)}) collective-permute-start(f32[5,80,8]{2,1,0:T(8,128)S(1)} %get-tuple-element.45), channel_id=1, source_target_pairs={{2,0},{3,1},{6,4},{7,5},{10,8},{11,9},{14,12},{15,13},{18,16},{19,... | collective-permute-start | bytes 38408 | tf_op jit(solution)/shard_map/ppermute | solution.py:24
  285.7 12.6 %collective-permute-start.12 = (f32[3,8,128]{1,2,0:T(8,128)S(1)}, f32[3,8,128]{1,2,0:T(8,128)S(1)}, u32[]{:S(2)}, u32[]{:S(2)}) collective-permute-start(f32[3,8,128]{1,2,0:T(8,128)S(1)} %get-tuple-element.46), channel_id=1, source_target_pairs={{0,4},{4,8},{8,12},{1,5},{5,9},{9,13},{2,6},{6,10},{10,14},{3,7},{... | collective-permute-start | bytes 36872 | tf_op jit(solution)/shard_map/ppermute | solution.py:21
  289.6 8.7 %collective-permute-start.13 = (f32[3,8,128]{1,2,0:T(8,128)S(1)}, f32[3,8,128]{1,2,0:T(8,128)S(1)}, u32[]{:S(2)}, u32[]{:S(2)}) collective-permute-start(f32[3,8,128]{1,2,0:T(8,128)S(1)} %get-tuple-element.47), channel_id=1, source_target_pairs={{4,0},{8,4},{12,8},{5,1},{9,5},{13,9},{6,2},{10,6},{14,10},{7,3},{... | collective-permute-start | bytes 36872 | tf_op jit(solution)/shard_map/ppermute | solution.py:24
  290.9 10.0 %collective-permute-start.16 = (f32[8192]{0:T(1024)S(1)}, f32[8192]{0:T(1024)S(1)}, u32[]{:S(2)}, u32[]{:S(2)}) collective-permute-start(f32[8192]{0:T(1024)S(1)} %get-tuple-element.54), channel_id=1, source_target_pairs={{12,0},{14,2},{0,4},{2,6},{4,8},{6,10},{8,12},{10,14},{13,1},{15,3... | collective-permute-start | bytes 98312 | tf_op jit(solution)/shard_map/ppermute | solution.py:13
  293.6 8.6 %collective-permute-start.17 = (f32[8192]{0:T(1024)S(1)}, f32[8192]{0:T(1024)S(1)}, u32[]{:S(2)}, u32[]{:S(2)}) collective-permute-start(f32[8192]{0:T(1024)S(1)} %get-tuple-element.53), channel_id=1, source_target_pairs={{14,0},{0,2},{2,4},{4,6},{6,8},{8,10},{10,12},{12,14},{15,1},{1,3}... | collective-permute-start | bytes 98312 | tf_op jit(solution)/shard_map/ppermute | solution.py:13
  293.6 8.6 %collective-permute-start.18 = (f32[8192]{0:T(1024)S(1)}, f32[8192]{0:T(1024)S(1)}, u32[]{:S(2)}, u32[]{:S(2)}) collective-permute-start(f32[8192]{0:T(1024)S(1)} %get-tuple-element.51), channel_id=1, source_target_pairs={{2,0},{4,2},{6,4},{8,6},{10,8},{12,10},{14,12},{0,14},{3,1},{5,3},... | collective-permute-start | bytes 98312 | tf_op jit(solution)/shard_map/ppermute | solution.py:13
  298.3 3.9 collective-permute-start.19
  298.4 164.8 %collective-permute-start.14 = (f32[3,80,8]{1,2,0:T(8,128)S(1)}, f32[3,80,8]{1,2,0:T(8,128)S(1)}, u32[]{:S(2)}, u32[]{:S(2)}) collective-permute-start(f32[3,80,8]{1,2,0:T(8,128)S(1)} %get-tuple-element.13), channel_id=1, source_target_pairs={{0,2},{1,3},{4,6},{5,7},{8,10},{9,11},{12,14},{13,15},{16,18},{17,... | collective-permute-start | bytes 23048 | tf_op jit(solution)/shard_map/ppermute | solution.py:21
  300.9 162.3 %collective-permute-start.15 = (f32[3,80,8]{1,2,0:T(8,128)S(1)}, f32[3,80,8]{1,2,0:T(8,128)S(1)}, u32[]{:S(2)}, u32[]{:S(2)}) collective-permute-start(f32[3,80,8]{1,2,0:T(8,128)S(1)} %get-tuple-element.14), channel_id=1, source_target_pairs={{2,0},{3,1},{6,4},{7,5},{10,8},{11,9},{14,12},{15,13},{18,16},{19,... | collective-permute-start | bytes 23048 | tf_op jit(solution)/shard_map/ppermute | solution.py:24
where the time goes:
time: 466 us; the launch traced here: 465 us
  local copies, waits for them, and re-layouts  394 us (85%)
  starting transfers between devices  42.5 us (9%)
  waiting for transfers between devices  17.7 us (4%)
  other arithmetic  5.32 us (1%)
  matrix products  4.98 us (1%)
    gather x1, local copies, waits for them, and re-layouts, shards(): atm_temp = backward[flat_slot][None, :]  161 us
    gather x1, local copies, waits for them, and re-layouts, shards(): padded_fields[:, slot_source]  139 us
    scatter x1, local copies, waits for them, and re-layouts, shards(): slot_source = jnp.full((NEIGHBOR_TILES * slot_limit,), column_count, jnp....  60.4 us
    ppermute x6, starting transfers between devices, padded_2(): lax.ppermute(lax.slice_in_dim(block, block.shape[dim] - width, None, axis...  18.5 us
    unnamed x27, local copies, waits for them, and re-layouts  17.9 us
    ppermute x8, starting transfers between devices, passed_along(): return lax.ppermute(block, axis, route)  16.3 us
    ppermute x6, waiting for transfers between devices, padded_2(): lax.ppermute(lax.slice_in_dim(block, 0, width, axis=dim), axis, backward)  12.2 us
  transfers between devices with their start and end apart: 20, of which 6 were waited for; matrix products, arithmetic and copies ran while one was open for 37% of the time, Pallas kernels for 0%

commit v1 on v0

v1 whole, which is shorter than its diff:
```python
import functools

import jax
import jax.numpy as jnp
from jax import lax
from jax.experimental import pallas as pl
from jax.experimental.pallas import tpu as pltpu
from jax.sharding import PartitionSpec as P

NEIGHBOR_TILES = 5
MIDDLE = NEIGHBOR_TILES // 2
SUBS = 8
LANES = 128
HALO = 2 * SUBS
FIELDS = 8
F32 = jnp.float32
BF16 = jnp.bfloat16
I32 = jnp.int32
VMEM_LIMIT = 48 * 1024 * 1024


def iota(shape, dim):
    return lax.broadcasted_iota(I32, shape, dim)


def dot(a, b):
    return jnp.dot(a, b, preferred_element_type=F32)


def dot_t(a, b):
    return lax.dot_general(a, b, (((1,), (1,)), ((), ())), preferred_element_type=F32)


def ones_where(mask):
    return jnp.where(mask, 1.0, 0.0).astype(BF16)


def offsets_of(destination, count_s, total):
    mine = lax.axis_index("tile") * count_s + lax.axis_index("sub")
    shifted = destination - mine + MIDDLE
    shifted = jnp.where(shifted < 0, shifted + total, shifted)
    return jnp.where(shifted >= total, shifted - total, shifted)


def ranks(offsets):
    rows = offsets.shape[0]
    r, c = iota((LANES, LANES), 0), iota((LANES, LANES), 1)
    before = ones_where(r < c)
    every = jnp.ones((LANES, LANES), BF16)
    earlier = ones_where(iota((rows, rows), 1) < iota((rows, rows), 0))
    result = []
    for o in range(NEIGHBOR_TILES):
        mask = offsets == o
        hot = ones_where(mask)
        inside = dot(hot, before)
        count = dot(hot, every)
        base = dot(earlier, count.astype(BF16))
        result.append((mask, hot, inside, count, base))
    return result


def route_kernel(
    count_s, total, dest_ref, x_ref, *rest
):
    outs = rest[:NEIGHBOR_TILES]
    comb, sorted_scr, place, pos_scr, vec, scal, sem = rest[NEIGHBOR_TILES:]
    blocks = dest_ref.shape[0]
    groups = outs[0].shape[0] // 4
    stride = (groups + 1) * 8
    offsets = offsets_of(dest_ref[...], count_s, total)
    parts = ranks(offsets)
    ones8 = jnp.ones((8, LANES), BF16)
    sub8 = iota((8, blocks), 0)
    before = ones_where(iota((blocks, blocks), 0) < iota((blocks, blocks), 1))
    start_t = jnp.zeros((8, blocks), F32)
    base_t = jnp.zeros((8, blocks), F32)
    starts_t = jnp.zeros((8, blocks), F32)
    start = jnp.zeros((blocks, LANES), F32)
    pos = jnp.zeros((blocks, LANES), F32)
    for o, (mask, hot, inside, count, base) in enumerate(parts):
        pos = jnp.where(mask, start + inside, pos)
        start = start + count
        count_t = dot_t(ones8, hot)
        base_row = dot(count_t.astype(BF16), before)
        base_t = jnp.where(sub8 == o, base_row, base_t)
        starts_t = jnp.where(sub8 == o, start_t, starts_t)
        start_t = start_t + count_t
    starts_t = jnp.where(sub8 == NEIGHBOR_TILES, start_t, starts_t)
    vec[0:8, :] = base_t.astype(I32)
    vec[8:16, :] = starts_t.astype(I32)
    copy = pltpu.make_async_copy(vec, scal, sem)
    copy.start()
    pos_scr[...] = pos.astype(I32)
    f, g = iota((8, 8), 1), jnp.bitwise_and(iota((8, 8), 0), 3)
    plus = ((g == 0) & (f == 0)) | ((g == 1) & (f == 1)) | ((g == 2) & (f == 3)) | ((g == 3) & (f >= 6))
    minus = ((g == 2) & (f == 2)) | ((g == 3) & ((f == 4) | (f == 5)))
    combine = (jnp.where(plus, 1.0, 0.0) - jnp.where(minus, 1.0, 0.0)).astype(BF16)
    comb[...] = dot(combine, x_ref[...]).astype(BF16)
    rows_id = iota((LANES, LANES), 0)

    def sort_step(i, carry):
        for u in range(8):
            b = i * 8 + u
            hot = ones_where(pos_scr[pl.ds(b, 1), :] == rows_id)
            columns = comb[:, pl.ds(pl.multiple_of(b * LANES, LANES), LANES)]
            sorted_scr[pl.ds(pl.multiple_of(b * 8, 8), 8), :] = dot_t(columns, hot)
        return carry

    lax.fori_loop(0, blocks // 8, sort_step, 0)
    copy.wait()
    lane = iota((8, LANES), 1)

    def place_step(i, current):
        current = list(current)
        for u in range(4):
            b = i * 4 + u
            values = sorted_scr[pl.ds(pl.multiple_of(b * 8, 8), 8), :]
            for o in range(NEIGHBOR_TILES):
                base = scal[o, b]
                first = scal[8 + o, b]
                length = scal[9 + o, b] - first
                at = jnp.bitwise_and(base, LANES - 1)
                turned = pltpu.roll(values, jnp.bitwise_and(at - first, LANES - 1), 1)
                merged = jnp.where(lane < at, current[o], turned)
                row = pl.multiple_of(o * stride + lax.shift_right_logical(base, 7) * 8, 8)
                place[pl.ds(row, 8), :] = merged
                current[o] = jnp.where(lane < at + length - LANES, turned, merged)
        return tuple(current)

    current = lax.fori_loop(
        0, blocks // 4, place_step, tuple(jnp.zeros((8, LANES), F32) for _ in range(NEIGHBOR_TILES))
    )
    pair_lane = jnp.where(iota((8, LANES), 0) < 4, lane, lane + LANES)
    upper = iota((groups // 2, 8, LANES), 1) < 4
    slot = iota((groups // 2, 8, LANES), 0) * (2 * LANES) + pair_lane[None]
    for o in range(NEIGHBOR_TILES):
        last = blocks - 1
        count = scal[o, last] + scal[9 + o, last] - scal[8 + o, last]
        row = pl.multiple_of(o * stride + lax.shift_right_logical(count, 7) * 8, 8)
        place[pl.ds(row, 8), :] = current[o]
        tiles = place[o * stride : o * stride + groups * 8, :].reshape(groups // 2, 2, 8, LANES)
        both = jnp.where(upper, tiles[:, 0], tiles[:, 1])
        both = jnp.where(slot < count, both, 0.0)
        outs[o][...] = both.reshape(groups * 4, LANES).astype(BF16)


def prepare_kernel(count_s, total, dest_ref, index_ref, code_ref, *hot_refs):
    blocks = dest_ref.shape[0]
    groups = hot_refs[0].shape[1]
    offsets = offsets_of(dest_ref[...], count_s, total)
    index = jnp.zeros((blocks, LANES), I32)
    code = jnp.zeros((blocks, LANES), I32)
    group_id = iota((blocks, groups), 1)
    for o, (mask, hot, inside, count, base) in enumerate(ranks(offsets)):
        base = base.astype(I32)
        rank = base + inside.astype(I32)
        first = lax.shift_right_logical(base, 7)
        index = jnp.where(mask, jnp.bitwise_and(rank, LANES - 1), index)
        code = jnp.where(mask, 2 * o + lax.shift_right_logical(rank, 7) - first, code)
        hot_refs[o][0:blocks, :] = ones_where(group_id == first[:, :groups])
        hot_refs[o][blocks:, :] = ones_where(group_id == first[:, :groups] + 1)
    index_ref[...] = index
    code_ref[...] = code


def packed_columns(fields, low):
    lane = iota(fields[0].shape, 1)
    packed = fields[0] if low else pltpu.roll(fields[0], HALO, 1)
    for i in range(1, FIELDS):
        turn = (i * HALO + (0 if low else HALO)) % LANES
        packed = jnp.where(
            lane >= i * HALO, pltpu.roll(fields[i], turn, 1) if turn else fields[i], packed
        )
    return packed


def remap_kernel(messages, ptr_ref, *rest):
    arrived = rest[:NEIGHBOR_TILES]
    (row_ref, w_ref, ocean_ref, skin_ref, depth_ref, mask_ref) = rest[NEIGHBOR_TILES : NEIGHBOR_TILES + 6]
    outs = rest[NEIGHBOR_TILES + 6 :]
    forcing_ref, own_ref = outs[:2]
    message_refs = outs[2 : 2 + len(messages)]
    slots, mapped, shares = outs[2 + len(messages) :]
    step = pl.program_id(0)
    per_step = w_ref.shape[0]
    size = arrived[0].shape[0]

    @pl.when(step == 0)
    def _():
        for o in range(NEIGHBOR_TILES):
            slots[o * size : (o + 1) * size, :] = arrived[o][...].astype(F32)
        slots[NEIGHBOR_TILES * size :, :] = jnp.zeros((8, LANES), F32)

    for j in range(per_step):
        k = step * per_step + j
        total = None
        for w in range(2):
            block = slots[pl.ds(ptr_ref[2 * k + w] * 4, 8), :].astype(BF16)
            product = dot_t(block, w_ref[j, w])
            total = product if total is None else total + product
        mapped[j * 8 : j * 8 + 8, :] = total
    u, v, p, h = (mapped[pl.ds(i, per_step, stride=8), :] for i in range(4))
    rows = pl.ds(pl.multiple_of(step * per_step, per_step), per_step)
    speed = jnp.sqrt(u * u + v * v + 1.0)
    forcing_ref[0, rows, :] = 0.2 * speed * u
    forcing_ref[1, rows, :] = 0.2 * speed * v
    forcing_ref[2, rows, :] = 0.5 * p
    sst = (skin_ref[rows, :] + 0.25 * mask_ref[rows, :].astype(F32) * h).astype(BF16).astype(F32)
    sub = iota((per_step, LANES), 0)
    for w in range(2):
        total = None
        for j in range(per_step):
            product = dot(jnp.where(sub == j, sst, 0.0).astype(BF16), w_ref[j, w])
            total = product if total is None else total + product
        shares[pl.ds(step * (2 * per_step) + w, per_step, stride=2), :] = total

    @pl.when(step == pl.num_programs(0) - 1)
    def _():
        count = shares.shape[0]
        every = shares[...]
        high = every.astype(BF16)
        low = (every - high.astype(F32)).astype(BF16)
        groups = own_ref.shape[0]
        returned = []
        for o in range(NEIGHBOR_TILES):
            hot = ones_where(iota((groups, count), 0) + o * groups == row_ref[...])
            returned.append((dot(hot, high) + dot(hot, low)).astype(BF16))
        own_ref[...] = returned[MIDDLE]
        fields = [ocean_ref[0], ocean_ref[1], ocean_ref[2], mask_ref[...].astype(F32), depth_ref[...]]
        fields += [forcing_ref[0], forcing_ref[1], forcing_ref[2]]
        high_columns = packed_columns(fields, False)
        low_columns = packed_columns(fields, True)
        tall = fields[0].shape[0]
        for (pairs, parts), out in zip(messages, message_refs):
            at = 0
            for kind, length in parts:
                if kind[0] == "ret":
                    value = returned[kind[1]]
                else:
                    _, dt, ds = kind
                    span = {1: slice(tall - HALO, tall), 0: slice(0, tall), -1: slice(0, HALO)}[dt]
                    if ds:
                        value = (high_columns if ds > 0 else low_columns)[span]
                    else:
                        value = jnp.concatenate([x[span] for x in fields], axis=0)
                    value = value.astype(BF16)
                out[at : at + length, :] = value
                at += length


def finish_kernel(messages, count_t, count_s, *rest):
    message_refs = rest[: len(messages)]
    own_ref, index_ref, code_ref = rest[len(messages) : len(messages) + 3]
    hot_refs = rest[len(messages) + 3 : len(messages) + 3 + NEIGHBOR_TILES]
    ocean_ref, depth_ref, mask_ref, forcing_ref, out_ref, warm_ref = rest[
        len(messages) + 3 + NEIGHBOR_TILES :
    ]
    t, s = lax.axis_index("tile"), lax.axis_index("sub")
    found = {("ret", MIDDLE): own_ref[...]}
    for (pairs, parts), ref in zip(messages, message_refs):
        at = 0
        for kind, length in parts:
            found[kind] = ref[at : at + length, :]
            at += length
    blocks = index_ref.shape[0]
    index = index_ref[...]
    code = code_ref[...]
    warm = jnp.zeros((blocks, LANES), F32)
    for o in range(NEIGHBOR_TILES):
        lines = dot(hot_refs[o][...], found[("ret", o)])
        for half in range(2):
            picked = jnp.take_along_axis(lines[half * blocks : (half + 1) * blocks], index, axis=1)
            warm = jnp.where(code == 2 * o + half, picked, warm)
    warm_ref[...] = warm

    tall = depth_ref.shape[0]
    full = tall + 2 * HALO

    def halo(dt, ds):
        ok = jnp.bool_(True)
        if dt == 1:
            ok &= t > 0
        if dt == -1:
            ok &= t < count_t - 1
        if ds == 1:
            ok &= s > 0
        if ds == -1:
            ok &= s < count_s - 1
        value = found[("halo", dt, ds)].astype(F32)
        return jnp.where(ok, value, 0.0)

    from_left = jnp.concatenate([halo(1, 1), halo(0, 1), halo(-1, 1)], axis=0)
    from_right = jnp.concatenate([halo(1, -1), halo(0, -1), halo(-1, -1)], axis=0)
    above, below = halo(1, 0), halo(-1, 0)
    lane = iota((full, LANES), 1)
    inner = [ocean_ref[0], ocean_ref[1], ocean_ref[2], mask_ref[...].astype(F32), depth_ref[...]]
    inner += [forcing_ref[0], forcing_ref[1], forcing_ref[2]]
    wide = []
    for i in range(FIELDS):
        rows = slice(i * HALO, (i + 1) * HALO)
        main = jnp.concatenate([above[rows], inner[i], below[rows]], axis=0)
        turn = (LANES - HALO - i * HALO) % LANES
        left = pltpu.roll(from_left, turn, 1) if turn else from_left
        turn = (LANES - i * HALO) % LANES
        right = pltpu.roll(from_right, turn, 1) if turn else from_right
        side = jnp.where(lane < HALO, right, jnp.where(lane >= LANES - HALO, left, 0.0))
        wide.append(jnp.concatenate([main, side], axis=1))
    eta, east, north, m, depth, stress_x, stress_y, fresh = wide
    row = iota((full, 2 * LANES), 0) + (t * tall - HALO)
    coriolis = 0.1 + 0.2 * (row.astype(F32) + 0.5) / (tall * count_t)

    def dx(a):
        return 0.5 * (pltpu.roll(a, 2 * LANES - 1, 1) - pltpu.roll(a, 1, 1))

    def dy(a):
        return 0.5 * (pltpu.roll(a, full - 1, 0) - pltpu.roll(a, 1, 0))

    for _ in range(SUBS):
        eta = m * (eta - (dx(east) + dy(north)) + fresh)
        new_east = m * (east + coriolis * north - depth * dx(eta) + stress_x)
        north = m * (north - coriolis * east - depth * dy(eta) + stress_y)
        east = new_east
    for i, a in enumerate((eta, east, north)):
        out_ref[i] = a[HALO : HALO + tall, :LANES]


def plan_messages(count_t, count_s, groups, tall):
    total = count_t * count_s
    by_distance = {}
    for o in range(NEIGHBOR_TILES):
        if o != MIDDLE:
            by_distance.setdefault(MIDDLE - o, []).append((("ret", o), groups))
    for dt in (-1, 0, 1):
        for ds in (-1, 0, 1):
            if dt or ds:
                length = tall if dt == 0 else (HALO if ds else HALO * FIELDS)
                by_distance.setdefault(dt * count_s + ds, []).append((("halo", dt, ds), length))
    messages, partial = [], []
    for distance, parts in sorted(by_distance.items()):
        if any(kind[0] == "ret" for kind, _ in parts):
            pairs = [(i, (i + distance) % total) for i in range(total)]
            messages.append((pairs, parts))
            continue
        pairs = []
        for (_, dt, ds), _ in parts:
            for t in range(count_t):
                for s in range(count_s):
                    if 0 <= t + dt < count_t and 0 <= s + ds < count_s:
                        pairs.append((t * count_s + s, (t + dt) * count_s + s + ds))
        for other in partial:
            if not {a for a, _ in pairs} & {a for a, _ in other[0]} and not (
                {b for _, b in pairs} & {b for _, b in other[0]}
            ):
                other[0].extend(pairs)
                other[1].extend(parts)
                break
        else:
            partial.append((pairs, list(parts)))
    return messages + partial


def shards(
    air_exchanges,
    air_destination,
    diagonal_group_pointer,
    interpolation_factors,
    marine_fields,
    skin_warmth_anomaly,
    gravity_bathymetry,
    marine_indicator,
):
    axes = ("tile", "sub")
    count_t, count_s = lax.axis_size("tile"), lax.axis_size("sub")
    total = count_t * count_s
    columns = air_destination.shape[1]
    blocks = columns // LANES
    groups = columns // 2 // LANES
    destination = air_destination.reshape(blocks, LANES)
    vmem = pl.BlockSpec(memory_space=pltpu.VMEM)
    params = pltpu.CompilerParams(vmem_limit_bytes=VMEM_LIMIT)
    outbound = pl.pallas_call(
        functools.partial(route_kernel, count_s, total),
        out_shape=[jax.ShapeDtypeStruct((groups * 4, LANES), BF16)] * NEIGHBOR_TILES,
        in_specs=[vmem, vmem],
        out_specs=[vmem] * NEIGHBOR_TILES,
        scratch_shapes=[
            pltpu.VMEM((8, columns), BF16),
            pltpu.VMEM((blocks * 8, LANES), F32),
            pltpu.VMEM((NEIGHBOR_TILES * (groups + 1) * 8, LANES), F32),
            pltpu.VMEM((blocks, LANES), I32),
            pltpu.VMEM((16, blocks), I32),
            pltpu.SMEM((16, blocks), I32),
            pltpu.SemaphoreType.DMA,
        ],
        compiler_params=params,
        name="route",
    )(destination, air_exchanges[0])
    arrived = list(outbound)
    for o in range(NEIGHBOR_TILES):
        if o != MIDDLE:
            pairs = [(i, (i + o - MIDDLE) % total) for i in range(total)]
            arrived[o] = lax.ppermute(outbound[o], axes, pairs)
    prepared = pl.pallas_call(
        functools.partial(prepare_kernel, count_s, total),
        out_shape=[jax.ShapeDtypeStruct((blocks, LANES), I32)] * 2
        + [jax.ShapeDtypeStruct((2 * blocks, groups), BF16)] * NEIGHBOR_TILES,
        in_specs=[vmem],
        out_specs=[vmem] * (2 + NEIGHBOR_TILES),
        compiler_params=params,
        cost_estimate=pl.CostEstimate(flops=2 * 15 * LANES**3, bytes_accessed=2**19, transcendentals=0),
        name="prepare",
    )(destination)

    pointers = diagonal_group_pointer.reshape(-1)
    weights = interpolation_factors[0, 0, 0]
    tall = skin_warmth_anomaly.shape[1]
    messages = plan_messages(count_t, count_s, groups, tall)
    lengths = [sum(n for _, n in parts) for _, parts in messages]
    row_blocks = weights.shape[0]
    per_step = 8
    whole = lambda shape: pl.BlockSpec(shape, lambda i, p: (0,) * len(shape))
    ocean, depth, mask = marine_fields[0], gravity_bathymetry[0], marine_indicator[0]
    outs = pl.pallas_call(
        functools.partial(remap_kernel, messages),
        out_shape=[
            jax.ShapeDtypeStruct((3, tall, LANES), F32),
            jax.ShapeDtypeStruct((groups, LANES), BF16),
        ]
        + [jax.ShapeDtypeStruct((n, LANES), BF16) for n in lengths],
        grid_spec=pltpu.PrefetchScalarGridSpec(
            num_scalar_prefetch=1,
            grid=(row_blocks // per_step,),
            in_specs=[whole((groups * 4, LANES))] * NEIGHBOR_TILES
            + [
                whole((1, 2 * row_blocks)),
                pl.BlockSpec((per_step, 2, LANES, LANES), lambda i, p: (i, 0, 0, 0)),
                whole((3, tall, LANES)),
                whole((tall, LANES)),
                whole((tall, LANES)),
                whole((tall, LANES)),
            ],
            out_specs=[whole((3, tall, LANES)), whole((groups, LANES))]
            + [whole((n, LANES)) for n in lengths],
            scratch_shapes=[
                pltpu.VMEM((NEIGHBOR_TILES * groups * 4 + 8, LANES), F32),
                pltpu.VMEM((per_step * 8, LANES), F32),
                pltpu.VMEM((2 * row_blocks, LANES), F32),
            ],
        ),
        compiler_params=params,
        name="remap",
    )(pointers, *arrived, pointers.reshape(1, -1), weights, ocean, skin_warmth_anomaly[0], depth, mask)
    forcing, own = outs[:2]
    received = [
        lax.ppermute(message, axes, pairs) for message, (pairs, _) in zip(outs[2:], messages)
    ]
    ocean_out, warm = pl.pallas_call(
        functools.partial(finish_kernel, messages, count_t, count_s),
        out_shape=[
            jax.ShapeDtypeStruct((3, tall, LANES), F32),
            jax.ShapeDtypeStruct((blocks, LANES), F32),
        ],
        in_specs=[vmem] * (len(messages) + 3 + NEIGHBOR_TILES + 4),
        out_specs=[vmem] * 2,
        compiler_params=params,
        name="finish",
    )(*received, own, *prepared, ocean, depth, mask, forcing)
    return ocean_out[None], warm.reshape(1, columns)


def solution(mesh):
    return jax.shard_map(
        shards,
        mesh=mesh,
        in_specs=(
            P(("member", "comp"), None, ("tile", "sub")),
            P("comp", ("tile", "sub"), None),
            P("comp", "tile", "sub", None, None),
            P("comp", "tile", "sub", None, None, None, None),
            P(("member", "comp"), None, "tile", "sub"),
            P(("member", "comp"), "tile", "sub"),
            P("comp", "tile", "sub"),
            P("comp", "tile", "sub"),
        ),
        out_specs=(
            P(("member", "comp"), None, "tile", "sub"),
            P(("member", "comp"), ("tile", "sub")),
        ),
        check_vma=False,
    )
```

time: 466 us -> 53.6 us (0.12)
  local copies, waits for them, and re-layouts: 394 us -> 8.18 us
  starting transfers between devices: 42.5 us -> 16.2 us
  Pallas kernels: 0 us -> 20.2 us
  waiting for transfers between devices: 17.7 us -> 7.78 us
  other arithmetic: 5.32 us -> 0 us
  matrix products: 4.98 us -> 0 us
    gather x3 -> x0, local copies, waits for them, and re-layouts: 301 us -> none  [the longest x1 161 us: shards(): atm_temp = backward[flat_slot][None, :]]
    scatter x1 -> x0, local copies, waits for them, and re-layouts: 60.4 us -> none  [shards(): slot_source = jnp.full((NEIGHBOR_TILES * slot_limit,), column_count, jnp....]
    ppermute x20 -> x9, starting transfers between devices: 42.5 us -> 16.2 us  [the longest x5 8.16 us: shards(): lax.ppermute(message, axes, pairs)]
    pallas_call x0 -> x4, Pallas kernels: none -> 20.2 us  [the longest x1 10.1 us: shards(): pl.pallas_call(functools.partial(route_kernel, count_s, total), out_shape...]
    unnamed x27 -> x17, local copies, waits for them, and re-layouts: 17.9 us -> 7.91 us
    ppermute x20 -> x9, waiting for transfers between devices: 17.7 us -> 7.78 us  [the longest x4 4.63 us: shards(): arrived[o] = lax.ppermute(outbound[o], axes, pairs)]
    slice x15 -> x0, local copies, waits for them, and re-layouts: 8.49 us -> none  [the longest x1 7.37 us: shards(): outbound[:, slot]]
    concatenate x1 -> x0, local copies, waits for them, and re-layouts: 5.4 us -> none  [shards(): jnp.concatenate([fluxes, jnp.zeros((field_count, 1), jnp.bfloat16)], axis=1)]
  transfers between devices with their start and end apart: 20 -> 9, of which waited for: 6 -> 3; matrix products, arithmetic and copies ran while one was open for 37% -> 2% of each run, Pallas kernels for 0% -> 2%
where the time goes in v1:
time: 53.6 us; the launch traced here: 53.1 us
  Pallas kernels  20.2 us (38%)
  starting transfers between devices  16.2 us (30%)
  local copies, waits for them, and re-layouts  8.18 us (15%)
  waiting for transfers between devices  7.78 us (15%)
  between operations  0.72 us (1%)
    pallas_call x1, Pallas kernels, shards(): pl.pallas_call(functools.partial(route_kernel, count_s, total), out_shape...  10.1 us
    ppermute x5, starting transfers between devices, shards(): lax.ppermute(message, axes, pairs)  8.16 us
    ppermute x4, starting transfers between devices, shards(): arrived[o] = lax.ppermute(outbound[o], axes, pairs)  8.06 us
    unnamed x17, local copies, waits for them, and re-layouts  7.91 us
    pallas_call x1, Pallas kernels, shards(): pl.pallas_call(functools.partial(remap_kernel, messages), out_shape=[jax....  5.86 us
    ppermute x4, waiting for transfers between devices, shards(): arrived[o] = lax.ppermute(outbound[o], axes, pairs)  4.63 us
    pallas_call x1, Pallas kernels, shards(): pl.pallas_call(functools.partial(finish_kernel, messages, count_t, count_...  3.18 us
    ppermute x5, waiting for transfers between devices, shards(): lax.ppermute(message, axes, pairs)  3.15 us
  transfers between devices with their start and end apart: 9, of which 3 were waited for; matrix products, arithmetic and copies ran while one was open for 2% of the time, Pallas kernels for 2%

profile of v1, /device:TPU:0, one launch (start us, length us, event | category | flops | bytes accessed | tf_op | source)
XLA Modules:
  0.0 53.1 jit_solution(3093822966060081834)
XLA Ops:
  0.6 0.0 copy-start.2
  0.6 0.9 %copy-done.2 = bf16[1,8,16384]{2,1,0:T(8,128)(2,1)S(1)} copy-done((bf16[1,8,16384]{2,1,0:T(8,128)(2,1)S(1)}, bf16[1,8,16384]{2,1,0:T(8,128)(2,1)}, u32[]{:S(2)}) %copy-start.2) | copy-done | bytes 262168
  1.6 0.0 copy-start.5
  1.6 0.8 %copy-done.5 = s32[1,16384,1]{1,2,0:T(1,128)S(1)} copy-done((s32[1,16384,1]{1,2,0:T(1,128)S(1)}, s32[1,16384,1]{1,2,0:T(1,128)}, u32[]{:S(2)}) %copy-start.5) | copy-done | bytes 65560
  2.4 0.0 copy-start.6
  2.4 10.1 %route.1 = (bf16[256,128]{1,0:T(8,128)(2,1)S(1)}, bf16[256,128]{1,0:T(8,128)(2,1)S(1)}, bf16[256,128]{1,0:T(8,128)(2,1)S(1)}, bf16[256,128]{1,0:T(8,128)(2,1)S(1)}, bf16[256,128]{1,0:T(8,128)(2,1)S(1)}) custom-call(s32[128,128]{1,0:T(8,128)S(1)} %bitcast.21, bf16[8,16384]{1,0:T(8,128)(2,1)S(1)} %bitcast.16), custom_call_target="tpu_custom_call" | custom-call | tf_op jit(solution)/shard_map/route/pallas_call | solution.py:381
  12.6 5.1 %collective-permute-start = (bf16[256,128]{1,0:T(8,128)(2,1)S(1)}, bf16[256,128]{1,0:T(8,128)(2,1)S(1)}, u32[]{:S(2)}, u32[]{:S(2)}) collective-permute-start(bf16[256,128]{1,0:T(8,128)(2,1)S(1)} %get-tuple-element.23), channel_id=1, source_target_pairs={{0,12},{2,14},{4,0},{6,2},{8,4},{10,6},{12,8},{14,10},{1,13},{3,15... | collective-permute-start | bytes 196616 | tf_op jit(solution)/shard_map/ppermute | solution.py:402
  17.7 1.4 %collective-permute-start.1 = (bf16[256,128]{1,0:T(8,128)(2,1)S(1)}, bf16[256,128]{1,0:T(8,128)(2,1)S(1)}, u32[]{:S(2)}, u32[]{:S(2)}) collective-permute-start(bf16[256,128]{1,0:T(8,128)(2,1)S(1)} %get-tuple-element.24), channel_id=1, source_target_pairs={{0,14},{2,0},{4,2},{6,4},{8,6},{10,8},{12,10},{14,12},{1,15},{3,1}... | collective-permute-start | bytes 196616 | tf_op jit(solution)/shard_map/ppermute | solution.py:402
  19.0 0.6 %collective-permute-start.2 = (bf16[256,128]{1,0:T(8,128)(2,1)S(1)}, bf16[256,128]{1,0:T(8,128)(2,1)S(1)}, u32[]{:S(2)}, u32[]{:S(2)}) collective-permute-start(bf16[256,128]{1,0:T(8,128)(2,1)S(1)} %get-tuple-element.26), channel_id=1, source_target_pairs={{0,2},{2,4},{4,6},{6,8},{8,10},{10,12},{12,14},{14,0},{1,3},{3,5},... | collective-permute-start | bytes 196616 | tf_op jit(solution)/shard_map/ppermute | solution.py:402
  19.7 0.9 %collective-permute-start.3 = (bf16[256,128]{1,0:T(8,128)(2,1)S(1)}, bf16[256,128]{1,0:T(8,128)(2,1)S(1)}, u32[]{:S(2)}, u32[]{:S(2)}) collective-permute-start(bf16[256,128]{1,0:T(8,128)(2,1)S(1)} %get-tuple-element.27), channel_id=1, source_target_pairs={{0,4},{2,6},{4,8},{6,10},{8,12},{10,14},{12,0},{14,2},{1,5},{3,7},... | collective-permute-start | bytes 196616 | tf_op jit(solution)/shard_map/ppermute | solution.py:402
  20.6 0.8 %copy.12 = s32[1,1,1,64,2]{4,3,2,1,0:T(8,128)S(1)} copy(s32[1,1,1,64,2]{3,4,2,1,0:T(2,128)} %param.10) | data formatting | bytes 1024 | tf_op args[2]
  21.4 0.1 reshape_reshape.3.rest_5_
  21.5 0.1 reshape.13.ptr_ref
  21.7 0.0 collective-permute-done.rest_0_
  21.7 0.2 collective-permute-done.1.rest_1_
  21.9 4.4 %collective-permute-done.2.rest_3_ = bf16[256,128]{1,0:T(8,128)(2,1)S(1)} collective-permute-done((bf16[256,128]{1,0:T(8,128)(2,1)S(1)}, bf16[256,128]{1,0:T(8,128)(2,1)S(1)}, u32[]{:S(2)}, u32[]{:S(2)}) %collective-permute-start.2) | collective-permute-done | bytes 65568 | tf_op jit(solution)/shard_map/ppermute | solution.py:402
  26.3 0.0 collective-permute-done.3.rest_4_
  26.3 0.0 copy-start
  26.3 2.2 %copy-done = bf16[1,1,1,64,2,128,128]{6,5,4,3,2,1,0:T(8,128)(2,1)S(1)} copy-done((bf16[1,1,1,64,2,128,128]{6,5,4,3,2,1,0:T(8,128)(2,1)S(1)}, bf16[1,1,1,64,2,128,128]{6,5,4,3,2,1,0:T(8,128)(2,1)}, u32[]{:S(2)}) %copy-start) | copy-done | bytes 4194328
  28.5 0.0 copy-start.1
  28.5 0.9 %copy-done.1 = f32[1,3,64,128]{3,2,1,0:T(8,128)S(1)} copy-done((f32[1,3,64,128]{3,2,1,0:T(8,128)S(1)}, f32[1,3,64,128]{3,2,1,0:T(8,128)}, u32[]{:S(2)}) %copy-start.1) | copy-done | bytes 98328
  29.4 0.0 copy-start.3
  29.4 0.8 %copy-done.3 = f32[1,64,128]{2,1,0:T(8,128)S(1)} copy-done((f32[1,64,128]{2,1,0:T(8,128)S(1)}, f32[1,64,128]{2,1,0:T(8,128)}, u32[]{:S(2)}) %copy-start.3) | copy-done | bytes 32792
  30.2 0.0 copy-start.4
  30.2 0.8 %copy-done.4 = s32[1,64,128]{2,1,0:T(8,128)S(1)} copy-done((s32[1,64,128]{2,1,0:T(8,128)S(1)}, s32[1,64,128]{2,1,0:T(8,128)}, u32[]{:S(2)}) %copy-start.4) | copy-done | bytes 32792
  30.9 0.0 copy-start.7
  30.9 0.8 %copy-done.7 = f32[1,64,128]{2,1,0:T(8,128)S(1)} copy-done((f32[1,64,128]{2,1,0:T(8,128)S(1)}, f32[1,64,128]{2,1,0:T(8,128)}, u32[]{:S(2)}) %copy-start.7) | copy-done | bytes 32792
  31.7 5.9 %remap.1 = (f32[3,64,128]{2,1,0:T(8,128)S(1)}, bf16[64,128]{1,0:T(8,128)(2,1)S(1)}, bf16[192,128]{1,0:T(8,128)(2,1)S(1)}, bf16[144,128]{1,0:T(8,128)(2,1)S(1)}, ...) custom-call(s32[128]{0:T(128)S(1)} %reshape.13.ptr_ref, ...), custom_call_target="tpu_custom_call" | custom-call | tf_op jit(solution)/shard_map/remap/pallas_call | solution.py:423
  37.5 0.1 collective-permute-start.4
  37.6 2.0 %collective-permute-start.7 = (bf16[192,128]{1,0:T(8,128)(2,1)S(1)}, bf16[192,128]{1,0:T(8,128)(2,1)S(1)}, u32[]{:S(2)}, u32[]{:S(2)}) collective-permute-start(bf16[192,128]{1,0:T(8,128)(2,1)S(1)} %get-tuple-element.31), channel_id=1, source_target_pairs={{0,4},{2,6},{4,8},{6,10},{8,12},{10,14},{12,0},{14,2},{1,5},{3,7},... | collective-permute-start | bytes 147464 | tf_op jit(solution)/shard_map/ppermute | solution.py:455
  39.6 3.5 %collective-permute-start.5 = (bf16[144,128]{1,0:T(8,128)(2,1)S(1)}, bf16[144,128]{1,0:T(8,128)(2,1)S(1)}, u32[]{:S(2)}, u32[]{:S(2)}) collective-permute-start(bf16[144,128]{1,0:T(8,128)(2,1)S(1)} %get-tuple-element.29), channel_id=1, source_target_pairs={{0,14},{2,0},{4,2},{6,4},{8,6},{10,8},{12,10},{14,12},{1,15},{3,1}... | collective-permute-start | bytes 110600 | tf_op jit(solution)/shard_map/ppermute | solution.py:455
  43.1 0.0 collective-permute-start.6
  43.1 2.6 %collective-permute-start.8 = (bf16[32,128]{1,0:T(8,128)(2,1)S(1)}, bf16[32,128]{1,0:T(8,128)(2,1)S(1)}, u32[]{:S(2)}, u32[]{:S(2)}) collective-permute-start(bf16[32,128]{1,0:T(8,128)(2,1)S(1)} %get-tuple-element.32), channel_id=1, source_target_pairs={{6,0},{10,4},{14,8},{0,6},{4,10},{8,14},{7,1},{11,5},{15,9},{1,7},... | collective-permute-start | bytes 24584 | tf_op jit(solution)/shard_map/ppermute | solution.py:455
  45.7 0.0 copy-done.6
  45.7 1.0 %prepare.1 = (s32[128,128]{1,0:T(8,128)S(1)}, s32[128,128]{1,0:T(8,128)S(1)}, bf16[256,64]{1,0:T(8,128)(2,1)S(1)}, bf16[256,64]{1,0:T(8,128)(2,1)S(1)}, bf16[256...) custom-call(s32[128,128]{1,0:T(8,128)S(1)} %bitcast.22), custom_call_target="tpu_custom_call" | custom-call | flops 62914560 | bytes 524288 | tf_op jit(solution)/shard_map/prepare/pallas_call | solution.py:403
  46.7 3.1 %collective-permute-done.8.rest_4_ = bf16[32,128]{1,0:T(8,128)(2,1)S(1)} collective-permute-done((bf16[32,128]{1,0:T(8,128)(2,1)S(1)}, bf16[32,128]{1,0:T(8,128)(2,1)S(1)}, u32[]{:S(2)}, u32[]{:S(2)}) %collective-permute-start.8) | collective-permute-done | bytes 8224 | tf_op jit(solution)/shard_map/ppermute | solution.py:455
  49.9 0.0 collective-permute-done.5.rest_1_
  49.9 0.0 collective-permute-done.6.rest_2_
  49.9 0.0 collective-permute-done.4.rest_0_
  49.9 0.0 collective-permute-done.7.rest_3_
  49.9 3.2 %finish.1 = (f32[3,64,128]{2,1,0:T(8,128)}, f32[128,128]{1,0:T(8,128)}) custom-call(bf16[192,128]{1,0:T(8,128)(2,1)S(1)} %collective-permute-done.4.rest_0_, bf16[144,128]{1,0:T(8,128)(2,1)S(1)} %collective-permute-done.5.rest_1_, bf16[144,128]{1,0:T(8,128)(2,1)S(1)} %collective-permute-done.6.rest_2_, bf16[192,128]{1,0:T(8,128)(2,1)S(1)} %collective-permute-done.7.rest_3_, ...), custom_call_target="tpu_custom_call" | custom-call | tf_op jit(solution)/shard_map/finish/pallas_call | solution.py:457
Async XLA Ops:
  0.6 1.0 %copy-start.2 = (bf16[1,8,16384]{2,1,0:T(8,128)(2,1)S(1)}, bf16[1,8,16384]{2,1,0:T(8,128)(2,1)}, u32[]{:S(2)}) copy-start(bf16[1,8,16384]{2,1,0:T(8,128)(2,1)} %param.8) | copy-start | bytes 786436
  1.6 0.8 %copy-start.5 = (s32[1,16384,1]{1,2,0:T(1,128)S(1)}, s32[1,16384,1]{1,2,0:T(1,128)}, u32[]{:S(2)}) copy-start(s32[1,16384,1]{1,2,0:T(1,128)} %param.9) | copy-start | bytes 196612
  2.4 43.3 %copy-start.6 = (s32[1,16384,1]{1,2,0:T(1,128)S(1)}, s32[1,16384,1]{1,2,0:T(1,128)}, u32[]{:S(2)}) copy-start(s32[1,16384,1]{1,2,0:T(1,128)} %param.9) | copy-start | bytes 196612
  12.6 9.1 %collective-permute-start = (bf16[256,128]{1,0:T(8,128)(2,1)S(1)}, bf16[256,128]{1,0:T(8,128)(2,1)S(1)}, u32[]{:S(2)}, u32[]{:S(2)}) collective-permute-start(bf16[256,128]{1,0:T(8,128)(2,1)S(1)} %get-tuple-element.23), channel_id=1, source_target_pairs={{0,12},{2,14},{4,0},{6,2},{8,4},{10,6},{12,8},{14,10},{1,13},{3,15... | collective-permute-start | bytes 196616 | tf_op jit(solution)/shard_map/ppermute | solution.py:402
  17.7 4.3 %collective-permute-start.1 = (bf16[256,128]{1,0:T(8,128)(2,1)S(1)}, bf16[256,128]{1,0:T(8,128)(2,1)S(1)}, u32[]{:S(2)}, u32[]{:S(2)}) collective-permute-start(bf16[256,128]{1,0:T(8,128)(2,1)S(1)} %get-tuple-element.24), channel_id=1, source_target_pairs={{0,14},{2,0},{4,2},{6,4},{8,6},{10,8},{12,10},{14,12},{1,15},{3,1}... | collective-permute-start | bytes 196616 | tf_op jit(solution)/shard_map/ppermute | solution.py:402
  19.0 7.3 %collective-permute-start.2 = (bf16[256,128]{1,0:T(8,128)(2,1)S(1)}, bf16[256,128]{1,0:T(8,128)(2,1)S(1)}, u32[]{:S(2)}, u32[]{:S(2)}) collective-permute-start(bf16[256,128]{1,0:T(8,128)(2,1)S(1)} %get-tuple-element.26), channel_id=1, source_target_pairs={{0,2},{2,4},{4,6},{6,8},{8,10},{10,12},{12,14},{14,0},{1,3},{3,5},... | collective-permute-start | bytes 196616 | tf_op jit(solution)/shard_map/ppermute | solution.py:402
  19.7 6.6 %collective-permute-start.3 = (bf16[256,128]{1,0:T(8,128)(2,1)S(1)}, bf16[256,128]{1,0:T(8,128)(2,1)S(1)}, u32[]{:S(2)}, u32[]{:S(2)}) collective-permute-start(bf16[256,128]{1,0:T(8,128)(2,1)S(1)} %get-tuple-element.27), channel_id=1, source_target_pairs={{0,4},{2,6},{4,8},{6,10},{8,12},{10,14},{12,0},{14,2},{1,5},{3,7},... | collective-permute-start | bytes 196616 | tf_op jit(solution)/shard_map/ppermute | solution.py:402
  26.3 2.2 %copy-start = (bf16[1,1,1,64,2,128,128]{6,5,4,3,2,1,0:T(8,128)(2,1)S(1)}, bf16[1,1,1,64,2,128,128]{6,5,4,3,2,1,0:T(8,128)(2,1)}, u32[]{:S(2)}) copy-start(bf16[1,1,1,64,2,128,128]{6,5,4,3,2,1,0:T(8,128)(2,1)} %param.11) | copy-start | bytes 12582916
  28.5 0.9 %copy-start.1 = (f32[1,3,64,128]{3,2,1,0:T(8,128)S(1)}, f32[1,3,64,128]{3,2,1,0:T(8,128)}, u32[]{:S(2)}) copy-start(f32[1,3,64,128]{3,2,1,0:T(8,128)} %param.12) | copy-start | bytes 294916
  29.4 0.8 %copy-start.3 = (f32[1,64,128]{2,1,0:T(8,128)S(1)}, f32[1,64,128]{2,1,0:T(8,128)}, u32[]{:S(2)}) copy-start(f32[1,64,128]{2,1,0:T(8,128)} %param.14) | copy-start | bytes 98308
  30.2 0.8 %copy-start.4 = (s32[1,64,128]{2,1,0:T(8,128)S(1)}, s32[1,64,128]{2,1,0:T(8,128)}, u32[]{:S(2)}) copy-start(s32[1,64,128]{2,1,0:T(8,128)} %param.15) | copy-start | bytes 98308
  30.9 0.8 %copy-start.7 = (f32[1,64,128]{2,1,0:T(8,128)S(1)}, f32[1,64,128]{2,1,0:T(8,128)}, u32[]{:S(2)}) copy-start(f32[1,64,128]{2,1,0:T(8,128)} %param.13) | copy-start | bytes 98308
  37.5 12.3 %collective-permute-start.4 = (bf16[192,128]{1,0:T(8,128)(2,1)S(1)}, bf16[192,128]{1,0:T(8,128)(2,1)S(1)}, u32[]{:S(2)}, u32[]{:S(2)}) collective-permute-start(bf16[192,128]{1,0:T(8,128)(2,1)S(1)} %get-tuple-element.28), channel_id=1, source_target_pairs={{0,12},{2,14},{4,0},{6,2},{8,4},{10,6},{12,8},{14,10},{1,13},{3,15... | collective-permute-start | bytes 147464 | tf_op jit(solution)/shard_map/ppermute | solution.py:455
  37.6 12.3 %collective-permute-start.7 = (bf16[192,128]{1,0:T(8,128)(2,1)S(1)}, bf16[192,128]{1,0:T(8,128)(2,1)S(1)}, u32[]{:S(2)}, u32[]{:S(2)}) collective-permute-start(bf16[192,128]{1,0:T(8,128)(2,1)S(1)} %get-tuple-element.31), channel_id=1, source_target_pairs={{0,4},{2,6},{4,8},{6,10},{8,12},{10,14},{12,0},{14,2},{1,5},{3,7},... | collective-permute-start | bytes 147464 | tf_op jit(solution)/shard_map/ppermute | solution.py:455
  39.6 10.3 %collective-permute-start.5 = (bf16[144,128]{1,0:T(8,128)(2,1)S(1)}, bf16[144,128]{1,0:T(8,128)(2,1)S(1)}, u32[]{:S(2)}, u32[]{:S(2)}) collective-permute-start(bf16[144,128]{1,0:T(8,128)(2,1)S(1)} %get-tuple-element.29), channel_id=1, source_target_pairs={{0,14},{2,0},{4,2},{6,4},{8,6},{10,8},{12,10},{14,12},{1,15},{3,1}... | collective-permute-start | bytes 110600 | tf_op jit(solution)/shard_map/ppermute | solution.py:455
  43.1 6.7 %collective-permute-start.6 = (bf16[144,128]{1,0:T(8,128)(2,1)S(1)}, bf16[144,128]{1,0:T(8,128)(2,1)S(1)}, u32[]{:S(2)}, u32[]{:S(2)}) collective-permute-start(bf16[144,128]{1,0:T(8,128)(2,1)S(1)} %get-tuple-element.30), channel_id=1, source_target_pairs={{0,2},{2,4},{4,6},{6,8},{8,10},{10,12},{12,14},{14,0},{1,3},{3,5},... | collective-permute-start | bytes 110600 | tf_op jit(solution)/shard_map/ppermute | solution.py:455
  43.1 6.7 %collective-permute-start.8 = (bf16[32,128]{1,0:T(8,128)(2,1)S(1)}, bf16[32,128]{1,0:T(8,128)(2,1)S(1)}, u32[]{:S(2)}, u32[]{:S(2)}) collective-permute-start(bf16[32,128]{1,0:T(8,128)(2,1)S(1)} %get-tuple-element.32), channel_id=1, source_target_pairs={{6,0},{10,4},{14,8},{0,6},{4,10},{8,14},{7,1},{11,5},{15,9},{1,7},... | collective-permute-start | bytes 24584 | tf_op jit(solution)/shard_map/ppermute | solution.py:455

commit v2 on v1

--- a/solution.py
+++ b/solution.py
@@ -16,6 +16,7 @@
 F32 = jnp.float32
 BF16 = jnp.bfloat16
 I32 = jnp.int32
+SORT_UNIT = 16
 VMEM_LIMIT = 48 * 1024 * 1024
 
 
@@ -59,89 +60,113 @@
     return result
 
 
-def route_kernel(
-    count_s, total, dest_ref, x_ref, *rest
-):
-    outs = rest[:NEIGHBOR_TILES]
-    comb, sorted_scr, place, pos_scr, vec, scal, sem = rest[NEIGHBOR_TILES:]
+def route_kernel(count_s, total, x_hbm, dest_hbm, *rest):
+    staged = len(rest) - NEIGHBOR_TILES - 8
+    sources, rest = rest[: staged // 2], rest[staged // 2 :]
+    outs, dest_ref, rest = rest[:NEIGHBOR_TILES], rest[NEIGHBOR_TILES], rest[NEIGHBOR_TILES + 1 :]
+    targets, rest = rest[: staged // 2], rest[staged // 2 :]
+    x_ref, comb, place, pos_scr, vec, scal, sem = rest
+    copies = [
+        pltpu.make_async_copy(a, b, sem.at[i])
+        for i, (a, b) in enumerate(
+            zip((dest_hbm, x_hbm) + tuple(sources), (dest_ref, x_ref) + tuple(targets))
+        )
+    ]
+    for copy in copies:
+        copy.start()
+    copies[0].wait()
     blocks = dest_ref.shape[0]
+    unit = SORT_UNIT
     groups = outs[0].shape[0] // 4
     stride = (groups + 1) * 8
     offsets = offsets_of(dest_ref[...], count_s, total)
-    parts = ranks(offsets)
     ones8 = jnp.ones((8, LANES), BF16)
     sub8 = iota((8, blocks), 0)
-    before = ones_where(iota((blocks, blocks), 0) < iota((blocks, blocks), 1))
+    earlier = ones_where(iota((blocks, blocks), 0) < iota((blocks, blocks), 1))
+    before = ones_where(iota((LANES, 2 * LANES), 0) < iota((LANES, 2 * LANES), 1))
+    hots = [ones_where(offsets == o) for o in range(NEIGHBOR_TILES)]
+    counts = jnp.zeros((8, blocks), F32)
     start_t = jnp.zeros((8, blocks), F32)
-    base_t = jnp.zeros((8, blocks), F32)
-    starts_t = jnp.zeros((8, blocks), F32)
+    starts = jnp.zeros((8, blocks), F32)
+    for o, hot in enumerate(hots):
+        count_t = dot_t(ones8, hot)
+        counts = jnp.where(sub8 == o, count_t, counts)
+        starts = jnp.where(sub8 == o, start_t, starts)
+        start_t = start_t + count_t
+    base = dot(counts.astype(BF16), earlier).astype(I32)
+    counts, starts = counts.astype(I32), starts.astype(I32)
+    at = jnp.bitwise_and(base, LANES - 1)
+    vec[0:8, :] = sub8 * stride + lax.shift_right_logical(base, 7) * 8
+    vec[8:16, :] = jnp.bitwise_and(at - starts, LANES - 1)
+    vec[16:24, :] = at
+    vec[24:32, :] = at + counts - LANES
+    copy = pltpu.make_async_copy(vec, scal, sem.at[len(copies)])
+    copy.start()
     start = jnp.zeros((blocks, LANES), F32)
     pos = jnp.zeros((blocks, LANES), F32)
-    for o, (mask, hot, inside, count, base) in enumerate(parts):
-        pos = jnp.where(mask, start + inside, pos)
-        start = start + count
-        count_t = dot_t(ones8, hot)
-        base_row = dot(count_t.astype(BF16), before)
-        base_t = jnp.where(sub8 == o, base_row, base_t)
-        starts_t = jnp.where(sub8 == o, start_t, starts_t)
-        start_t = start_t + count_t
-    starts_t = jnp.where(sub8 == NEIGHBOR_TILES, start_t, starts_t)
-    vec[0:8, :] = base_t.astype(I32)
-    vec[8:16, :] = starts_t.astype(I32)
-    copy = pltpu.make_async_copy(vec, scal, sem)
-    copy.start()
+    for o, hot in enumerate(hots):
+        inside = dot(hot, before)
+        pos = jnp.where(offsets == o, start + inside[:, :LANES], pos)
+        start = start + inside[:, LANES:]
     pos_scr[...] = pos.astype(I32)
     f, g = iota((8, 8), 1), jnp.bitwise_and(iota((8, 8), 0), 3)
     plus = ((g == 0) & (f == 0)) | ((g == 1) & (f == 1)) | ((g == 2) & (f == 3)) | ((g == 3) & (f >= 6))
     minus = ((g == 2) & (f == 2)) | ((g == 3) & ((f == 4) | (f == 5)))
     combine = (jnp.where(plus, 1.0, 0.0) - jnp.where(minus, 1.0, 0.0)).astype(BF16)
+    copies[1].wait()
     comb[...] = dot(combine, x_ref[...]).astype(BF16)
-    rows_id = iota((LANES, LANES), 0)
-
-    def sort_step(i, carry):
-        for u in range(8):
-            b = i * 8 + u
-            hot = ones_where(pos_scr[pl.ds(b, 1), :] == rows_id)
-            columns = comb[:, pl.ds(pl.multiple_of(b * LANES, LANES), LANES)]
-            sorted_scr[pl.ds(pl.multiple_of(b * 8, 8), 8), :] = dot_t(columns, hot)
-        return carry
-
-    lax.fori_loop(0, blocks // 8, sort_step, 0)
+
+    lines = iota((LANES, LANES), 0)
+
+    def sort_blocks(i):
+        result = []
+        for u in range(0, unit, 2):
+            b = i * unit + u
+            columns = comb[:, pl.ds(pl.multiple_of(b * LANES, 2 * LANES), 2 * LANES)].astype(F32)
+            columns = jnp.concatenate([columns[:, :LANES], columns[:, LANES:]], axis=0).astype(BF16)
+            hot = [ones_where(pos_scr[pl.ds(b + v, 1), :] == lines) for v in range(2)]
+            both = dot_t(columns, jnp.concatenate(hot, axis=0))
+            result += [both[:8, :LANES], both[8:, LANES:]]
+        return result
+
+    lane = iota((8, LANES), 1)
+
+    def place_blocks(i, values, current):
+        current = list(current)
+        for u in range(unit):
+            b = i * unit + u
+            for o in range(NEIGHBOR_TILES):
+                turned = pltpu.roll(values[u], scal[8 + o, b], 1)
+                merged = jnp.where(lane < scal[16 + o, b], current[o], turned)
+                place[pl.ds(pl.multiple_of(scal[o, b], 8), 8), :] = merged
+                current[o] = jnp.where(lane < scal[24 + o, b], turned, merged)
+        return current
+
+    def step(i, carry):
+        values = sort_blocks(i + 1)
+        return tuple(place_blocks(i, carry[NEIGHBOR_TILES:], carry[:NEIGHBOR_TILES])) + tuple(values)
+
+    steps = blocks // unit
+    current = [jnp.zeros((8, LANES), F32) for _ in range(NEIGHBOR_TILES)]
+    values = sort_blocks(0)
     copy.wait()
-    lane = iota((8, LANES), 1)
-
-    def place_step(i, current):
-        current = list(current)
-        for u in range(4):
-            b = i * 4 + u
-            values = sorted_scr[pl.ds(pl.multiple_of(b * 8, 8), 8), :]
-            for o in range(NEIGHBOR_TILES):
-                base = scal[o, b]
-                first = scal[8 + o, b]
-                length = scal[9 + o, b] - first
-                at = jnp.bitwise_and(base, LANES - 1)
-                turned = pltpu.roll(values, jnp.bitwise_and(at - first, LANES - 1), 1)
-                merged = jnp.where(lane < at, current[o], turned)
-                row = pl.multiple_of(o * stride + lax.shift_right_logical(base, 7) * 8, 8)
-                place[pl.ds(row, 8), :] = merged
-                current[o] = jnp.where(lane < at + length - LANES, turned, merged)
-        return tuple(current)
-
-    current = lax.fori_loop(
-        0, blocks // 4, place_step, tuple(jnp.zeros((8, LANES), F32) for _ in range(NEIGHBOR_TILES))
-    )
+    carry = lax.fori_loop(0, steps - 1, step, tuple(current) + tuple(values))
+    current = place_blocks(steps - 1, carry[NEIGHBOR_TILES:], carry[:NEIGHBOR_TILES])
     pair_lane = jnp.where(iota((8, LANES), 0) < 4, lane, lane + LANES)
     upper = iota((groups // 2, 8, LANES), 1) < 4
     slot = iota((groups // 2, 8, LANES), 0) * (2 * LANES) + pair_lane[None]
-    for o in range(NEIGHBOR_TILES):
-        last = blocks - 1
-        count = scal[o, last] + scal[9 + o, last] - scal[8 + o, last]
-        row = pl.multiple_of(o * stride + lax.shift_right_logical(count, 7) * 8, 8)
-        place[pl.ds(row, 8), :] = current[o]
+    last = blocks - 1
+    for o in range(NEIGHBOR_TILES):
+        row = scal[o, last] - o * stride
+        count = row * (LANES // 8) + scal[24 + o, last] + LANES
+        full = lax.shift_right_logical(count, 7) * 8 + o * stride
+        place[pl.ds(pl.multiple_of(full, 8), 8), :] = current[o]
         tiles = place[o * stride : o * stride + groups * 8, :].reshape(groups // 2, 2, 8, LANES)
         both = jnp.where(upper, tiles[:, 0], tiles[:, 1])
         both = jnp.where(slot < count, both, 0.0)
         outs[o][...] = both.reshape(groups * 4, LANES).astype(BF16)
+    for copy in copies[2:]:
+        copy.wait()
 
 
 def prepare_kernel(count_s, total, dest_ref, index_ref, code_ref, *hot_refs):
@@ -174,78 +199,95 @@
     return packed
 
 
-def remap_kernel(messages, ptr_ref, *rest):
+def remap_kernel(messages, *rest):
     arrived = rest[:NEIGHBOR_TILES]
-    (row_ref, w_ref, ocean_ref, skin_ref, depth_ref, mask_ref) = rest[NEIGHBOR_TILES : NEIGHBOR_TILES + 6]
-    outs = rest[NEIGHBOR_TILES + 6 :]
+    ptr_hbm, row_ref, w_ref, ocean_ref, skin_ref, depth_ref, mask_ref = rest[
+        NEIGHBOR_TILES : NEIGHBOR_TILES + 7
+    ]
+    outs = rest[NEIGHBOR_TILES + 7 :]
     forcing_ref, own_ref = outs[:2]
     message_refs = outs[2 : 2 + len(messages)]
-    slots, mapped, shares = outs[2 + len(messages) :]
-    step = pl.program_id(0)
-    per_step = w_ref.shape[0]
+    slots, mapped, shares, ptr_ref, sem = outs[2 + len(messages) :]
+    pointers = pltpu.make_async_copy(ptr_hbm, ptr_ref, sem)
+    pointers.start()
+    per_step = 8
     size = arrived[0].shape[0]
-
-    @pl.when(step == 0)
-    def _():
-        for o in range(NEIGHBOR_TILES):
-            slots[o * size : (o + 1) * size, :] = arrived[o][...].astype(F32)
-        slots[NEIGHBOR_TILES * size :, :] = jnp.zeros((8, LANES), F32)
-
-    for j in range(per_step):
-        k = step * per_step + j
-        total = None
+    for o in range(NEIGHBOR_TILES):
+        slots[o * size : (o + 1) * size, :] = arrived[o][...].astype(F32)
+    slots[NEIGHBOR_TILES * size :, :] = jnp.zeros((8, LANES), F32)
+    pointers.wait()
+    sub = iota((per_step, LANES), 0)
+
+    def forward(step):
+        for j in range(per_step):
+            k = step * per_step + j
+            both = [slots[pl.ds(ptr_ref[w, k] * 4, 8), :] for w in range(2)]
+            both = jnp.concatenate(both, axis=0).astype(BF16)
+            product = dot_t(both, w_ref[k].reshape(2 * LANES, LANES))
+            mapped[pl.ds(k * 8, 8), :] = product[:8, :LANES] + product[8:, LANES:]
+
+    def middle(step):
+        rows = pl.ds(step * per_step, per_step)
+        u, v, p, h = (mapped[pl.ds(step * per_step * 8 + i, per_step, stride=8), :] for i in range(4))
+        speed = jnp.sqrt(u * u + v * v + 1.0)
+        forcing_ref[0, rows, :] = 0.2 * speed * u
+        forcing_ref[1, rows, :] = 0.2 * speed * v
+        forcing_ref[2, rows, :] = 0.5 * p
+        return (skin_ref[rows, :] + 0.25 * mask_ref[rows, :].astype(F32) * h).astype(BF16).astype(F32)
+
+    def back(step, sst):
+        left = []
+        for j in range(per_step):
+            only = jnp.where(sub == j, sst, 0.0)
+            zero = jnp.zeros_like(only)
+            left.append(jnp.concatenate([only, zero], axis=0).astype(BF16))
+            left.append(jnp.concatenate([zero, only], axis=0).astype(BF16))
+        left = jnp.concatenate(left, axis=1)
+        right = w_ref[pl.ds(step * per_step, per_step)].reshape(per_step * 2 * LANES, LANES)
+        total = dot(left, right)
         for w in range(2):
-            block = slots[pl.ds(ptr_ref[2 * k + w] * 4, 8), :].astype(BF16)
-            product = dot_t(block, w_ref[j, w])
-            total = product if total is None else total + product
-        mapped[j * 8 : j * 8 + 8, :] = total
-    u, v, p, h = (mapped[pl.ds(i, per_step, stride=8), :] for i in range(4))
-    rows = pl.ds(pl.multiple_of(step * per_step, per_step), per_step)
-    speed = jnp.sqrt(u * u + v * v + 1.0)
-    forcing_ref[0, rows, :] = 0.2 * speed * u
-    forcing_ref[1, rows, :] = 0.2 * speed * v
-    forcing_ref[2, rows, :] = 0.5 * p
-    sst = (skin_ref[rows, :] + 0.25 * mask_ref[rows, :].astype(F32) * h).astype(BF16).astype(F32)
-    sub = iota((per_step, LANES), 0)
-    for w in range(2):
-        total = None
-        for j in range(per_step):
-            product = dot(jnp.where(sub == j, sst, 0.0).astype(BF16), w_ref[j, w])
-            total = product if total is None else total + product
-        shares[pl.ds(step * (2 * per_step) + w, per_step, stride=2), :] = total
-
-    @pl.when(step == pl.num_programs(0) - 1)
-    def _():
-        count = shares.shape[0]
-        every = shares[...]
-        high = every.astype(BF16)
-        low = (every - high.astype(F32)).astype(BF16)
-        groups = own_ref.shape[0]
-        returned = []
-        for o in range(NEIGHBOR_TILES):
-            hot = ones_where(iota((groups, count), 0) + o * groups == row_ref[...])
-            returned.append((dot(hot, high) + dot(hot, low)).astype(BF16))
-        own_ref[...] = returned[MIDDLE]
-        fields = [ocean_ref[0], ocean_ref[1], ocean_ref[2], mask_ref[...].astype(F32), depth_ref[...]]
-        fields += [forcing_ref[0], forcing_ref[1], forcing_ref[2]]
-        high_columns = packed_columns(fields, False)
-        low_columns = packed_columns(fields, True)
-        tall = fields[0].shape[0]
-        for (pairs, parts), out in zip(messages, message_refs):
-            at = 0
-            for kind, length in parts:
-                if kind[0] == "ret":
-                    value = returned[kind[1]]
+            rows = slice((w * steps + step) * per_step, (w * steps + step + 1) * per_step)
+            shares[rows, :] = total[w * per_step : (w + 1) * per_step]
+
+    steps = w_ref.shape[0] // per_step
+    for i in range(steps):
+        forward(i)
+    for i in range(steps):
+        back(i, middle(i))
+
+    every = shares[...]
+    high = every.astype(BF16)
+    low = (every - high.astype(F32)).astype(BF16)
+    split = jnp.concatenate([high, low], axis=1)
+    count = shares.shape[0]
+    groups = own_ref.shape[0]
+    returned = []
+    row = jnp.concatenate([row_ref[0:1, :], row_ref[1:2, :]], axis=1)
+    for o in range(NEIGHBOR_TILES):
+        hot = ones_where(iota((groups, count), 0) + o * groups == row)
+        value = dot(hot, split)
+        returned.append((value[:, :LANES] + value[:, LANES:]).astype(BF16))
+    own_ref[...] = returned[MIDDLE]
+    fields = [ocean_ref[0], ocean_ref[1], ocean_ref[2], mask_ref[...].astype(F32), depth_ref[...]]
+    fields += [forcing_ref[0], forcing_ref[1], forcing_ref[2]]
+    high_columns = packed_columns(fields, False)
+    low_columns = packed_columns(fields, True)
+    tall = fields[0].shape[0]
+    for (pairs, parts), out in zip(messages, message_refs):
+        at = 0
+        for kind, length in parts:
+            if kind[0] == "ret":
+                value = returned[kind[1]]
+            else:
+                _, dt, ds = kind
+                span = {1: slice(tall - HALO, tall), 0: slice(0, tall), -1: slice(0, HALO)}[dt]
+                if ds:
+                    value = (high_columns if ds > 0 else low_columns)[span]
                 else:
-                    _, dt, ds = kind
-                    span = {1: slice(tall - HALO, tall), 0: slice(0, tall), -1: slice(0, HALO)}[dt]
-                    if ds:
-                        value = (high_columns if ds > 0 else low_columns)[span]
-                    else:
-                        value = jnp.concatenate([x[span] for x in fields], axis=0)
-                    value = value.astype(BF16)
-                out[at : at + length, :] = value
-                at += length
+                    value = jnp.concatenate([x[span] for x in fields], axis=0)
+                value = value.astype(BF16)
+            out[at : at + length, :] = value
+            at += length
 
 
 def finish_kernel(messages, count_t, count_s, *rest):
@@ -378,23 +420,36 @@
     destination = air_destination.reshape(blocks, LANES)
     vmem = pl.BlockSpec(memory_space=pltpu.VMEM)
     params = pltpu.CompilerParams(vmem_limit_bytes=VMEM_LIMIT)
-    outbound = pl.pallas_call(
+    hbm = pl.BlockSpec(memory_space=pltpu.HBM)
+    pointers = diagonal_group_pointer[0, 0, 0].T
+    to_stage = (
+        pointers,
+        interpolation_factors[0, 0, 0],
+        marine_fields[0],
+        skin_warmth_anomaly[0],
+        gravity_bathymetry[0],
+        marine_indicator[0],
+    )
+    results = pl.pallas_call(
         functools.partial(route_kernel, count_s, total),
-        out_shape=[jax.ShapeDtypeStruct((groups * 4, LANES), BF16)] * NEIGHBOR_TILES,
-        in_specs=[vmem, vmem],
-        out_specs=[vmem] * NEIGHBOR_TILES,
+        out_shape=[jax.ShapeDtypeStruct((groups * 4, LANES), BF16)] * NEIGHBOR_TILES
+        + [jax.ShapeDtypeStruct(a.shape, a.dtype) for a in (destination,) + to_stage],
+        in_specs=[hbm] * (2 + len(to_stage)),
+        out_specs=[vmem] * (NEIGHBOR_TILES + 1 + len(to_stage)),
         scratch_shapes=[
             pltpu.VMEM((8, columns), BF16),
-            pltpu.VMEM((blocks * 8, LANES), F32),
+            pltpu.VMEM((8, columns), BF16),
             pltpu.VMEM((NEIGHBOR_TILES * (groups + 1) * 8, LANES), F32),
             pltpu.VMEM((blocks, LANES), I32),
-            pltpu.VMEM((16, blocks), I32),
-            pltpu.SMEM((16, blocks), I32),
-            pltpu.SemaphoreType.DMA,
+            pltpu.VMEM((32, blocks), I32),
+            pltpu.SMEM((32, blocks), I32),
+            pltpu.SemaphoreType.DMA((3 + len(to_stage),)),
         ],
         compiler_params=params,
         name="route",
-    )(destination, air_exchanges[0])
+    )(*(pltpu.with_memory_space_constraint(a, pltpu.HBM) for a in (air_exchanges[0], destination) + to_stage))
+    outbound = results[:NEIGHBOR_TILES]
+    destination, rows, weights, ocean, skin, depth, mask = results[NEIGHBOR_TILES:]
     arrived = list(outbound)
     for o in range(NEIGHBOR_TILES):
         if o != MIDDLE:
@@ -411,15 +466,10 @@
         name="prepare",
     )(destination)
 
-    pointers = diagonal_group_pointer.reshape(-1)
-    weights = interpolation_factors[0, 0, 0]
-    tall = skin_warmth_anomaly.shape[1]
+    tall = skin.shape[0]
     messages = plan_messages(count_t, count_s, groups, tall)
     lengths = [sum(n for _, n in parts) for _, parts in messages]
     row_blocks = weights.shape[0]
-    per_step = 8
-    whole = lambda shape: pl.BlockSpec(shape, lambda i, p: (0,) * len(shape))
-    ocean, depth, mask = marine_fields[0], gravity_bathymetry[0], marine_indicator[0]
     outs = pl.pallas_call(
         functools.partial(remap_kernel, messages),
         out_shape=[
@@ -427,29 +477,18 @@
             jax.ShapeDtypeStruct((groups, LANES), BF16),
         ]
         + [jax.ShapeDtypeStruct((n, LANES), BF16) for n in lengths],
-        grid_spec=pltpu.PrefetchScalarGridSpec(
-            num_scalar_prefetch=1,
-            grid=(row_blocks // per_step,),
-            in_specs=[whole((groups * 4, LANES))] * NEIGHBOR_TILES
-            + [
-                whole((1, 2 * row_blocks)),
-                pl.BlockSpec((per_step, 2, LANES, LANES), lambda i, p: (i, 0, 0, 0)),
-                whole((3, tall, LANES)),
-                whole((tall, LANES)),
-                whole((tall, LANES)),
-                whole((tall, LANES)),
-            ],
-            out_specs=[whole((3, tall, LANES)), whole((groups, LANES))]
-            + [whole((n, LANES)) for n in lengths],
-            scratch_shapes=[
-                pltpu.VMEM((NEIGHBOR_TILES * groups * 4 + 8, LANES), F32),
-                pltpu.VMEM((per_step * 8, LANES), F32),
-                pltpu.VMEM((2 * row_blocks, LANES), F32),
-            ],
-        ),
+        in_specs=[vmem] * NEIGHBOR_TILES + [hbm] + [vmem] * 6,
+        out_specs=[vmem] * (2 + len(lengths)),
+        scratch_shapes=[
+            pltpu.VMEM((NEIGHBOR_TILES * groups * 4 + 8, LANES), F32),
+            pltpu.VMEM((row_blocks * 8, LANES), F32),
+            pltpu.VMEM((2 * row_blocks, LANES), F32),
+            pltpu.SMEM(pointers.shape, I32),
+            pltpu.SemaphoreType.DMA,
+        ],
         compiler_params=params,
         name="remap",
-    )(pointers, *arrived, pointers.reshape(1, -1), weights, ocean, skin_warmth_anomaly[0], depth, mask)
+    )(*arrived, pltpu.with_memory_space_constraint(pointers, pltpu.HBM), rows, weights, ocean, skin, depth, mask)
     forcing, own = outs[:2]
     received = [
         lax.ppermute(message, axes, pairs) for message, (pairs, _) in zip(outs[2:], messages)

time: 53.6 us -> 37.6 us (0.70)
  Pallas kernels: 20.2 us -> 11.6 us
  local copies, waits for them, and re-layouts: 8.18 us -> 0 us
  waiting for transfers between devices: 7.78 us -> 8.85 us
    unnamed x17 -> x0, local copies, waits for them, and re-layouts: 7.91 us -> none
    pallas_call x1, Pallas kernels: 10.1 us -> 4.79 us  [shards(): pl.pallas_call(functools.partial(route_kernel, count_s, total), out_shape...]
    pallas_call x1, Pallas kernels: 5.86 us -> 2.66 us  [shards(): pl.pallas_call(functools.partial(remap_kernel, messages), out_shape=[jax....]
    ppermute x4, waiting for transfers between devices: 4.63 us -> 5.69 us  [shards(): arrived[o] = lax.ppermute(outbound[o], axes, pairs)]
  transfers between devices with their start and end apart: 9 -> 9, of which waited for: 3 -> 3; matrix products, arithmetic and copies ran while one was open for 2% -> 0% of each run, Pallas kernels for 2% -> 3%
where the time goes in v2:
time: 37.6 us; the launch traced here: 37.4 us
  starting transfers between devices  16.2 us (43%)
  Pallas kernels  11.6 us (31%)
  waiting for transfers between devices  8.85 us (24%)
  between operations  0.69 us (2%)
    ppermute x5, starting transfers between devices, shards(): lax.ppermute(message, axes, pairs)  8.16 us
    ppermute x4, starting transfers between devices, shards(): arrived[o] = lax.ppermute(outbound[o], axes, pairs)  8.06 us
    ppermute x4, waiting for transfers between devices, shards(): arrived[o] = lax.ppermute(outbound[o], axes, pairs)  5.69 us
    pallas_call x1, Pallas kernels, shards(): pl.pallas_call(functools.partial(route_kernel, count_s, total), out_shape...  4.79 us
    pallas_call x1, Pallas kernels, shards(): pl.pallas_call(functools.partial(finish_kernel, messages, count_t, count_...  3.19 us
    ppermute x5, waiting for transfers between devices, shards(): lax.ppermute(message, axes, pairs)  3.16 us
    pallas_call x1, Pallas kernels, shards(): pl.pallas_call(functools.partial(remap_kernel, messages), out_shape=[jax....  2.66 us
    pallas_call x1, Pallas kernels, shards(): pl.pallas_call(functools.partial(prepare_kernel, count_s, total), out_sha...  1 us
  transfers between devices with their start and end apart: 9, of which 3 were waited for; matrix products, arithmetic and copies ran while one was open for 0% of the time, Pallas kernels for 3%

profile of v2, /device:TPU:0, one launch (start us, length us, event | category | flops | bytes accessed | tf_op | source)
XLA Modules:
  0.0 37.4 jit_solution(8753598312729246955)
XLA Ops:
  0.6 4.8 %route.1 = (bf16[256,128]{1,0:T(8,128)(2,1)S(1)}, bf16[256,128]{1,0:T(8,128)(2,1)S(1)}, bf16[256,128]{1,0:T(8,128)(2,1)S(1)}, bf16[256,128]{1,0:T(8,128)(2,1)S(1...) custom-call(bf16[8,16384]{1,0:T(8,128)(2,1)} %bitcast.13, ...), custom_call_target="tpu_custom_call" | custom-call | tf_op jit(solution)/shard_map/route/pallas_call | solution.py:433
  5.4 5.1 %collective-permute-start = (bf16[256,128]{1,0:T(8,128)(2,1)S(1)}, bf16[256,128]{1,0:T(8,128)(2,1)S(1)}, u32[]{:S(2)}, u32[]{:S(2)}) collective-permute-start(bf16[256,128]{1,0:T(8,128)(2,1)S(1)} %get-tuple-element.30), channel_id=1, source_target_pairs={{0,12},{2,14},{4,0},{6,2},{8,4},{10,6},{12,8},{14,10},{1,13},{3,15... | collective-permute-start | bytes 196616 | tf_op jit(solution)/shard_map/ppermute | solution.py:457
  10.5 1.4 %collective-permute-start.1 = (bf16[256,128]{1,0:T(8,128)(2,1)S(1)}, bf16[256,128]{1,0:T(8,128)(2,1)S(1)}, u32[]{:S(2)}, u32[]{:S(2)}) collective-permute-start(bf16[256,128]{1,0:T(8,128)(2,1)S(1)} %get-tuple-element.31), channel_id=1, source_target_pairs={{0,14},{2,0},{4,2},{6,4},{8,6},{10,8},{12,10},{14,12},{1,15},{3,1}... | collective-permute-start | bytes 196616 | tf_op jit(solution)/shard_map/ppermute | solution.py:457
  11.9 0.6 %collective-permute-start.2 = (bf16[256,128]{1,0:T(8,128)(2,1)S(1)}, bf16[256,128]{1,0:T(8,128)(2,1)S(1)}, u32[]{:S(2)}, u32[]{:S(2)}) collective-permute-start(bf16[256,128]{1,0:T(8,128)(2,1)S(1)} %get-tuple-element.33), channel_id=1, source_target_pairs={{0,2},{2,4},{4,6},{6,8},{8,10},{10,12},{12,14},{14,0},{1,3},{3,5},... | collective-permute-start | bytes 196616 | tf_op jit(solution)/shard_map/ppermute | solution.py:457
  12.6 0.9 %collective-permute-start.3 = (bf16[256,128]{1,0:T(8,128)(2,1)S(1)}, bf16[256,128]{1,0:T(8,128)(2,1)S(1)}, u32[]{:S(2)}, u32[]{:S(2)}) collective-permute-start(bf16[256,128]{1,0:T(8,128)(2,1)S(1)} %get-tuple-element.34), channel_id=1, source_target_pairs={{0,4},{2,6},{4,8},{6,10},{8,12},{10,14},{12,0},{14,2},{1,5},{3,7},... | collective-permute-start | bytes 196616 | tf_op jit(solution)/shard_map/ppermute | solution.py:457
  13.5 0.0 collective-permute-done.rest_0_
  13.5 1.3 %collective-permute-done.1.rest_1_ = bf16[256,128]{1,0:T(8,128)(2,1)S(1)} collective-permute-done((bf16[256,128]{1,0:T(8,128)(2,1)S(1)}, bf16[256,128]{1,0:T(8,128)(2,1)S(1)}, u32[]{:S(2)}, u32[]{:S(2)}) %collective-permute-start.1) | collective-permute-done | bytes 65568 | tf_op jit(solution)/shard_map/ppermute | solution.py:457
  14.8 4.4 %collective-permute-done.2.rest_3_ = bf16[256,128]{1,0:T(8,128)(2,1)S(1)} collective-permute-done((bf16[256,128]{1,0:T(8,128)(2,1)S(1)}, bf16[256,128]{1,0:T(8,128)(2,1)S(1)}, u32[]{:S(2)}, u32[]{:S(2)}) %collective-permute-start.2) | collective-permute-done | bytes 65568 | tf_op jit(solution)/shard_map/ppermute | solution.py:457
  19.2 0.0 collective-permute-done.3.rest_4_
  19.2 2.7 %remap.1 = (f32[3,64,128]{2,1,0:T(8,128)S(1)}, bf16[64,128]{1,0:T(8,128)(2,1)S(1)}, bf16[192,128]{1,0:T(8,128)(2,1)S(1)}, bf16[144,128]{1,0:T(8,128)(2,1)S(1)}, ...) custom-call(bf16[256,128]{1,0:T(8,128)(2,1)S(1)} %collective-permute-done.rest_0_, ...), custom_call_target="tpu_custom_call" | custom-call | tf_op jit(solution)/shard_map/remap/pallas_call | solution.py:473
  21.8 0.1 collective-permute-start.4
  21.9 2.0 %collective-permute-start.7 = (bf16[192,128]{1,0:T(8,128)(2,1)S(1)}, bf16[192,128]{1,0:T(8,128)(2,1)S(1)}, u32[]{:S(2)}, u32[]{:S(2)}) collective-permute-start(bf16[192,128]{1,0:T(8,128)(2,1)S(1)} %get-tuple-element.44), channel_id=1, source_target_pairs={{0,4},{2,6},{4,8},{6,10},{8,12},{10,14},{12,0},{14,2},{1,5},{3,7},... | collective-permute-start | bytes 147464 | tf_op jit(solution)/shard_map/ppermute | solution.py:494
  23.9 3.5 %collective-permute-start.5 = (bf16[144,128]{1,0:T(8,128)(2,1)S(1)}, bf16[144,128]{1,0:T(8,128)(2,1)S(1)}, u32[]{:S(2)}, u32[]{:S(2)}) collective-permute-start(bf16[144,128]{1,0:T(8,128)(2,1)S(1)} %get-tuple-element.42), channel_id=1, source_target_pairs={{0,14},{2,0},{4,2},{6,4},{8,6},{10,8},{12,10},{14,12},{1,15},{3,1}... | collective-permute-start | bytes 110600 | tf_op jit(solution)/shard_map/ppermute | solution.py:494
  27.4 0.0 collective-permute-start.6
  27.4 2.6 %collective-permute-start.8 = (bf16[32,128]{1,0:T(8,128)(2,1)S(1)}, bf16[32,128]{1,0:T(8,128)(2,1)S(1)}, u32[]{:S(2)}, u32[]{:S(2)}) collective-permute-start(bf16[32,128]{1,0:T(8,128)(2,1)S(1)} %get-tuple-element.45), channel_id=1, source_target_pairs={{6,0},{10,4},{14,8},{0,6},{4,10},{8,14},{7,1},{11,5},{15,9},{1,7},... | collective-permute-start | bytes 24584 | tf_op jit(solution)/shard_map/ppermute | solution.py:494
  30.0 1.0 %prepare.1 = (s32[128,128]{1,0:T(8,128)S(1)}, s32[128,128]{1,0:T(8,128)S(1)}, bf16[256,64]{1,0:T(8,128)(2,1)S(1)}, bf16[256,64]{1,0:T(8,128)(2,1)S(1)}, bf16[256...) custom-call(s32[128,128]{1,0:T(8,128)S(1)} %get-tuple-element.47.dest_ref), custom_call_target="tpu_custom_call" | custom-call | flops 62914560 | bytes 524288 | tf_op jit(solution)/shard_map/prepare/pallas_call | solution.py:458
  31.0 3.2 %collective-permute-done.8.rest_4_ = bf16[32,128]{1,0:T(8,128)(2,1)S(1)} collective-permute-done((bf16[32,128]{1,0:T(8,128)(2,1)S(1)}, bf16[32,128]{1,0:T(8,128)(2,1)S(1)}, u32[]{:S(2)}, u32[]{:S(2)}) %collective-permute-start.8) | collective-permute-done | bytes 8224 | tf_op jit(solution)/shard_map/ppermute | solution.py:494
  34.2 0.0 collective-permute-done.5.rest_1_
  34.2 0.0 collective-permute-done.6.rest_2_
  34.2 0.0 collective-permute-done.4.rest_0_
  34.2 0.0 collective-permute-done.7.rest_3_
  34.2 3.2 %finish.1 = (f32[3,64,128]{2,1,0:T(8,128)}, f32[128,128]{1,0:T(8,128)}) custom-call(bf16[192,128]{1,0:T(8,128)(2,1)S(1)} %collective-permute-done.4.rest_0_, bf16[144,128]{1,0:T(8,128)(2,1)S(1)} %collective-permute-done.5.rest_1_, bf16[144,128]{1,0:T(8,128)(2,1)S(1)} %collective-permute-done.6.rest_2_, bf16[192,128]{1,0:T(8,128)(2,1)S(1)} %collective-permute-done.7.rest_3_, ...), custom_call_target="tpu_custom_call" | custom-call | tf_op jit(solution)/shard_map/finish/pallas_call | solution.py:496
Async XLA Ops:
  5.4 8.1 %collective-permute-start = (bf16[256,128]{1,0:T(8,128)(2,1)S(1)}, bf16[256,128]{1,0:T(8,128)(2,1)S(1)}, u32[]{:S(2)}, u32[]{:S(2)}) collective-permute-start(bf16[256,128]{1,0:T(8,128)(2,1)S(1)} %get-tuple-element.30), channel_id=1, source_target_pairs={{0,12},{2,14},{4,0},{6,2},{8,4},{10,6},{12,8},{14,10},{1,13},{3,15... | collective-permute-start | bytes 196616 | tf_op jit(solution)/shard_map/ppermute | solution.py:457
  10.5 4.3 %collective-permute-start.1 = (bf16[256,128]{1,0:T(8,128)(2,1)S(1)}, bf16[256,128]{1,0:T(8,128)(2,1)S(1)}, u32[]{:S(2)}, u32[]{:S(2)}) collective-permute-start(bf16[256,128]{1,0:T(8,128)(2,1)S(1)} %get-tuple-element.31), channel_id=1, source_target_pairs={{0,14},{2,0},{4,2},{6,4},{8,6},{10,8},{12,10},{14,12},{1,15},{3,1}... | collective-permute-start | bytes 196616 | tf_op jit(solution)/shard_map/ppermute | solution.py:457
  11.9 7.3 %collective-permute-start.2 = (bf16[256,128]{1,0:T(8,128)(2,1)S(1)}, bf16[256,128]{1,0:T(8,128)(2,1)S(1)}, u32[]{:S(2)}, u32[]{:S(2)}) collective-permute-start(bf16[256,128]{1,0:T(8,128)(2,1)S(1)} %get-tuple-element.33), channel_id=1, source_target_pairs={{0,2},{2,4},{4,6},{6,8},{8,10},{10,12},{12,14},{14,0},{1,3},{3,5},... | collective-permute-start | bytes 196616 | tf_op jit(solution)/shard_map/ppermute | solution.py:457
  12.6 6.6 %collective-permute-start.3 = (bf16[256,128]{1,0:T(8,128)(2,1)S(1)}, bf16[256,128]{1,0:T(8,128)(2,1)S(1)}, u32[]{:S(2)}, u32[]{:S(2)}) collective-permute-start(bf16[256,128]{1,0:T(8,128)(2,1)S(1)} %get-tuple-element.34), channel_id=1, source_target_pairs={{0,4},{2,6},{4,8},{6,10},{8,12},{10,14},{12,0},{14,2},{1,5},{3,7},... | collective-permute-start | bytes 196616 | tf_op jit(solution)/shard_map/ppermute | solution.py:457
  21.8 12.3 %collective-permute-start.4 = (bf16[192,128]{1,0:T(8,128)(2,1)S(1)}, bf16[192,128]{1,0:T(8,128)(2,1)S(1)}, u32[]{:S(2)}, u32[]{:S(2)}) collective-permute-start(bf16[192,128]{1,0:T(8,128)(2,1)S(1)} %get-tuple-element.41), channel_id=1, source_target_pairs={{0,12},{2,14},{4,0},{6,2},{8,4},{10,6},{12,8},{14,10},{1,13},{3,15... | collective-permute-start | bytes 147464 | tf_op jit(solution)/shard_map/ppermute | solution.py:494
  21.9 12.3 %collective-permute-start.7 = (bf16[192,128]{1,0:T(8,128)(2,1)S(1)}, bf16[192,128]{1,0:T(8,128)(2,1)S(1)}, u32[]{:S(2)}, u32[]{:S(2)}) collective-permute-start(bf16[192,128]{1,0:T(8,128)(2,1)S(1)} %get-tuple-element.44), channel_id=1, source_target_pairs={{0,4},{2,6},{4,8},{6,10},{8,12},{10,14},{12,0},{14,2},{1,5},{3,7},... | collective-permute-start | bytes 147464 | tf_op jit(solution)/shard_map/ppermute | solution.py:494
  23.9 10.3 %collective-permute-start.5 = (bf16[144,128]{1,0:T(8,128)(2,1)S(1)}, bf16[144,128]{1,0:T(8,128)(2,1)S(1)}, u32[]{:S(2)}, u32[]{:S(2)}) collective-permute-start(bf16[144,128]{1,0:T(8,128)(2,1)S(1)} %get-tuple-element.42), channel_id=1, source_target_pairs={{0,14},{2,0},{4,2},{6,4},{8,6},{10,8},{12,10},{14,12},{1,15},{3,1}... | collective-permute-start | bytes 110600 | tf_op jit(solution)/shard_map/ppermute | solution.py:494
  27.4 6.7 %collective-permute-start.6 = (bf16[144,128]{1,0:T(8,128)(2,1)S(1)}, bf16[144,128]{1,0:T(8,128)(2,1)S(1)}, u32[]{:S(2)}, u32[]{:S(2)}) collective-permute-start(bf16[144,128]{1,0:T(8,128)(2,1)S(1)} %get-tuple-element.43), channel_id=1, source_target_pairs={{0,2},{2,4},{4,6},{6,8},{8,10},{10,12},{12,14},{14,0},{1,3},{3,5},... | collective-permute-start | bytes 110600 | tf_op jit(solution)/shard_map/ppermute | solution.py:494
  27.4 6.7 %collective-permute-start.8 = (bf16[32,128]{1,0:T(8,128)(2,1)S(1)}, bf16[32,128]{1,0:T(8,128)(2,1)S(1)}, u32[]{:S(2)}, u32[]{:S(2)}) collective-permute-start(bf16[32,128]{1,0:T(8,128)(2,1)S(1)} %get-tuple-element.45), channel_id=1, source_target_pairs={{6,0},{10,4},{14,8},{0,6},{4,10},{8,14},{7,1},{11,5},{15,9},{1,7},... | collective-permute-start | bytes 24584 | tf_op jit(solution)/shard_map/ppermute | solution.py:494

commit v3 on v2

--- a/solution.py
+++ b/solution.py
@@ -32,13 +32,26 @@
     return lax.dot_general(a, b, (((1,), (1,)), ((), ())), preferred_element_type=F32)
 
 
+def position():
+    return lax.axis_index("tile") * lax.axis_size("sub") + lax.axis_index("sub")
+
+
+def pick(values):
+    usual = max(sorted(set(values)), key=values.count)
+    mine = position()
+    result = jnp.int32(usual)
+    for device, value in enumerate(values):
+        if value != usual:
+            result = jnp.where(mine == device, value, result)
+    return result
+
+
 def ones_where(mask):
     return jnp.where(mask, 1.0, 0.0).astype(BF16)
 
 
-def offsets_of(destination, count_s, total):
-    mine = lax.axis_index("tile") * count_s + lax.axis_index("sub")
-    shifted = destination - mine + MIDDLE
+def offsets_of(destination, total):
+    shifted = destination - position() + MIDDLE
     shifted = jnp.where(shifted < 0, shifted + total, shifted)
     return jnp.where(shifted >= total, shifted - total, shifted)
 
@@ -60,10 +73,10 @@
     return result
 
 
-def route_kernel(count_s, total, x_hbm, dest_hbm, *rest):
-    staged = len(rest) - NEIGHBOR_TILES - 8
+def route_kernel(sent, total, x_hbm, dest_hbm, *rest):
+    staged = len(rest) - len(sent) - 8
     sources, rest = rest[: staged // 2], rest[staged // 2 :]
-    outs, dest_ref, rest = rest[:NEIGHBOR_TILES], rest[NEIGHBOR_TILES], rest[NEIGHBOR_TILES + 1 :]
+    outs, dest_ref, rest = rest[: len(sent)], rest[len(sent)], rest[len(sent) + 1 :]
     targets, rest = rest[: staged // 2], rest[staged // 2 :]
     x_ref, comb, place, pos_scr, vec, scal, sem = rest
     copies = [
@@ -79,7 +92,7 @@
     unit = SORT_UNIT
     groups = outs[0].shape[0] // 4
     stride = (groups + 1) * 8
-    offsets = offsets_of(dest_ref[...], count_s, total)
+    offsets = offsets_of(dest_ref[...], total)
     ones8 = jnp.ones((8, LANES), BF16)
     sub8 = iota((8, blocks), 0)
     earlier = ones_where(iota((blocks, blocks), 0) < iota((blocks, blocks), 1))
@@ -156,23 +169,28 @@
     upper = iota((groups // 2, 8, LANES), 1) < 4
     slot = iota((groups // 2, 8, LANES), 0) * (2 * LANES) + pair_lane[None]
     last = blocks - 1
+
+    def length(o):
+        return (scal[o, last] - o * stride) * (LANES // 8) + scal[24 + o, last] + LANES
+
     for o in range(NEIGHBOR_TILES):
-        row = scal[o, last] - o * stride
-        count = row * (LANES // 8) + scal[24 + o, last] + LANES
-        full = lax.shift_right_logical(count, 7) * 8 + o * stride
+        full = lax.shift_right_logical(length(o), 7) * 8 + o * stride
         place[pl.ds(pl.multiple_of(full, 8), 8), :] = current[o]
-        tiles = place[o * stride : o * stride + groups * 8, :].reshape(groups // 2, 2, 8, LANES)
+    for offset, out in zip(sent, outs):
+        o = pick(offset)
+        tiles = place[pl.ds(pl.multiple_of(o * stride, 8), groups * 8), :]
+        tiles = tiles.reshape(groups // 2, 2, 8, LANES)
         both = jnp.where(upper, tiles[:, 0], tiles[:, 1])
-        both = jnp.where(slot < count, both, 0.0)
-        outs[o][...] = both.reshape(groups * 4, LANES).astype(BF16)
+        both = jnp.where(slot < length(o), both, 0.0)
+        out[...] = both.reshape(groups * 4, LANES).astype(BF16)
     for copy in copies[2:]:
         copy.wait()
 
 
-def prepare_kernel(count_s, total, dest_ref, index_ref, code_ref, *hot_refs):
+def prepare_kernel(total, dest_ref, row_ref, blocks_ref, index_ref, code_ref, *hot_refs):
     blocks = dest_ref.shape[0]
     groups = hot_refs[0].shape[1]
-    offsets = offsets_of(dest_ref[...], count_s, total)
+    offsets = offsets_of(dest_ref[...], total)
     index = jnp.zeros((blocks, LANES), I32)
     code = jnp.zeros((blocks, LANES), I32)
     group_id = iota((blocks, groups), 1)
@@ -186,6 +204,8 @@
         hot_refs[o][blocks:, :] = ones_where(group_id == first[:, :groups] + 1)
     index_ref[...] = index
     code_ref[...] = code
+    row = jnp.concatenate([row_ref[0:1, :], row_ref[1:2, :]], axis=1)
+    blocks_ref[...] = ones_where(iota(blocks_ref.shape, 0) == row)
 
 
 def packed_columns(fields, low):
@@ -199,21 +219,19 @@
     return packed
 
 
-def remap_kernel(messages, *rest):
-    arrived = rest[:NEIGHBOR_TILES]
-    ptr_hbm, row_ref, w_ref, ocean_ref, skin_ref, depth_ref, mask_ref = rest[
-        NEIGHBOR_TILES : NEIGHBOR_TILES + 7
-    ]
-    outs = rest[NEIGHBOR_TILES + 7 :]
-    forcing_ref, own_ref = outs[:2]
-    message_refs = outs[2 : 2 + len(messages)]
-    slots, mapped, shares, ptr_ref, sem = outs[2 + len(messages) :]
+def remap_kernel(came, returns, edges, *rest):
+    arrived, rest = rest[: len(came)], rest[len(came) :]
+    ptr_hbm, hot_ref, w_ref, ocean_ref, skin_ref, depth_ref, mask_ref = rest[:7]
+    forcing_ref, own_ref = rest[7:9]
+    message_refs = rest[9 : 9 + len(returns)]
+    slots, mapped, shares, homebound, bank, ptr_ref, sem = rest[9 + len(returns) :]
     pointers = pltpu.make_async_copy(ptr_hbm, ptr_ref, sem)
     pointers.start()
     per_step = 8
     size = arrived[0].shape[0]
-    for o in range(NEIGHBOR_TILES):
-        slots[o * size : (o + 1) * size, :] = arrived[o][...].astype(F32)
+    for offset, block in zip(came, arrived):
+        o = pick(offset)
+        slots[pl.ds(pl.multiple_of(o * size, size), size), :] = block[...].astype(F32)
     slots[NEIGHBOR_TILES * size :, :] = jnp.zeros((8, LANES), F32)
     pointers.wait()
     sub = iota((per_step, LANES), 0)
@@ -259,57 +277,47 @@
     high = every.astype(BF16)
     low = (every - high.astype(F32)).astype(BF16)
     split = jnp.concatenate([high, low], axis=1)
-    count = shares.shape[0]
     groups = own_ref.shape[0]
-    returned = []
-    row = jnp.concatenate([row_ref[0:1, :], row_ref[1:2, :]], axis=1)
-    for o in range(NEIGHBOR_TILES):
-        hot = ones_where(iota((groups, count), 0) + o * groups == row)
-        value = dot(hot, split)
-        returned.append((value[:, :LANES] + value[:, LANES:]).astype(BF16))
-    own_ref[...] = returned[MIDDLE]
+    value = dot(hot_ref[...], split)
+    returned = (value[:, :LANES] + value[:, LANES:]).astype(BF16)
+    homebound[...] = returned
+    own_ref[...] = returned[MIDDLE * groups : (MIDDLE + 1) * groups]
     fields = [ocean_ref[0], ocean_ref[1], ocean_ref[2], mask_ref[...].astype(F32), depth_ref[...]]
     fields += [forcing_ref[0], forcing_ref[1], forcing_ref[2]]
-    high_columns = packed_columns(fields, False)
-    low_columns = packed_columns(fields, True)
     tall = fields[0].shape[0]
-    for (pairs, parts), out in zip(messages, message_refs):
-        at = 0
-        for kind, length in parts:
-            if kind[0] == "ret":
-                value = returned[kind[1]]
-            else:
-                _, dt, ds = kind
-                span = {1: slice(tall - HALO, tall), 0: slice(0, tall), -1: slice(0, HALO)}[dt]
-                if ds:
-                    value = (high_columns if ds > 0 else low_columns)[span]
-                else:
-                    value = jnp.concatenate([x[span] for x in fields], axis=0)
-                value = value.astype(BF16)
-            out[at : at + length, :] = value
-            at += length
-
-
-def finish_kernel(messages, count_t, count_s, *rest):
-    message_refs = rest[: len(messages)]
-    own_ref, index_ref, code_ref = rest[len(messages) : len(messages) + 3]
-    hot_refs = rest[len(messages) + 3 : len(messages) + 3 + NEIGHBOR_TILES]
-    ocean_ref, depth_ref, mask_ref, forcing_ref, out_ref, warm_ref = rest[
-        len(messages) + 3 + NEIGHBOR_TILES :
-    ]
+    rows = HALO * FIELDS
+    bank[0:rows, :] = jnp.concatenate([x[tall - HALO :] for x in fields], axis=0).astype(BF16)
+    bank[rows : 2 * rows, :] = jnp.concatenate([x[:HALO] for x in fields], axis=0).astype(BF16)
+    bank[2 * rows : 2 * rows + tall, :] = packed_columns(fields, False).astype(BF16)
+    bank[2 * rows + tall : 2 * rows + 2 * tall, :] = packed_columns(fields, True).astype(BF16)
+    bank[2 * rows + 2 * tall :, :] = jnp.zeros((rows, LANES), BF16)
+    for offset, edge, out in zip(returns, edges, message_refs):
+        first = pl.multiple_of(pick(offset) * groups, 16)
+        out[0:groups, :] = homebound[pl.ds(first, groups), :]
+        first = pl.multiple_of(pick(edge), 16)
+        out[groups:, :] = bank[pl.ds(first, rows), :]
+
+
+def finish_kernel(sources, halos, count_t, count_s, messages, *rest):
+    message_refs, rest = rest[:messages], rest[messages:]
+    own_ref, index_ref, code_ref = rest[:3]
+    hot_refs, rest = rest[3 : 3 + NEIGHBOR_TILES], rest[3 + NEIGHBOR_TILES :]
+    ocean_ref, depth_ref, mask_ref, forcing_ref, out_ref, warm_ref, inbox = rest
     t, s = lax.axis_index("tile"), lax.axis_index("sub")
-    found = {("ret", MIDDLE): own_ref[...]}
-    for (pairs, parts), ref in zip(messages, message_refs):
-        at = 0
-        for kind, length in parts:
-            found[kind] = ref[at : at + length, :]
-            at += length
+    size = message_refs[0].shape[0]
+    groups = own_ref.shape[0]
+    for i, ref in enumerate(message_refs):
+        inbox[i * size : (i + 1) * size, :] = ref[...]
     blocks = index_ref.shape[0]
     index = index_ref[...]
     code = code_ref[...]
     warm = jnp.zeros((blocks, LANES), F32)
     for o in range(NEIGHBOR_TILES):
-        lines = dot(hot_refs[o][...], found[("ret", o)])
+        if o == MIDDLE:
+            value = own_ref[...]
+        else:
+            value = inbox[pl.ds(pl.multiple_of(pick(sources[o]) * size, 16), groups), :]
+        lines = dot(hot_refs[o][...], value)
         for half in range(2):
             picked = jnp.take_along_axis(lines[half * blocks : (half + 1) * blocks], index, axis=1)
             warm = jnp.where(code == 2 * o + half, picked, warm)
@@ -328,7 +336,9 @@
             ok &= s > 0
         if ds == -1:
             ok &= s < count_s - 1
-        value = found[("halo", dt, ds)].astype(F32)
+        rows = tall if dt == 0 else (HALO if ds else HALO * FIELDS)
+        first = pl.multiple_of(pick(halos[dt, ds]) * size + groups, 16)
+        value = inbox[pl.ds(first, rows), :].astype(F32)
         return jnp.where(ok, value, 0.0)
 
     from_left = jnp.concatenate([halo(1, 1), halo(0, 1), halo(-1, 1)], axis=0)
@@ -366,39 +376,89 @@
         out_ref[i] = a[HALO : HALO + tall, :LANES]
 
 
-def plan_messages(count_t, count_s, groups, tall):
+SCHEDULES = {
+    (4, 2): (
+        [
+            [1, 3, 4, 2, 6, 7, 0, 5],
+            [7, 2, 1, 5, 3, 6, 4, 0],
+            [6, 7, 0, 4, 2, 3, 5, 1],
+            [2, 0, 3, 1, 5, 4, 7, 6],
+        ],
+        [
+            [3, 7, 1, 4, 2, 6, 0, 5],
+            [7, 2, 4, 5, 6, 3, -1, 0],
+            [6, 3, 5, 0, 7, 2, 4, 1],
+            [2, -1, 0, 1, 3, 7, 5, 4],
+            [1, 0, 3, 2, 5, 4, 7, 6],
+        ],
+    ),
+}
+
+
+def schedule(count_t, count_s):
     total = count_t * count_s
-    by_distance = {}
-    for o in range(NEIGHBOR_TILES):
-        if o != MIDDLE:
-            by_distance.setdefault(MIDDLE - o, []).append((("ret", o), groups))
-    for dt in (-1, 0, 1):
+    if (count_t, count_s) in SCHEDULES:
+        return SCHEDULES[count_t, count_s]
+    rings = [
+        [(i + distance) % total for i in range(total)]
+        for distance in range(-MIDDLE, MIDDLE + 1)
+        if distance
+    ]
+    others = []
+    for dt in (-1, 1):
         for ds in (-1, 0, 1):
-            if dt or ds:
-                length = tall if dt == 0 else (HALO if ds else HALO * FIELDS)
-                by_distance.setdefault(dt * count_s + ds, []).append((("halo", dt, ds), length))
-    messages, partial = [], []
-    for distance, parts in sorted(by_distance.items()):
-        if any(kind[0] == "ret" for kind, _ in parts):
-            pairs = [(i, (i + distance) % total) for i in range(total)]
-            messages.append((pairs, parts))
-            continue
-        pairs = []
-        for (_, dt, ds), _ in parts:
-            for t in range(count_t):
-                for s in range(count_s):
-                    if 0 <= t + dt < count_t and 0 <= s + ds < count_s:
-                        pairs.append((t * count_s + s, (t + dt) * count_s + s + ds))
-        for other in partial:
-            if not {a for a, _ in pairs} & {a for a, _ in other[0]} and not (
-                {b for _, b in pairs} & {b for _, b in other[0]}
-            ):
-                other[0].extend(pairs)
-                other[1].extend(parts)
-                break
-        else:
-            partial.append((pairs, list(parts)))
-    return messages + partial
+            if MIDDLE < abs(dt * count_s + ds):
+                targets = [-1] * total
+                for device in range(total):
+                    t, s = device // count_s + dt, device % count_s + ds
+                    if 0 <= t < count_t and 0 <= s < count_s:
+                        targets[device] = t * count_s + s
+                others.append(targets)
+    return rings, rings + others
+
+
+def plan(count_t, count_s, groups, tall):
+    total = count_t * count_s
+    outward, homeward = schedule(count_t, count_s)
+
+    def offset(a, b):
+        o = (b - a + MIDDLE) % total
+        return o if o < NEIGHBOR_TILES else -1
+
+    def step(a, b):
+        dt, ds = b // count_s - a // count_s, b % count_s - a % count_s
+        return (dt, ds) if abs(dt) <= 1 and abs(ds) <= 1 else None
+
+    def senders(targets):
+        return [targets.index(d) if d in targets else -1 for d in range(total)]
+
+    rows = HALO * FIELDS
+    start = {(1, 0): 0, (-1, 0): rows}
+    for ds, first in ((1, 2 * rows), (-1, 2 * rows + tall)):
+        start[0, ds] = start[-1, ds] = first
+        start[1, ds] = first + tall - HALO
+    result = {"outward": outward, "homeward": homeward}
+    result["sent"] = [[offset(a, b) for a, b in enumerate(p)] for p in outward]
+    result["sent"].insert(0, [MIDDLE] * total)
+    result["came"] = [[offset(a, b) for b, a in enumerate(senders(p))] for p in outward]
+    result["came"].insert(0, [MIDDLE] * total)
+    result["returns"] = [
+        [max(offset(b, a), 0) if b >= 0 else 0 for a, b in enumerate(p)] for p in homeward
+    ]
+    result["edges"] = [
+        [start[step(a, b)] if b >= 0 and step(a, b) else 0 for a, b in enumerate(p)] for p in homeward
+    ]
+    sources = [[0] * total for _ in range(NEIGHBOR_TILES)]
+    halos = {(dt, ds): [0] * total for dt in (-1, 0, 1) for ds in (-1, 0, 1)}
+    for i, p in enumerate(homeward):
+        for a, b in enumerate(p):
+            if b >= 0:
+                if offset(b, a) >= 0:
+                    sources[offset(b, a)][b] = i
+                if step(a, b):
+                    halos[step(a, b)][b] = i
+    result["sources"], result["halos"] = sources, halos
+    return result
 
 
 def shards(
@@ -430,12 +490,15 @@
         gravity_bathymetry[0],
         marine_indicator[0],
     )
+    tall = skin_warmth_anomaly.shape[1]
+    moves = plan(count_t, count_s, groups, tall)
+    sends = len(moves["sent"])
     results = pl.pallas_call(
-        functools.partial(route_kernel, count_s, total),
-        out_shape=[jax.ShapeDtypeStruct((groups * 4, LANES), BF16)] * NEIGHBOR_TILES
+        functools.partial(route_kernel, moves["sent"], total),
+        out_shape=[jax.ShapeDtypeStruct((groups * 4, LANES), BF16)] * sends
         + [jax.ShapeDtypeStruct(a.shape, a.dtype) for a in (destination,) + to_stage],
         in_specs=[hbm] * (2 + len(to_stage)),
-        out_specs=[vmem] * (NEIGHBOR_TILES + 1 + len(to_stage)),
+        out_specs=[vmem] * (sends + 1 + len(to_stage)),
         scratch_shapes=[
             pltpu.VMEM((8, columns), BF16),
             pltpu.VMEM((8, columns), BF16),
@@ -448,62 +511,63 @@
         compiler_params=params,
         name="route",
     )(*(pltpu.with_memory_space_constraint(a, pltpu.HBM) for a in (air_exchanges[0], destination) + to_stage))
-    outbound = results[:NEIGHBOR_TILES]
-    destination, rows, weights, ocean, skin, depth, mask = results[NEIGHBOR_TILES:]
-    arrived = list(outbound)
-    for o in range(NEIGHBOR_TILES):
-        if o != MIDDLE:
-            pairs = [(i, (i + o - MIDDLE) % total) for i in range(total)]
-            arrived[o] = lax.ppermute(outbound[o], axes, pairs)
+    destination, rows, weights, ocean, skin, depth, mask = results[sends:]
+
+    def send(array, targets):
+        return lax.ppermute(array, axes, [(a, b) for a, b in enumerate(targets) if b >= 0])
+
+    arrived = [results[0]] + [send(a, p) for a, p in zip(results[1:], moves["outward"])]
     prepared = pl.pallas_call(
-        functools.partial(prepare_kernel, count_s, total),
-        out_shape=[jax.ShapeDtypeStruct((blocks, LANES), I32)] * 2
+        functools.partial(prepare_kernel, total),
+        out_shape=[jax.ShapeDtypeStruct((NEIGHBOR_TILES * groups, LANES), BF16)]
+        + [jax.ShapeDtypeStruct((blocks, LANES), I32)] * 2
         + [jax.ShapeDtypeStruct((2 * blocks, groups), BF16)] * NEIGHBOR_TILES,
-        in_specs=[vmem],
-        out_specs=[vmem] * (2 + NEIGHBOR_TILES),
+        in_specs=[vmem] * 2,
+        out_specs=[vmem] * (3 + NEIGHBOR_TILES),
         compiler_params=params,
         cost_estimate=pl.CostEstimate(flops=2 * 15 * LANES**3, bytes_accessed=2**19, transcendentals=0),
         name="prepare",
-    )(destination)
-
-    tall = skin.shape[0]
-    messages = plan_messages(count_t, count_s, groups, tall)
-    lengths = [sum(n for _, n in parts) for _, parts in messages]
+    )(destination, rows)
+    returns = len(moves["returns"])
+    message = (groups + HALO * FIELDS, LANES)
     row_blocks = weights.shape[0]
     outs = pl.pallas_call(
-        functools.partial(remap_kernel, messages),
+        functools.partial(remap_kernel, moves["came"], moves["returns"], moves["edges"]),
         out_shape=[
             jax.ShapeDtypeStruct((3, tall, LANES), F32),
             jax.ShapeDtypeStruct((groups, LANES), BF16),
         ]
-        + [jax.ShapeDtypeStruct((n, LANES), BF16) for n in lengths],
-        in_specs=[vmem] * NEIGHBOR_TILES + [hbm] + [vmem] * 6,
-        out_specs=[vmem] * (2 + len(lengths)),
+        + [jax.ShapeDtypeStruct(message, BF16)] * returns,
+        in_specs=[vmem] * sends + [hbm] + [vmem] * 6,
+        out_specs=[vmem] * (2 + returns),
         scratch_shapes=[
             pltpu.VMEM((NEIGHBOR_TILES * groups * 4 + 8, LANES), F32),
             pltpu.VMEM((row_blocks * 8, LANES), F32),
             pltpu.VMEM((2 * row_blocks, LANES), F32),
+            pltpu.VMEM((NEIGHBOR_TILES * groups, LANES), BF16),
+            pltpu.VMEM((3 * HALO * FIELDS + 2 * tall, LANES), BF16),
             pltpu.SMEM(pointers.shape, I32),
             pltpu.SemaphoreType.DMA,
         ],
         compiler_params=params,
         name="remap",
-    )(*arrived, pltpu.with_memory_space_constraint(pointers, pltpu.HBM), rows, weights, ocean, skin, depth, mask)
+    )(*arrived, pltpu.with_memory_space_constraint(pointers, pltpu.HBM), prepared[0], weights, ocean, skin, depth, mask)
     forcing, own = outs[:2]
-    received = [
-        lax.ppermute(message, axes, pairs) for message, (pairs, _) in zip(outs[2:], messages)
-    ]
+    received = [send(a, p) for a, p in zip(outs[2:], moves["homeward"])]
     ocean_out, warm = pl.pallas_call(
-        functools.partial(finish_kernel, messages, count_t, count_s),
+        functools.partial(
+            finish_kernel, moves["sources"], moves["halos"], count_t, count_s, returns
+        ),
         out_shape=[
             jax.ShapeDtypeStruct((3, tall, LANES), F32),
             jax.ShapeDtypeStruct((blocks, LANES), F32),
         ],
-        in_specs=[vmem] * (len(messages) + 3 + NEIGHBOR_TILES + 4),
+        in_specs=[vmem] * (returns + 3 + NEIGHBOR_TILES + 4),
         out_specs=[vmem] * 2,
+        scratch_shapes=[pltpu.VMEM((returns * message[0], LANES), BF16)],
         compiler_params=params,
         name="finish",
-    )(*received, own, *prepared, ocean, depth, mask, forcing)
+    )(*received, own, *prepared[1:], ocean, depth, mask, forcing)
     return ocean_out[None], warm.reshape(1, columns)
 
 

time: 37.6 us -> 35.6 us (0.947)
  waiting for transfers between devices: 8.85 us -> 6.03 us
  starting transfers between devices: 16.2 us -> 17 us
    ppermute x9, waiting for transfers between devices: 8.85 us -> 6.03 us  [send(): lax.ppermute(array, axes, [(a, b) for a, b in enumerate(targets) if b >= 0])]
    ppermute x9, starting transfers between devices: 16.2 us -> 17 us  [send(): lax.ppermute(array, axes, [(a, b) for a, b in enumerate(targets) if b >= 0])]
  transfers between devices with their start and end apart: 9 -> 9, of which waited for: 3 -> 6; matrix products, arithmetic and copies ran while one was open for 0% -> 0% of each run, Pallas kernels for 3% -> 3%
where the time goes in v3:
time: 35.6 us; the launch traced here: 35.4 us
  starting transfers between devices  17 us (48%)
  Pallas kernels  11.7 us (33%)
  waiting for transfers between devices  6.03 us (17%)
  between operations  0.7 us (2%)
    ppermute x9, starting transfers between devices, send(): lax.ppermute(array, axes, [(a, b) for a, b in enumerate(targets) if b >= 0])  17 us
    ppermute x9, waiting for transfers between devices, send(): lax.ppermute(array, axes, [(a, b) for a, b in enumerate(targets) if b >= 0])  6.03 us
    pallas_call x1, Pallas kernels, shards(): pl.pallas_call(functools.partial(route_kernel, moves['sent'], total), out...  4.84 us
    pallas_call x1, Pallas kernels, shards(): pl.pallas_call(functools.partial(finish_kernel, moves['sources'], moves['...  3.19 us
    pallas_call x1, Pallas kernels, shards(): pl.pallas_call(functools.partial(remap_kernel, moves['came'], moves['retu...  2.67 us
    pallas_call x1, Pallas kernels, shards(): pl.pallas_call(functools.partial(prepare_kernel, total), out_shape=[jax.S...  1 us
  transfers between devices with their start and end apart: 9, of which 6 were waited for; matrix products, arithmetic and copies ran while one was open for 0% of the time, Pallas kernels for 3%

profile of v3, /device:TPU:0, one launch (start us, length us, event | category | flops | bytes accessed | tf_op | source)
XLA Modules:
  0.0 35.4 jit_solution(7155309988739851067)
XLA Ops:
  0.6 4.8 %route.1 = (bf16[256,128]{1,0:T(8,128)(2,1)S(1)}, bf16[256,128]{1,0:T(8,128)(2,1)S(1)}, bf16[256,128]{1,0:T(8,128)(2,1)S(1)}, bf16[256,128]{1,0:T(8,128)(2,1)S(1...) custom-call(bf16[8,16384]{1,0:T(8,128)(2,1)} %bitcast.13, ...), custom_call_target="tpu_custom_call" | custom-call | tf_op jit(solution)/shard_map/route/pallas_call | solution.py:496
  5.5 3.0 %collective-permute-start = (bf16[256,128]{1,0:T(8,128)(2,1)S(1)}, bf16[256,128]{1,0:T(8,128)(2,1)S(1)}, u32[]{:S(2)}, u32[]{:S(2)}) collective-permute-start(bf16[256,128]{1,0:T(8,128)(2,1)S(1)} %get-tuple-element.32), channel_id=1, source_target_pairs={{0,2},{2,6},{4,8},{6,4},{8,12},{10,14},{12,0},{14,10},{1,3},{3,7},... | collective-permute-start | bytes 196616 | tf_op jit(solution)/shard_map/ppermute | solution.py:517
  8.5 3.5 %collective-permute-start.1 = (bf16[256,128]{1,0:T(8,128)(2,1)S(1)}, bf16[256,128]{1,0:T(8,128)(2,1)S(1)}, u32[]{:S(2)}, u32[]{:S(2)}) collective-permute-start(bf16[256,128]{1,0:T(8,128)(2,1)S(1)} %get-tuple-element.33), channel_id=1, source_target_pairs={{0,14},{2,4},{4,2},{6,10},{8,6},{10,12},{12,8},{14,0},{1,15},{3,5}... | collective-permute-start | bytes 196616 | tf_op jit(solution)/shard_map/ppermute | solution.py:517
  12.0 0.6 %collective-permute-start.2 = (bf16[256,128]{1,0:T(8,128)(2,1)S(1)}, bf16[256,128]{1,0:T(8,128)(2,1)S(1)}, u32[]{:S(2)}, u32[]{:S(2)}) collective-permute-start(bf16[256,128]{1,0:T(8,128)(2,1)S(1)} %get-tuple-element.34), channel_id=1, source_target_pairs={{0,12},{2,14},{4,0},{6,8},{8,4},{10,6},{12,10},{14,2},{1,13},{3,15... | collective-permute-start | bytes 196616 | tf_op jit(solution)/shard_map/ppermute | solution.py:517
  12.6 1.4 %collective-permute-start.3 = (bf16[256,128]{1,0:T(8,128)(2,1)S(1)}, bf16[256,128]{1,0:T(8,128)(2,1)S(1)}, u32[]{:S(2)}, u32[]{:S(2)}) collective-permute-start(bf16[256,128]{1,0:T(8,128)(2,1)S(1)} %get-tuple-element.35), channel_id=1, source_target_pairs={{0,4},{2,0},{4,6},{6,2},{8,10},{10,8},{12,14},{14,12},{1,5},{3,1},... | collective-permute-start | bytes 196616 | tf_op jit(solution)/shard_map/ppermute | solution.py:517
  14.0 1.0 %prepare.1 = (bf16[320,128]{1,0:T(8,128)(2,1)S(1)}, s32[128,128]{1,0:T(8,128)S(1)}, s32[128,128]{1,0:T(8,128)S(1)}, bf16[256,64]{1,0:T(8,128)(2,1)S(1)}, bf16[25...) custom-call(s32[128,128]{1,0:T(8,128)S(1)} %get-tuple-element.36.des, ...), custom_call_target="tpu_custom_call" | custom-call | flops 62914560 | bytes 524288 | tf_op jit(solution)/shard_map/prepare/pallas_call | solution.py:520
  15.0 0.0 collective-permute-done.rest_1_
  15.0 1.3 %collective-permute-done.1.rest_2_ = bf16[256,128]{1,0:T(8,128)(2,1)S(1)} collective-permute-done((bf16[256,128]{1,0:T(8,128)(2,1)S(1)}, bf16[256,128]{1,0:T(8,128)(2,1)S(1)}, u32[]{:S(2)}, u32[]{:S(2)}) %collective-permute-start.1) | collective-permute-done | bytes 65568 | tf_op jit(solution)/shard_map/ppermute | solution.py:517
  16.3 0.0 collective-permute-done.2.rest_3_
  16.3 0.6 %collective-permute-done.3.rest_4_ = bf16[256,128]{1,0:T(8,128)(2,1)S(1)} collective-permute-done((bf16[256,128]{1,0:T(8,128)(2,1)S(1)}, bf16[256,128]{1,0:T(8,128)(2,1)S(1)}, u32[]{:S(2)}, u32[]{:S(2)}) %collective-permute-start.3) | collective-permute-done | bytes 65568 | tf_op jit(solution)/shard_map/ppermute | solution.py:517
  17.0 2.7 %remap.1 = (f32[3,64,128]{2,1,0:T(8,128)S(1)}, bf16[64,128]{1,0:T(8,128)(2,1)S(1)}, bf16[192,128]{1,0:T(8,128)(2,1)S(1)}, bf16[192,128]{1,0:T(8,128)(2,1)S(1)}, ...) custom-call(bf16[256,128]{1,0:T(8,128)(2,1)S(1)} %get-tuple-element.31.rest_0_, ...), custom_call_target="tpu_custom_call" | custom-call | tf_op jit(solution)/shard_map/remap/pallas_call | solution.py:534
  19.6 1.4 %collective-permute-start.4 = (bf16[192,128]{1,0:T(8,128)(2,1)S(1)}, bf16[192,128]{1,0:T(8,128)(2,1)S(1)}, u32[]{:S(2)}, u32[]{:S(2)}) collective-permute-start(bf16[192,128]{1,0:T(8,128)(2,1)S(1)} %get-tuple-element.44), channel_id=1, source_target_pairs={{0,6},{2,14},{4,2},{6,8},{8,4},{10,12},{12,0},{14,10},{1,7},{3,15}... | collective-permute-start | bytes 147464 | tf_op jit(solution)/shard_map/ppermute | solution.py:517
  21.0 3.4 %collective-permute-start.5 = (bf16[192,128]{1,0:T(8,128)(2,1)S(1)}, bf16[192,128]{1,0:T(8,128)(2,1)S(1)}, u32[]{:S(2)}, u32[]{:S(2)}) collective-permute-start(bf16[192,128]{1,0:T(8,128)(2,1)S(1)} %get-tuple-element.45), channel_id=1, source_target_pairs={{0,14},{2,4},{4,8},{6,10},{8,12},{10,6},{14,0},{1,15},{3,5},{5,9},... | collective-permute-start | bytes 147464 | tf_op jit(solution)/shard_map/ppermute | solution.py:517
  24.5 0.4 %collective-permute-start.6 = (bf16[192,128]{1,0:T(8,128)(2,1)S(1)}, bf16[192,128]{1,0:T(8,128)(2,1)S(1)}, u32[]{:S(2)}, u32[]{:S(2)}) collective-permute-start(bf16[192,128]{1,0:T(8,128)(2,1)S(1)} %get-tuple-element.46), channel_id=1, source_target_pairs={{0,12},{2,6},{4,10},{6,0},{8,14},{10,4},{12,8},{14,2},{1,13},{3,7}... | collective-permute-start | bytes 147464 | tf_op jit(solution)/shard_map/ppermute | solution.py:517
  24.8 3.2 %collective-permute-start.7 = (bf16[192,128]{1,0:T(8,128)(2,1)S(1)}, bf16[192,128]{1,0:T(8,128)(2,1)S(1)}, u32[]{:S(2)}, u32[]{:S(2)}) collective-permute-start(bf16[192,128]{1,0:T(8,128)(2,1)S(1)} %get-tuple-element.47), channel_id=1, source_target_pairs={{0,4},{4,0},{6,2},{8,6},{10,14},{12,10},{14,8},{1,5},{5,1},{7,3},{... | collective-permute-start | bytes 147464 | tf_op jit(solution)/shard_map/ppermute | solution.py:517
  28.1 0.1 collective-permute-start.8
  28.1 0.0 collective-permute-done.4.rest_0_
  28.1 1.9 %collective-permute-done.5.rest_1_ = bf16[192,128]{1,0:T(8,128)(2,1)S(1)} collective-permute-done((bf16[192,128]{1,0:T(8,128)(2,1)S(1)}, bf16[192,128]{1,0:T(8,128)(2,1)S(1)}, u32[]{:S(2)}, u32[]{:S(2)}) %collective-permute-start.5) | collective-permute-done | bytes 49184 | tf_op jit(solution)/shard_map/ppermute | solution.py:517
  30.0 0.7 %collective-permute-done.6.rest_2_ = bf16[192,128]{1,0:T(8,128)(2,1)S(1)} collective-permute-done((bf16[192,128]{1,0:T(8,128)(2,1)S(1)}, bf16[192,128]{1,0:T(8,128)(2,1)S(1)}, u32[]{:S(2)}, u32[]{:S(2)}) %collective-permute-start.6) | collective-permute-done | bytes 49184 | tf_op jit(solution)/shard_map/ppermute | solution.py:517
  30.8 0.1 collective-permute-done.7.rest_3_
  30.8 1.4 %collective-permute-done.8.rest_4_ = bf16[192,128]{1,0:T(8,128)(2,1)S(1)} collective-permute-done((bf16[192,128]{1,0:T(8,128)(2,1)S(1)}, bf16[192,128]{1,0:T(8,128)(2,1)S(1)}, u32[]{:S(2)}, u32[]{:S(2)}) %collective-permute-start.8) | collective-permute-done | bytes 49184 | tf_op jit(solution)/shard_map/ppermute | solution.py:517
  32.2 3.2 %finish.1 = (f32[3,64,128]{2,1,0:T(8,128)}, f32[128,128]{1,0:T(8,128)}) custom-call(bf16[192,128]{1,0:T(8,128)(2,1)S(1)} %collective-permute-done.4.rest_0_, bf16[192,128]{1,0:T(8,128)(2,1)S(1)} %collective-permute-done.5.rest_1_, bf16[192,128]{1,0:T(8,128)(2,1)S(1)} %collective-permute-done.6.rest_2_, bf16[192,128]{1,0:T(8,128)(2,1)S(1)} %collective-permute-done.7.rest_3_, ...), custom_call_target="tpu_custom_call" | custom-call | tf_op jit(solution)/shard_map/finish/pallas_call | solution.py:557
Async XLA Ops:
  5.5 9.5 %collective-permute-start = (bf16[256,128]{1,0:T(8,128)(2,1)S(1)}, bf16[256,128]{1,0:T(8,128)(2,1)S(1)}, u32[]{:S(2)}, u32[]{:S(2)}) collective-permute-start(bf16[256,128]{1,0:T(8,128)(2,1)S(1)} %get-tuple-element.32), channel_id=1, source_target_pairs={{0,2},{2,6},{4,8},{6,4},{8,12},{10,14},{12,0},{14,10},{1,3},{3,7},... | collective-permute-start | bytes 196616 | tf_op jit(solution)/shard_map/ppermute | solution.py:517
  8.5 7.9 %collective-permute-start.1 = (bf16[256,128]{1,0:T(8,128)(2,1)S(1)}, bf16[256,128]{1,0:T(8,128)(2,1)S(1)}, u32[]{:S(2)}, u32[]{:S(2)}) collective-permute-start(bf16[256,128]{1,0:T(8,128)(2,1)S(1)} %get-tuple-element.33), channel_id=1, source_target_pairs={{0,14},{2,4},{4,2},{6,10},{8,6},{10,12},{12,8},{14,0},{1,15},{3,5}... | collective-permute-start | bytes 196616 | tf_op jit(solution)/shard_map/ppermute | solution.py:517
  12.0 4.4 %collective-permute-start.2 = (bf16[256,128]{1,0:T(8,128)(2,1)S(1)}, bf16[256,128]{1,0:T(8,128)(2,1)S(1)}, u32[]{:S(2)}, u32[]{:S(2)}) collective-permute-start(bf16[256,128]{1,0:T(8,128)(2,1)S(1)} %get-tuple-element.34), channel_id=1, source_target_pairs={{0,12},{2,14},{4,0},{6,8},{8,4},{10,6},{12,10},{14,2},{1,13},{3,15... | collective-permute-start | bytes 196616 | tf_op jit(solution)/shard_map/ppermute | solution.py:517
  12.6 4.4 %collective-permute-start.3 = (bf16[256,128]{1,0:T(8,128)(2,1)S(1)}, bf16[256,128]{1,0:T(8,128)(2,1)S(1)}, u32[]{:S(2)}, u32[]{:S(2)}) collective-permute-start(bf16[256,128]{1,0:T(8,128)(2,1)S(1)} %get-tuple-element.35), channel_id=1, source_target_pairs={{0,4},{2,0},{4,6},{6,2},{8,10},{10,8},{12,14},{14,12},{1,5},{3,1},... | collective-permute-start | bytes 196616 | tf_op jit(solution)/shard_map/ppermute | solution.py:517
  19.6 8.5 %collective-permute-start.4 = (bf16[192,128]{1,0:T(8,128)(2,1)S(1)}, bf16[192,128]{1,0:T(8,128)(2,1)S(1)}, u32[]{:S(2)}, u32[]{:S(2)}) collective-permute-start(bf16[192,128]{1,0:T(8,128)(2,1)S(1)} %get-tuple-element.44), channel_id=1, source_target_pairs={{0,6},{2,14},{4,2},{6,8},{8,4},{10,12},{12,0},{14,10},{1,7},{3,15}... | collective-permute-start | bytes 147464 | tf_op jit(solution)/shard_map/ppermute | solution.py:517
  21.0 9.0 %collective-permute-start.5 = (bf16[192,128]{1,0:T(8,128)(2,1)S(1)}, bf16[192,128]{1,0:T(8,128)(2,1)S(1)}, u32[]{:S(2)}, u32[]{:S(2)}) collective-permute-start(bf16[192,128]{1,0:T(8,128)(2,1)S(1)} %get-tuple-element.45), channel_id=1, source_target_pairs={{0,14},{2,4},{4,8},{6,10},{8,12},{10,6},{14,0},{1,15},{3,5},{5,9},... | collective-permute-start | bytes 147464 | tf_op jit(solution)/shard_map/ppermute | solution.py:517
  24.5 6.3 %collective-permute-start.6 = (bf16[192,128]{1,0:T(8,128)(2,1)S(1)}, bf16[192,128]{1,0:T(8,128)(2,1)S(1)}, u32[]{:S(2)}, u32[]{:S(2)}) collective-permute-start(bf16[192,128]{1,0:T(8,128)(2,1)S(1)} %get-tuple-element.46), channel_id=1, source_target_pairs={{0,12},{2,6},{4,10},{6,0},{8,14},{10,4},{12,8},{14,2},{1,13},{3,7}... | collective-permute-start | bytes 147464 | tf_op jit(solution)/shard_map/ppermute | solution.py:517
  24.8 6.0 %collective-permute-start.7 = (bf16[192,128]{1,0:T(8,128)(2,1)S(1)}, bf16[192,128]{1,0:T(8,128)(2,1)S(1)}, u32[]{:S(2)}, u32[]{:S(2)}) collective-permute-start(bf16[192,128]{1,0:T(8,128)(2,1)S(1)} %get-tuple-element.47), channel_id=1, source_target_pairs={{0,4},{4,0},{6,2},{8,6},{10,14},{12,10},{14,8},{1,5},{5,1},{7,3},{... | collective-permute-start | bytes 147464 | tf_op jit(solution)/shard_map/ppermute | solution.py:517
  28.1 4.2 %collective-permute-start.8 = (bf16[192,128]{1,0:T(8,128)(2,1)S(1)}, bf16[192,128]{1,0:T(8,128)(2,1)S(1)}, u32[]{:S(2)}, u32[]{:S(2)}) collective-permute-start(bf16[192,128]{1,0:T(8,128)(2,1)S(1)} %get-tuple-element.48), channel_id=1, source_target_pairs={{0,2},{2,0},{4,6},{6,4},{8,10},{10,8},{12,14},{14,12},{1,3},{3,1},... | collective-permute-start | bytes 147464 | tf_op jit(solution)/shard_map/ppermute | solution.py:517

commit v4 on v3

--- a/solution.py
+++ b/solution.py
@@ -385,10 +385,10 @@
             [2, 0, 3, 1, 5, 4, 7, 6],
         ],
         [
-            [3, 7, 1, 4, 2, 6, 0, 5],
-            [7, 2, 4, 5, 6, 3, -1, 0],
-            [6, 3, 5, 0, 7, 2, 4, 1],
-            [2, -1, 0, 1, 3, 7, 5, 4],
+            [3, 6, 5, 0, 7, 2, 1, 4],
+            [2, 3, 1, 4, 6, 7, 0, 5],
+            [7, 2, 4, 1, 3, 6, 5, 0],
+            [6, 7, 0, 5, 2, 3, 4, 1],
             [1, 0, 3, 2, 5, 4, 7, 6],
         ],
     ),

time: 35.6 us -> 32.9 us (0.924)
  waiting for transfers between devices: 6.03 us -> 4.34 us
  starting transfers between devices: 17 us -> 15.8 us
    ppermute x9, waiting for transfers between devices: 6.03 us -> 4.34 us  [send(): lax.ppermute(array, axes, [(a, b) for a, b in enumerate(targets) if b >= 0])]
    ppermute x9, starting transfers between devices: 17 us -> 15.8 us  [send(): lax.ppermute(array, axes, [(a, b) for a, b in enumerate(targets) if b >= 0])]
where the time goes in v4:
time: 32.9 us; the launch traced here: 32.5 us
  starting transfers between devices  15.8 us (48%)
  Pallas kernels  11.7 us (36%)
  waiting for transfers between devices  4.34 us (13%)
  between operations  0.67 us (2%)
    ppermute x9, starting transfers between devices, send(): lax.ppermute(array, axes, [(a, b) for a, b in enumerate(targets) if b >= 0])  15.8 us
    pallas_call x1, Pallas kernels, shards(): pl.pallas_call(functools.partial(route_kernel, moves['sent'], total), out...  4.84 us
    ppermute x9, waiting for transfers between devices, send(): lax.ppermute(array, axes, [(a, b) for a, b in enumerate(targets) if b >= 0])  4.34 us
    pallas_call x1, Pallas kernels, shards(): pl.pallas_call(functools.partial(finish_kernel, moves['sources'], moves['...  3.19 us
    pallas_call x1, Pallas kernels, shards(): pl.pallas_call(functools.partial(remap_kernel, moves['came'], moves['retu...  2.68 us
    pallas_call x1, Pallas kernels, shards(): pl.pallas_call(functools.partial(prepare_kernel, total), out_shape=[jax.S...  1 us
  transfers between devices with their start and end apart: 9, of which 6 were waited for; matrix products, arithmetic and copies ran while one was open for 0% of the time, Pallas kernels for 3%

profile of v4, /device:TPU:0, one launch (start us, length us, event | category | flops | bytes accessed | tf_op | source)
XLA Modules:
  0.0 32.5 jit_solution(8802988789131028481)
XLA Ops:
  0.6 4.8 %route.1 = (bf16[256,128]{1,0:T(8,128)(2,1)S(1)}, bf16[256,128]{1,0:T(8,128)(2,1)S(1)}, bf16[256,128]{1,0:T(8,128)(2,1)S(1)}, bf16[256,128]{1,0:T(8,128)(2,1)S(1...) custom-call(bf16[8,16384]{1,0:T(8,128)(2,1)} %bitcast.13, ...), custom_call_target="tpu_custom_call" | custom-call | tf_op jit(solution)/shard_map/route/pallas_call | solution.py:496
  5.5 3.0 %collective-permute-start = (bf16[256,128]{1,0:T(8,128)(2,1)S(1)}, bf16[256,128]{1,0:T(8,128)(2,1)S(1)}, u32[]{:S(2)}, u32[]{:S(2)}) collective-permute-start(bf16[256,128]{1,0:T(8,128)(2,1)S(1)} %get-tuple-element.32), channel_id=1, source_target_pairs={{0,2},{2,6},{4,8},{6,4},{8,12},{10,14},{12,0},{14,10},{1,3},{3,7},... | collective-permute-start | bytes 196616 | tf_op jit(solution)/shard_map/ppermute | solution.py:517
  8.5 3.5 %collective-permute-start.1 = (bf16[256,128]{1,0:T(8,128)(2,1)S(1)}, bf16[256,128]{1,0:T(8,128)(2,1)S(1)}, u32[]{:S(2)}, u32[]{:S(2)}) collective-permute-start(bf16[256,128]{1,0:T(8,128)(2,1)S(1)} %get-tuple-element.33), channel_id=1, source_target_pairs={{0,14},{2,4},{4,2},{6,10},{8,6},{10,12},{12,8},{14,0},{1,15},{3,5}... | collective-permute-start | bytes 196616 | tf_op jit(solution)/shard_map/ppermute | solution.py:517
  12.0 0.6 %collective-permute-start.2 = (bf16[256,128]{1,0:T(8,128)(2,1)S(1)}, bf16[256,128]{1,0:T(8,128)(2,1)S(1)}, u32[]{:S(2)}, u32[]{:S(2)}) collective-permute-start(bf16[256,128]{1,0:T(8,128)(2,1)S(1)} %get-tuple-element.34), channel_id=1, source_target_pairs={{0,12},{2,14},{4,0},{6,8},{8,4},{10,6},{12,10},{14,2},{1,13},{3,15... | collective-permute-start | bytes 196616 | tf_op jit(solution)/shard_map/ppermute | solution.py:517
  12.6 1.4 %collective-permute-start.3 = (bf16[256,128]{1,0:T(8,128)(2,1)S(1)}, bf16[256,128]{1,0:T(8,128)(2,1)S(1)}, u32[]{:S(2)}, u32[]{:S(2)}) collective-permute-start(bf16[256,128]{1,0:T(8,128)(2,1)S(1)} %get-tuple-element.35), channel_id=1, source_target_pairs={{0,4},{2,0},{4,6},{6,2},{8,10},{10,8},{12,14},{14,12},{1,5},{3,1},... | collective-permute-start | bytes 196616 | tf_op jit(solution)/shard_map/ppermute | solution.py:517
  14.0 1.0 %prepare.1 = (bf16[320,128]{1,0:T(8,128)(2,1)S(1)}, s32[128,128]{1,0:T(8,128)S(1)}, s32[128,128]{1,0:T(8,128)S(1)}, bf16[256,64]{1,0:T(8,128)(2,1)S(1)}, bf16[25...) custom-call(s32[128,128]{1,0:T(8,128)S(1)} %get-tuple-element.36.des, ...), custom_call_target="tpu_custom_call" | custom-call | flops 62914560 | bytes 524288 | tf_op jit(solution)/shard_map/prepare/pallas_call | solution.py:520
  15.0 0.0 collective-permute-done.rest_1_
  15.0 1.3 %collective-permute-done.1.rest_2_ = bf16[256,128]{1,0:T(8,128)(2,1)S(1)} collective-permute-done((bf16[256,128]{1,0:T(8,128)(2,1)S(1)}, bf16[256,128]{1,0:T(8,128)(2,1)S(1)}, u32[]{:S(2)}, u32[]{:S(2)}) %collective-permute-start.1) | collective-permute-done | bytes 65568 | tf_op jit(solution)/shard_map/ppermute | solution.py:517
  16.3 0.0 collective-permute-done.2.rest_3_
  16.3 0.6 %collective-permute-done.3.rest_4_ = bf16[256,128]{1,0:T(8,128)(2,1)S(1)} collective-permute-done((bf16[256,128]{1,0:T(8,128)(2,1)S(1)}, bf16[256,128]{1,0:T(8,128)(2,1)S(1)}, u32[]{:S(2)}, u32[]{:S(2)}) %collective-permute-start.3) | collective-permute-done | bytes 65568 | tf_op jit(solution)/shard_map/ppermute | solution.py:517
  17.0 2.7 %remap.1 = (f32[3,64,128]{2,1,0:T(8,128)S(1)}, bf16[64,128]{1,0:T(8,128)(2,1)S(1)}, bf16[192,128]{1,0:T(8,128)(2,1)S(1)}, bf16[192,128]{1,0:T(8,128)(2,1)S(1)}, ...) custom-call(bf16[256,128]{1,0:T(8,128)(2,1)S(1)} %get-tuple-element.31.rest_0_, ...), custom_call_target="tpu_custom_call" | custom-call | tf_op jit(solution)/shard_map/remap/pallas_call | solution.py:534
  19.6 1.4 %collective-permute-start.4 = (bf16[192,128]{1,0:T(8,128)(2,1)S(1)}, bf16[192,128]{1,0:T(8,128)(2,1)S(1)}, u32[]{:S(2)}, u32[]{:S(2)}) collective-permute-start(bf16[192,128]{1,0:T(8,128)(2,1)S(1)} %get-tuple-element.44), channel_id=1, source_target_pairs={{0,6},{2,12},{4,10},{6,0},{8,14},{10,4},{12,2},{14,8},{1,7},{3,13}... | collective-permute-start | bytes 147464 | tf_op jit(solution)/shard_map/ppermute | solution.py:517
  21.1 0.6 %collective-permute-start.5 = (bf16[192,128]{1,0:T(8,128)(2,1)S(1)}, bf16[192,128]{1,0:T(8,128)(2,1)S(1)}, u32[]{:S(2)}, u32[]{:S(2)}) collective-permute-start(bf16[192,128]{1,0:T(8,128)(2,1)S(1)} %get-tuple-element.45), channel_id=1, source_target_pairs={{0,4},{2,6},{4,2},{6,8},{8,12},{10,14},{12,0},{14,10},{1,5},{3,7},... | collective-permute-start | bytes 147464 | tf_op jit(solution)/shard_map/ppermute | solution.py:517
  21.7 3.2 %collective-permute-start.6 = (bf16[192,128]{1,0:T(8,128)(2,1)S(1)}, bf16[192,128]{1,0:T(8,128)(2,1)S(1)}, u32[]{:S(2)}, u32[]{:S(2)}) collective-permute-start(bf16[192,128]{1,0:T(8,128)(2,1)S(1)} %get-tuple-element.46), channel_id=1, source_target_pairs={{0,14},{2,4},{4,8},{6,2},{8,6},{10,12},{12,10},{14,0},{1,15},{3,5}... | collective-permute-start | bytes 147464 | tf_op jit(solution)/shard_map/ppermute | solution.py:517
  24.9 0.2 collective-permute-start.7
  25.1 1.9 %collective-permute-start.8 = (bf16[192,128]{1,0:T(8,128)(2,1)S(1)}, bf16[192,128]{1,0:T(8,128)(2,1)S(1)}, u32[]{:S(2)}, u32[]{:S(2)}) collective-permute-start(bf16[192,128]{1,0:T(8,128)(2,1)S(1)} %get-tuple-element.48), channel_id=1, source_target_pairs={{0,2},{2,0},{4,6},{6,4},{8,10},{10,8},{12,14},{14,12},{1,3},{3,1},... | collective-permute-start | bytes 147464 | tf_op jit(solution)/shard_map/ppermute | solution.py:517
  27.0 0.0 collective-permute-done.4.rest_0_
  27.0 1.5 %collective-permute-done.5.rest_1_ = bf16[192,128]{1,0:T(8,128)(2,1)S(1)} collective-permute-done((bf16[192,128]{1,0:T(8,128)(2,1)S(1)}, bf16[192,128]{1,0:T(8,128)(2,1)S(1)}, u32[]{:S(2)}, u32[]{:S(2)}) %collective-permute-start.5) | collective-permute-done | bytes 49184 | tf_op jit(solution)/shard_map/ppermute | solution.py:517
  28.4 0.4 %collective-permute-done.6.rest_2_ = bf16[192,128]{1,0:T(8,128)(2,1)S(1)} collective-permute-done((bf16[192,128]{1,0:T(8,128)(2,1)S(1)}, bf16[192,128]{1,0:T(8,128)(2,1)S(1)}, u32[]{:S(2)}, u32[]{:S(2)}) %collective-permute-start.6) | collective-permute-done | bytes 49184 | tf_op jit(solution)/shard_map/ppermute | solution.py:517
  28.8 0.2 collective-permute-done.7.rest_3_
  29.0 0.3 %collective-permute-done.8.rest_4_ = bf16[192,128]{1,0:T(8,128)(2,1)S(1)} collective-permute-done((bf16[192,128]{1,0:T(8,128)(2,1)S(1)}, bf16[192,128]{1,0:T(8,128)(2,1)S(1)}, u32[]{:S(2)}, u32[]{:S(2)}) %collective-permute-start.8) | collective-permute-done | bytes 49184 | tf_op jit(solution)/shard_map/ppermute | solution.py:517
  29.3 3.2 %finish.1 = (f32[3,64,128]{2,1,0:T(8,128)}, f32[128,128]{1,0:T(8,128)}) custom-call(bf16[192,128]{1,0:T(8,128)(2,1)S(1)} %collective-permute-done.4.rest_0_, bf16[192,128]{1,0:T(8,128)(2,1)S(1)} %collective-permute-done.5.rest_1_, bf16[192,128]{1,0:T(8,128)(2,1)S(1)} %collective-permute-done.6.rest_2_, bf16[192,128]{1,0:T(8,128)(2,1)S(1)} %collective-permute-done.7.rest_3_, ...), custom_call_target="tpu_custom_call" | custom-call | tf_op jit(solution)/shard_map/finish/pallas_call | solution.py:557
Async XLA Ops:
  5.5 9.5 %collective-permute-start = (bf16[256,128]{1,0:T(8,128)(2,1)S(1)}, bf16[256,128]{1,0:T(8,128)(2,1)S(1)}, u32[]{:S(2)}, u32[]{:S(2)}) collective-permute-start(bf16[256,128]{1,0:T(8,128)(2,1)S(1)} %get-tuple-element.32), channel_id=1, source_target_pairs={{0,2},{2,6},{4,8},{6,4},{8,12},{10,14},{12,0},{14,10},{1,3},{3,7},... | collective-permute-start | bytes 196616 | tf_op jit(solution)/shard_map/ppermute | solution.py:517
  8.5 7.9 %collective-permute-start.1 = (bf16[256,128]{1,0:T(8,128)(2,1)S(1)}, bf16[256,128]{1,0:T(8,128)(2,1)S(1)}, u32[]{:S(2)}, u32[]{:S(2)}) collective-permute-start(bf16[256,128]{1,0:T(8,128)(2,1)S(1)} %get-tuple-element.33), channel_id=1, source_target_pairs={{0,14},{2,4},{4,2},{6,10},{8,6},{10,12},{12,8},{14,0},{1,15},{3,5}... | collective-permute-start | bytes 196616 | tf_op jit(solution)/shard_map/ppermute | solution.py:517
  12.0 4.4 %collective-permute-start.2 = (bf16[256,128]{1,0:T(8,128)(2,1)S(1)}, bf16[256,128]{1,0:T(8,128)(2,1)S(1)}, u32[]{:S(2)}, u32[]{:S(2)}) collective-permute-start(bf16[256,128]{1,0:T(8,128)(2,1)S(1)} %get-tuple-element.34), channel_id=1, source_target_pairs={{0,12},{2,14},{4,0},{6,8},{8,4},{10,6},{12,10},{14,2},{1,13},{3,15... | collective-permute-start | bytes 196616 | tf_op jit(solution)/shard_map/ppermute | solution.py:517
  12.6 4.4 %collective-permute-start.3 = (bf16[256,128]{1,0:T(8,128)(2,1)S(1)}, bf16[256,128]{1,0:T(8,128)(2,1)S(1)}, u32[]{:S(2)}, u32[]{:S(2)}) collective-permute-start(bf16[256,128]{1,0:T(8,128)(2,1)S(1)} %get-tuple-element.35), channel_id=1, source_target_pairs={{0,4},{2,0},{4,6},{6,2},{8,10},{10,8},{12,14},{14,12},{1,5},{3,1},... | collective-permute-start | bytes 196616 | tf_op jit(solution)/shard_map/ppermute | solution.py:517
  19.6 7.3 %collective-permute-start.4 = (bf16[192,128]{1,0:T(8,128)(2,1)S(1)}, bf16[192,128]{1,0:T(8,128)(2,1)S(1)}, u32[]{:S(2)}, u32[]{:S(2)}) collective-permute-start(bf16[192,128]{1,0:T(8,128)(2,1)S(1)} %get-tuple-element.44), channel_id=1, source_target_pairs={{0,6},{2,12},{4,10},{6,0},{8,14},{10,4},{12,2},{14,8},{1,7},{3,13}... | collective-permute-start | bytes 147464 | tf_op jit(solution)/shard_map/ppermute | solution.py:517
  21.1 7.4 %collective-permute-start.5 = (bf16[192,128]{1,0:T(8,128)(2,1)S(1)}, bf16[192,128]{1,0:T(8,128)(2,1)S(1)}, u32[]{:S(2)}, u32[]{:S(2)}) collective-permute-start(bf16[192,128]{1,0:T(8,128)(2,1)S(1)} %get-tuple-element.45), channel_id=1, source_target_pairs={{0,4},{2,6},{4,2},{6,8},{8,12},{10,14},{12,0},{14,10},{1,5},{3,7},... | collective-permute-start | bytes 147464 | tf_op jit(solution)/shard_map/ppermute | solution.py:517
  21.7 7.2 %collective-permute-start.6 = (bf16[192,128]{1,0:T(8,128)(2,1)S(1)}, bf16[192,128]{1,0:T(8,128)(2,1)S(1)}, u32[]{:S(2)}, u32[]{:S(2)}) collective-permute-start(bf16[192,128]{1,0:T(8,128)(2,1)S(1)} %get-tuple-element.46), channel_id=1, source_target_pairs={{0,14},{2,4},{4,8},{6,2},{8,6},{10,12},{12,10},{14,0},{1,15},{3,5}... | collective-permute-start | bytes 147464 | tf_op jit(solution)/shard_map/ppermute | solution.py:517
  24.9 4.1 %collective-permute-start.7 = (bf16[192,128]{1,0:T(8,128)(2,1)S(1)}, bf16[192,128]{1,0:T(8,128)(2,1)S(1)}, u32[]{:S(2)}, u32[]{:S(2)}) collective-permute-start(bf16[192,128]{1,0:T(8,128)(2,1)S(1)} %get-tuple-element.47), channel_id=1, source_target_pairs={{0,12},{2,14},{4,0},{6,10},{8,4},{10,6},{12,8},{14,2},{1,13},{3,15... | collective-permute-start | bytes 147464 | tf_op jit(solution)/shard_map/ppermute | solution.py:517
  25.1 4.3 %collective-permute-start.8 = (bf16[192,128]{1,0:T(8,128)(2,1)S(1)}, bf16[192,128]{1,0:T(8,128)(2,1)S(1)}, u32[]{:S(2)}, u32[]{:S(2)}) collective-permute-start(bf16[192,128]{1,0:T(8,128)(2,1)S(1)} %get-tuple-element.48), channel_id=1, source_target_pairs={{0,2},{2,0},{4,6},{6,4},{8,10},{10,8},{12,14},{14,12},{1,3},{3,1},... | collective-permute-start | bytes 147464 | tf_op jit(solution)/shard_map/ppermute | solution.py:517

commit v5 on v4

--- a/solution.py
+++ b/solution.py
@@ -194,12 +194,14 @@
     index = jnp.zeros((blocks, LANES), I32)
     code = jnp.zeros((blocks, LANES), I32)
     group_id = iota((blocks, groups), 1)
+    lane = iota((blocks, LANES), 1)
     for o, (mask, hot, inside, count, base) in enumerate(ranks(offsets)):
         base = base.astype(I32)
         rank = base + inside.astype(I32)
         first = lax.shift_right_logical(base, 7)
         index = jnp.where(mask, jnp.bitwise_and(rank, LANES - 1), index)
-        code = jnp.where(mask, 2 * o + lax.shift_right_logical(rank, 7) - first, code)
+        code = jnp.where(mask, code + o, code)
+        code = jnp.where(lane >= jnp.bitwise_and(base, LANES - 1), code + (8 << o), code)
         hot_refs[o][0:blocks, :] = ones_where(group_id == first[:, :groups])
         hot_refs[o][blocks:, :] = ones_where(group_id == first[:, :groups] + 1)
     index_ref[...] = index
@@ -302,7 +304,7 @@
     message_refs, rest = rest[:messages], rest[messages:]
     own_ref, index_ref, code_ref = rest[:3]
     hot_refs, rest = rest[3 : 3 + NEIGHBOR_TILES], rest[3 + NEIGHBOR_TILES :]
-    ocean_ref, depth_ref, mask_ref, forcing_ref, out_ref, warm_ref, inbox = rest
+    ocean_ref, depth_ref, mask_ref, forcing_ref, out_ref, warm_ref, inbox, shifted = rest
     t, s = lax.axis_index("tile"), lax.axis_index("sub")
     size = message_refs[0].shape[0]
     groups = own_ref.shape[0]
@@ -318,9 +320,10 @@
         else:
             value = inbox[pl.ds(pl.multiple_of(pick(sources[o]) * size, 16), groups), :]
         lines = dot(hot_refs[o][...], value)
-        for half in range(2):
-            picked = jnp.take_along_axis(lines[half * blocks : (half + 1) * blocks], index, axis=1)
-            warm = jnp.where(code == 2 * o + half, picked, warm)
+        upper = jnp.bitwise_and(code, 8 << o) != 0
+        lines = jnp.where(upper, lines[:blocks], lines[blocks:])
+        picked = jnp.take_along_axis(lines, index, axis=1)
+        warm = jnp.where(jnp.bitwise_and(code, 7) == o, picked, warm)
     warm_ref[...] = warm
 
     tall = depth_ref.shape[0]
@@ -356,24 +359,67 @@
         turn = (LANES - i * HALO) % LANES
         right = pltpu.roll(from_right, turn, 1) if turn else from_right
         side = jnp.where(lane < HALO, right, jnp.where(lane >= LANES - HALO, left, 0.0))
-        wide.append(jnp.concatenate([main, side], axis=1))
+        wide.append([main, side])
     eta, east, north, m, depth, stress_x, stress_y, fresh = wide
-    row = iota((full, 2 * LANES), 0) + (t * tall - HALO)
+    row = iota((full, LANES), 0) + (t * tall - HALO)
     coriolis = 0.1 + 0.2 * (row.astype(F32) + 0.5) / (tall * count_t)
 
-    def dx(a):
-        return 0.5 * (pltpu.roll(a, 2 * LANES - 1, 1) - pltpu.roll(a, 1, 1))
-
-    def dy(a):
-        return 0.5 * (pltpu.roll(a, full - 1, 0) - pltpu.roll(a, 1, 0))
-
-    for _ in range(SUBS):
-        eta = m * (eta - (dx(east) + dy(north)) + fresh)
-        new_east = m * (east + coriolis * north - depth * dx(eta) + stress_x)
-        north = m * (north - coriolis * east - depth * dy(eta) + stress_y)
+    both = range(2)
+    half_m = [0.5 * m[i] for i in both]
+    half_d = [half_m[i] * depth[i] for i in both]
+    turning = [m[i] * coriolis for i in both]
+    fresh = [m[i] * fresh[i] for i in both]
+    stress_x = [m[i] * stress_x[i] for i in both]
+    stress_y = [m[i] * stress_y[i] for i in both]
+    shifted[:, 0:8, :] = jnp.zeros((4, 8, LANES), F32)
+    shifted[:, 8 + full :, :] = jnp.zeros((4, 8, LANES), F32)
+
+    def across(a):
+        ahead = [pltpu.roll(a[i], LANES - 1, 1) for i in both]
+        behind = [pltpu.roll(a[i], 1, 1) for i in both]
+        columns = lane[: a[0].shape[0]]
+        return [
+            jnp.where(columns == LANES - 1, ahead[1 - i], ahead[i])
+            - jnp.where(columns == 0, behind[1 - i], behind[i])
+            for i in both
+        ]
+
+    def along(a, first, rows, place):
+        result = []
+        for i in both:
+            shifted[place + i, 8 + first : 8 + first + a[i].shape[0], :] = a[i]
+            result.append(
+                shifted[place + i, 9 + rows.start : 9 + rows.stop, :]
+                - shifted[place + i, 7 + rows.start : 7 + rows.stop, :]
+            )
+        return result
+
+    first, last = 0, full
+    out_east, out_north = across(east), along(north, 0, slice(0, full), 0)
+    eta, east, north = ([m[i] * a[i] for i in both] for a in (eta, east, north))
+    for step in range(1, SUBS + 1):
+        if step > 1:
+            out_east, out_north = across(east), along(north, first, slice(first, last), 0)
+        eta = [eta[i] + fresh[i] - half_m[i] * (out_east[i] + out_north[i]) for i in both]
+        below_first = 2 * step // 8 * 8
+        slope_y = along(eta, first, slice(below_first, full - below_first), 2)
+        if below_first > first:
+            cut = slice(below_first - first, full - below_first - first)
+            eta, east, north, turning, stress_x, stress_y, half_d, fresh, half_m = (
+                [x[cut] for x in a]
+                for a in (eta, east, north, turning, stress_x, stress_y, half_d, fresh, half_m)
+            )
+            first, last = below_first, full - below_first
+        slope_x = across(eta)
+        new_east = [
+            east[i] + turning[i] * north[i] + stress_x[i] - half_d[i] * slope_x[i] for i in both
+        ]
+        north = [
+            north[i] - turning[i] * east[i] + stress_y[i] - half_d[i] * slope_y[i] for i in both
+        ]
         east = new_east
     for i, a in enumerate((eta, east, north)):
-        out_ref[i] = a[HALO : HALO + tall, :LANES]
+        out_ref[i] = a[0][HALO - first : HALO - first + tall]
 
 
 SCHEDULES = {
@@ -564,7 +610,10 @@
         ],
         in_specs=[vmem] * (returns + 3 + NEIGHBOR_TILES + 4),
         out_specs=[vmem] * 2,
-        scratch_shapes=[pltpu.VMEM((returns * message[0], LANES), BF16)],
+        scratch_shapes=[
+            pltpu.VMEM((returns * message[0], LANES), BF16),
+            pltpu.VMEM((4, tall + 2 * HALO + 16, LANES), F32),
+        ],
         compiler_params=params,
         name="finish",
     )(*received, own, *prepared[1:], ocean, depth, mask, forcing)

time: 32.9 us -> 32.5 us (0.988)
  Pallas kernels: 11.7 us -> 11.3 us
    pallas_call x1, Pallas kernels: 3.19 us -> 2.78 us  [shards(): pl.pallas_call(functools.partial(finish_kernel, moves['sources'], moves['...]
where the time goes in v5:
time: 32.5 us; the launch traced here: 32.1 us
  starting transfers between devices  15.8 us (49%)
  Pallas kernels  11.3 us (35%)
  waiting for transfers between devices  4.35 us (13%)
  between operations  0.67 us (2%)
    ppermute x9, starting transfers between devices, send(): lax.ppermute(array, axes, [(a, b) for a, b in enumerate(targets) if b >= 0])  15.8 us
    pallas_call x1, Pallas kernels, shards(): pl.pallas_call(functools.partial(route_kernel, moves['sent'], total), out...  4.84 us
    ppermute x9, waiting for transfers between devices, send(): lax.ppermute(array, axes, [(a, b) for a, b in enumerate(targets) if b >= 0])  4.35 us
    pallas_call x1, Pallas kernels, shards(): pl.pallas_call(functools.partial(finish_kernel, moves['sources'], moves['...  2.78 us
    pallas_call x1, Pallas kernels, shards(): pl.pallas_call(functools.partial(remap_kernel, moves['came'], moves['retu...  2.68 us
    pallas_call x1, Pallas kernels, shards(): pl.pallas_call(functools.partial(prepare_kernel, total), out_shape=[jax.S...  0.99 us
  transfers between devices with their start and end apart: 9, of which 6 were waited for; matrix products, arithmetic and copies ran while one was open for 0% of the time, Pallas kernels for 3%

profile of v5, /device:TPU:0, one launch (start us, length us, event | category | flops | bytes accessed | tf_op | source)
XLA Modules:
  0.0 32.1 jit_solution(9147718183375128771)
XLA Ops:
  0.6 4.8 %route.1 = (bf16[256,128]{1,0:T(8,128)(2,1)S(1)}, bf16[256,128]{1,0:T(8,128)(2,1)S(1)}, bf16[256,128]{1,0:T(8,128)(2,1)S(1)}, bf16[256,128]{1,0:T(8,128)(2,1)S(1...) custom-call(bf16[8,16384]{1,0:T(8,128)(2,1)} %bitcast.13, ...), custom_call_target="tpu_custom_call" | custom-call | tf_op jit(solution)/shard_map/route/pallas_call | solution.py:542
  5.5 3.0 %collective-permute-start = (bf16[256,128]{1,0:T(8,128)(2,1)S(1)}, bf16[256,128]{1,0:T(8,128)(2,1)S(1)}, u32[]{:S(2)}, u32[]{:S(2)}) collective-permute-start(bf16[256,128]{1,0:T(8,128)(2,1)S(1)} %get-tuple-element.32), channel_id=1, source_target_pairs={{0,2},{2,6},{4,8},{6,4},{8,12},{10,14},{12,0},{14,10},{1,3},{3,7},... | collective-permute-start | bytes 196616 | tf_op jit(solution)/shard_map/ppermute | solution.py:563
  8.5 3.5 %collective-permute-start.1 = (bf16[256,128]{1,0:T(8,128)(2,1)S(1)}, bf16[256,128]{1,0:T(8,128)(2,1)S(1)}, u32[]{:S(2)}, u32[]{:S(2)}) collective-permute-start(bf16[256,128]{1,0:T(8,128)(2,1)S(1)} %get-tuple-element.33), channel_id=1, source_target_pairs={{0,14},{2,4},{4,2},{6,10},{8,6},{10,12},{12,8},{14,0},{1,15},{3,5}... | collective-permute-start | bytes 196616 | tf_op jit(solution)/shard_map/ppermute | solution.py:563
  12.0 0.6 %collective-permute-start.2 = (bf16[256,128]{1,0:T(8,128)(2,1)S(1)}, bf16[256,128]{1,0:T(8,128)(2,1)S(1)}, u32[]{:S(2)}, u32[]{:S(2)}) collective-permute-start(bf16[256,128]{1,0:T(8,128)(2,1)S(1)} %get-tuple-element.34), channel_id=1, source_target_pairs={{0,12},{2,14},{4,0},{6,8},{8,4},{10,6},{12,10},{14,2},{1,13},{3,15... | collective-permute-start | bytes 196616 | tf_op jit(solution)/shard_map/ppermute | solution.py:563
  12.6 1.4 %collective-permute-start.3 = (bf16[256,128]{1,0:T(8,128)(2,1)S(1)}, bf16[256,128]{1,0:T(8,128)(2,1)S(1)}, u32[]{:S(2)}, u32[]{:S(2)}) collective-permute-start(bf16[256,128]{1,0:T(8,128)(2,1)S(1)} %get-tuple-element.35), channel_id=1, source_target_pairs={{0,4},{2,0},{4,6},{6,2},{8,10},{10,8},{12,14},{14,12},{1,5},{3,1},... | collective-permute-start | bytes 196616 | tf_op jit(solution)/shard_map/ppermute | solution.py:563
  14.0 1.0 %prepare.1 = (bf16[320,128]{1,0:T(8,128)(2,1)S(1)}, s32[128,128]{1,0:T(8,128)S(1)}, s32[128,128]{1,0:T(8,128)S(1)}, bf16[256,64]{1,0:T(8,128)(2,1)S(1)}, bf16[25...) custom-call(s32[128,128]{1,0:T(8,128)S(1)} %get-tuple-element.36.des, ...), custom_call_target="tpu_custom_call" | custom-call | flops 62914560 | bytes 524288 | tf_op jit(solution)/shard_map/prepare/pallas_call | solution.py:566
  15.0 0.0 collective-permute-done.rest_1_
  15.0 1.3 %collective-permute-done.1.rest_2_ = bf16[256,128]{1,0:T(8,128)(2,1)S(1)} collective-permute-done((bf16[256,128]{1,0:T(8,128)(2,1)S(1)}, bf16[256,128]{1,0:T(8,128)(2,1)S(1)}, u32[]{:S(2)}, u32[]{:S(2)}) %collective-permute-start.1) | collective-permute-done | bytes 65568 | tf_op jit(solution)/shard_map/ppermute | solution.py:563
  16.3 0.0 collective-permute-done.2.rest_3_
  16.3 0.6 %collective-permute-done.3.rest_4_ = bf16[256,128]{1,0:T(8,128)(2,1)S(1)} collective-permute-done((bf16[256,128]{1,0:T(8,128)(2,1)S(1)}, bf16[256,128]{1,0:T(8,128)(2,1)S(1)}, u32[]{:S(2)}, u32[]{:S(2)}) %collective-permute-start.3) | collective-permute-done | bytes 65568 | tf_op jit(solution)/shard_map/ppermute | solution.py:563
  17.0 2.7 %remap.1 = (f32[3,64,128]{2,1,0:T(8,128)S(1)}, bf16[64,128]{1,0:T(8,128)(2,1)S(1)}, bf16[192,128]{1,0:T(8,128)(2,1)S(1)}, bf16[192,128]{1,0:T(8,128)(2,1)S(1)}, ...) custom-call(bf16[256,128]{1,0:T(8,128)(2,1)S(1)} %get-tuple-element.31.rest_0_, ...), custom_call_target="tpu_custom_call" | custom-call | tf_op jit(solution)/shard_map/remap/pallas_call | solution.py:580
  19.6 1.4 %collective-permute-start.4 = (bf16[192,128]{1,0:T(8,128)(2,1)S(1)}, bf16[192,128]{1,0:T(8,128)(2,1)S(1)}, u32[]{:S(2)}, u32[]{:S(2)}) collective-permute-start(bf16[192,128]{1,0:T(8,128)(2,1)S(1)} %get-tuple-element.44), channel_id=1, source_target_pairs={{0,6},{2,12},{4,10},{6,0},{8,14},{10,4},{12,2},{14,8},{1,7},{3,13}... | collective-permute-start | bytes 147464 | tf_op jit(solution)/shard_map/ppermute | solution.py:563
  21.1 0.6 %collective-permute-start.5 = (bf16[192,128]{1,0:T(8,128)(2,1)S(1)}, bf16[192,128]{1,0:T(8,128)(2,1)S(1)}, u32[]{:S(2)}, u32[]{:S(2)}) collective-permute-start(bf16[192,128]{1,0:T(8,128)(2,1)S(1)} %get-tuple-element.45), channel_id=1, source_target_pairs={{0,4},{2,6},{4,2},{6,8},{8,12},{10,14},{12,0},{14,10},{1,5},{3,7},... | collective-permute-start | bytes 147464 | tf_op jit(solution)/shard_map/ppermute | solution.py:563
  21.7 3.2 %collective-permute-start.6 = (bf16[192,128]{1,0:T(8,128)(2,1)S(1)}, bf16[192,128]{1,0:T(8,128)(2,1)S(1)}, u32[]{:S(2)}, u32[]{:S(2)}) collective-permute-start(bf16[192,128]{1,0:T(8,128)(2,1)S(1)} %get-tuple-element.46), channel_id=1, source_target_pairs={{0,14},{2,4},{4,8},{6,2},{8,6},{10,12},{12,10},{14,0},{1,15},{3,5}... | collective-permute-start | bytes 147464 | tf_op jit(solution)/shard_map/ppermute | solution.py:563
  24.9 0.2 collective-permute-start.7
  25.1 1.9 %collective-permute-start.8 = (bf16[192,128]{1,0:T(8,128)(2,1)S(1)}, bf16[192,128]{1,0:T(8,128)(2,1)S(1)}, u32[]{:S(2)}, u32[]{:S(2)}) collective-permute-start(bf16[192,128]{1,0:T(8,128)(2,1)S(1)} %get-tuple-element.48), channel_id=1, source_target_pairs={{0,2},{2,0},{4,6},{6,4},{8,10},{10,8},{12,14},{14,12},{1,3},{3,1},... | collective-permute-start | bytes 147464 | tf_op jit(solution)/shard_map/ppermute | solution.py:563
  27.0 0.0 collective-permute-done.4.rest_0_
  27.0 1.5 %collective-permute-done.5.rest_1_ = bf16[192,128]{1,0:T(8,128)(2,1)S(1)} collective-permute-done((bf16[192,128]{1,0:T(8,128)(2,1)S(1)}, bf16[192,128]{1,0:T(8,128)(2,1)S(1)}, u32[]{:S(2)}, u32[]{:S(2)}) %collective-permute-start.5) | collective-permute-done | bytes 49184 | tf_op jit(solution)/shard_map/ppermute | solution.py:563
  28.4 0.4 %collective-permute-done.6.rest_2_ = bf16[192,128]{1,0:T(8,128)(2,1)S(1)} collective-permute-done((bf16[192,128]{1,0:T(8,128)(2,1)S(1)}, bf16[192,128]{1,0:T(8,128)(2,1)S(1)}, u32[]{:S(2)}, u32[]{:S(2)}) %collective-permute-start.6) | collective-permute-done | bytes 49184 | tf_op jit(solution)/shard_map/ppermute | solution.py:563
  28.8 0.2 collective-permute-done.7.rest_3_
  29.0 0.3 %collective-permute-done.8.rest_4_ = bf16[192,128]{1,0:T(8,128)(2,1)S(1)} collective-permute-done((bf16[192,128]{1,0:T(8,128)(2,1)S(1)}, bf16[192,128]{1,0:T(8,128)(2,1)S(1)}, u32[]{:S(2)}, u32[]{:S(2)}) %collective-permute-start.8) | collective-permute-done | bytes 49184 | tf_op jit(solution)/shard_map/ppermute | solution.py:563
  29.3 2.8 %finish.1 = (f32[3,64,128]{2,1,0:T(8,128)}, f32[128,128]{1,0:T(8,128)}) custom-call(bf16[192,128]{1,0:T(8,128)(2,1)S(1)} %collective-permute-done.4.rest_0_, bf16[192,128]{1,0:T(8,128)(2,1)S(1)} %collective-permute-done.5.rest_1_, bf16[192,128]{1,0:T(8,128)(2,1)S(1)} %collective-permute-done.6.rest_2_, bf16[192,128]{1,0:T(8,128)(2,1)S(1)} %collective-permute-done.7.rest_3_, ...), custom_call_target="tpu_custom_call" | custom-call | tf_op jit(solution)/shard_map/finish/pallas_call | solution.py:603
Async XLA Ops:
  5.5 9.5 %collective-permute-start = (bf16[256,128]{1,0:T(8,128)(2,1)S(1)}, bf16[256,128]{1,0:T(8,128)(2,1)S(1)}, u32[]{:S(2)}, u32[]{:S(2)}) collective-permute-start(bf16[256,128]{1,0:T(8,128)(2,1)S(1)} %get-tuple-element.32), channel_id=1, source_target_pairs={{0,2},{2,6},{4,8},{6,4},{8,12},{10,14},{12,0},{14,10},{1,3},{3,7},... | collective-permute-start | bytes 196616 | tf_op jit(solution)/shard_map/ppermute | solution.py:563
  8.5 7.9 %collective-permute-start.1 = (bf16[256,128]{1,0:T(8,128)(2,1)S(1)}, bf16[256,128]{1,0:T(8,128)(2,1)S(1)}, u32[]{:S(2)}, u32[]{:S(2)}) collective-permute-start(bf16[256,128]{1,0:T(8,128)(2,1)S(1)} %get-tuple-element.33), channel_id=1, source_target_pairs={{0,14},{2,4},{4,2},{6,10},{8,6},{10,12},{12,8},{14,0},{1,15},{3,5}... | collective-permute-start | bytes 196616 | tf_op jit(solution)/shard_map/ppermute | solution.py:563
  12.0 4.4 %collective-permute-start.2 = (bf16[256,128]{1,0:T(8,128)(2,1)S(1)}, bf16[256,128]{1,0:T(8,128)(2,1)S(1)}, u32[]{:S(2)}, u32[]{:S(2)}) collective-permute-start(bf16[256,128]{1,0:T(8,128)(2,1)S(1)} %get-tuple-element.34), channel_id=1, source_target_pairs={{0,12},{2,14},{4,0},{6,8},{8,4},{10,6},{12,10},{14,2},{1,13},{3,15... | collective-permute-start | bytes 196616 | tf_op jit(solution)/shard_map/ppermute | solution.py:563
  12.6 4.4 %collective-permute-start.3 = (bf16[256,128]{1,0:T(8,128)(2,1)S(1)}, bf16[256,128]{1,0:T(8,128)(2,1)S(1)}, u32[]{:S(2)}, u32[]{:S(2)}) collective-permute-start(bf16[256,128]{1,0:T(8,128)(2,1)S(1)} %get-tuple-element.35), channel_id=1, source_target_pairs={{0,4},{2,0},{4,6},{6,2},{8,10},{10,8},{12,14},{14,12},{1,5},{3,1},... | collective-permute-start | bytes 196616 | tf_op jit(solution)/shard_map/ppermute | solution.py:563
  19.6 7.3 %collective-permute-start.4 = (bf16[192,128]{1,0:T(8,128)(2,1)S(1)}, bf16[192,128]{1,0:T(8,128)(2,1)S(1)}, u32[]{:S(2)}, u32[]{:S(2)}) collective-permute-start(bf16[192,128]{1,0:T(8,128)(2,1)S(1)} %get-tuple-element.44), channel_id=1, source_target_pairs={{0,6},{2,12},{4,10},{6,0},{8,14},{10,4},{12,2},{14,8},{1,7},{3,13}... | collective-permute-start | bytes 147464 | tf_op jit(solution)/shard_map/ppermute | solution.py:563
  21.1 7.4 %collective-permute-start.5 = (bf16[192,128]{1,0:T(8,128)(2,1)S(1)}, bf16[192,128]{1,0:T(8,128)(2,1)S(1)}, u32[]{:S(2)}, u32[]{:S(2)}) collective-permute-start(bf16[192,128]{1,0:T(8,128)(2,1)S(1)} %get-tuple-element.45), channel_id=1, source_target_pairs={{0,4},{2,6},{4,2},{6,8},{8,12},{10,14},{12,0},{14,10},{1,5},{3,7},... | collective-permute-start | bytes 147464 | tf_op jit(solution)/shard_map/ppermute | solution.py:563
  21.7 7.2 %collective-permute-start.6 = (bf16[192,128]{1,0:T(8,128)(2,1)S(1)}, bf16[192,128]{1,0:T(8,128)(2,1)S(1)}, u32[]{:S(2)}, u32[]{:S(2)}) collective-permute-start(bf16[192,128]{1,0:T(8,128)(2,1)S(1)} %get-tuple-element.46), channel_id=1, source_target_pairs={{0,14},{2,4},{4,8},{6,2},{8,6},{10,12},{12,10},{14,0},{1,15},{3,5}... | collective-permute-start | bytes 147464 | tf_op jit(solution)/shard_map/ppermute | solution.py:563
  24.9 4.1 %collective-permute-start.7 = (bf16[192,128]{1,0:T(8,128)(2,1)S(1)}, bf16[192,128]{1,0:T(8,128)(2,1)S(1)}, u32[]{:S(2)}, u32[]{:S(2)}) collective-permute-start(bf16[192,128]{1,0:T(8,128)(2,1)S(1)} %get-tuple-element.47), channel_id=1, source_target_pairs={{0,12},{2,14},{4,0},{6,10},{8,4},{10,6},{12,8},{14,2},{1,13},{3,15... | collective-permute-start | bytes 147464 | tf_op jit(solution)/shard_map/ppermute | solution.py:563
  25.1 4.3 %collective-permute-start.8 = (bf16[192,128]{1,0:T(8,128)(2,1)S(1)}, bf16[192,128]{1,0:T(8,128)(2,1)S(1)}, u32[]{:S(2)}, u32[]{:S(2)}) collective-permute-start(bf16[192,128]{1,0:T(8,128)(2,1)S(1)} %get-tuple-element.48), channel_id=1, source_target_pairs={{0,2},{2,0},{4,6},{6,4},{8,10},{10,8},{12,14},{14,12},{1,3},{3,1},... | collective-permute-start | bytes 147464 | tf_op jit(solution)/shard_map/ppermute | solution.py:563

commit v6 on v5

--- a/solution.py
+++ b/solution.py
@@ -187,7 +187,10 @@
         copy.wait()
 
 
-def prepare_kernel(total, dest_ref, row_ref, blocks_ref, index_ref, code_ref, *hot_refs):
+def prepare_kernel(
+    total, dest_ref, row_ref, ocean_ref, depth_ref, mask_ref,
+    blocks_ref, edge_rows, edge_columns, index_ref, code_ref, *hot_refs
+):
     blocks = dest_ref.shape[0]
     groups = hot_refs[0].shape[1]
     offsets = offsets_of(dest_ref[...], total)
@@ -208,22 +211,31 @@
     code_ref[...] = code
     row = jnp.concatenate([row_ref[0:1, :], row_ref[1:2, :]], axis=1)
     blocks_ref[...] = ones_where(iota(blocks_ref.shape, 0) == row)
-
-
-def packed_columns(fields, low):
+    fields = [ocean_ref[0], ocean_ref[1], ocean_ref[2], mask_ref[...].astype(F32), depth_ref[...]]
+    for i, low in enumerate((False, True)):
+        edge_rows[i] = packed_rows(fields, low).astype(BF16)
+        edge_columns[i] = packed_columns(fields, low, 0).astype(BF16)
+
+
+def packed_columns(fields, low, start):
     lane = iota(fields[0].shape, 1)
-    packed = fields[0] if low else pltpu.roll(fields[0], HALO, 1)
-    for i in range(1, FIELDS):
+    packed = None
+    for i, field in enumerate(fields, start):
         turn = (i * HALO + (0 if low else HALO)) % LANES
-        packed = jnp.where(
-            lane >= i * HALO, pltpu.roll(fields[i], turn, 1) if turn else fields[i], packed
-        )
+        turned = pltpu.roll(field, turn, 1) if turn else field
+        packed = turned if packed is None else jnp.where(lane >= i * HALO, turned, packed)
     return packed
+
+
+def packed_rows(fields, low):
+    tall = fields[0].shape[0]
+    span = slice(0, HALO) if low else slice(tall - HALO, tall)
+    return jnp.concatenate([x[span] for x in fields], axis=0)
 
 
 def remap_kernel(came, returns, edges, *rest):
     arrived, rest = rest[: len(came)], rest[len(came) :]
-    ptr_hbm, hot_ref, w_ref, ocean_ref, skin_ref, depth_ref, mask_ref = rest[:7]
+    ptr_hbm, hot_ref, edge_rows, edge_columns, w_ref, skin_ref, mask_ref = rest[:7]
     forcing_ref, own_ref = rest[7:9]
     message_refs = rest[9 : 9 + len(returns)]
     slots, mapped, shares, homebound, bank, ptr_ref, sem = rest[9 + len(returns) :]
@@ -284,14 +296,17 @@
     returned = (value[:, :LANES] + value[:, LANES:]).astype(BF16)
     homebound[...] = returned
     own_ref[...] = returned[MIDDLE * groups : (MIDDLE + 1) * groups]
-    fields = [ocean_ref[0], ocean_ref[1], ocean_ref[2], mask_ref[...].astype(F32), depth_ref[...]]
-    fields += [forcing_ref[0], forcing_ref[1], forcing_ref[2]]
+    fields = [forcing_ref[0], forcing_ref[1], forcing_ref[2]]
     tall = fields[0].shape[0]
     rows = HALO * FIELDS
-    bank[0:rows, :] = jnp.concatenate([x[tall - HALO :] for x in fields], axis=0).astype(BF16)
-    bank[rows : 2 * rows, :] = jnp.concatenate([x[:HALO] for x in fields], axis=0).astype(BF16)
-    bank[2 * rows : 2 * rows + tall, :] = packed_columns(fields, False).astype(BF16)
-    bank[2 * rows + tall : 2 * rows + 2 * tall, :] = packed_columns(fields, True).astype(BF16)
+    still = HALO * (FIELDS - len(fields))
+    lane = iota((tall, LANES), 1)
+    for i, low in enumerate((False, True)):
+        bank[i * rows : i * rows + still, :] = edge_rows[i]
+        bank[i * rows + still : (i + 1) * rows, :] = packed_rows(fields, low).astype(BF16)
+        columns = packed_columns(fields, low, FIELDS - len(fields))
+        columns = jnp.where(lane < still, edge_columns[i].astype(F32), columns)
+        bank[2 * rows + i * tall : 2 * rows + (i + 1) * tall, :] = columns.astype(BF16)
     bank[2 * rows + 2 * tall :, :] = jnp.zeros((rows, LANES), BF16)
     for offset, edge, out in zip(returns, edges, message_refs):
         first = pl.multiple_of(pick(offset) * groups, 16)
@@ -425,15 +440,15 @@
 SCHEDULES = {
     (4, 2): (
         [
-            [1, 3, 4, 2, 6, 7, 0, 5],
+            [2, 3, 4, 1, 6, 7, 0, 5],
             [7, 2, 1, 5, 3, 6, 4, 0],
             [6, 7, 0, 4, 2, 3, 5, 1],
-            [2, 0, 3, 1, 5, 4, 7, 6],
+            [1, 0, 3, 2, 5, 4, 7, 6],
         ],
         [
             [3, 6, 5, 0, 7, 2, 1, 4],
-            [2, 3, 1, 4, 6, 7, 0, 5],
-            [7, 2, 4, 1, 3, 6, 5, 0],
+            [2, 3, 4, 1, 6, 7, 0, 5],
+            [7, 2, 1, 4, 3, 6, 5, 0],
             [6, 7, 0, 5, 2, 3, 4, 1],
             [1, 0, 3, 2, 5, 4, 7, 6],
         ],
@@ -565,15 +580,19 @@
     arrived = [results[0]] + [send(a, p) for a, p in zip(results[1:], moves["outward"])]
     prepared = pl.pallas_call(
         functools.partial(prepare_kernel, total),
-        out_shape=[jax.ShapeDtypeStruct((NEIGHBOR_TILES * groups, LANES), BF16)]
+        out_shape=[
+            jax.ShapeDtypeStruct((NEIGHBOR_TILES * groups, LANES), BF16),
+            jax.ShapeDtypeStruct((2, HALO * (FIELDS - 3), LANES), BF16),
+            jax.ShapeDtypeStruct((2, tall, LANES), BF16),
+        ]
         + [jax.ShapeDtypeStruct((blocks, LANES), I32)] * 2
         + [jax.ShapeDtypeStruct((2 * blocks, groups), BF16)] * NEIGHBOR_TILES,
-        in_specs=[vmem] * 2,
-        out_specs=[vmem] * (3 + NEIGHBOR_TILES),
+        in_specs=[vmem] * 5,
+        out_specs=[vmem] * (5 + NEIGHBOR_TILES),
         compiler_params=params,
         cost_estimate=pl.CostEstimate(flops=2 * 15 * LANES**3, bytes_accessed=2**19, transcendentals=0),
         name="prepare",
-    )(destination, rows)
+    )(destination, rows, ocean, depth, mask)
     returns = len(moves["returns"])
     message = (groups + HALO * FIELDS, LANES)
     row_blocks = weights.shape[0]
@@ -597,7 +616,7 @@
         ],
         compiler_params=params,
         name="remap",
-    )(*arrived, pltpu.with_memory_space_constraint(pointers, pltpu.HBM), prepared[0], weights, ocean, skin, depth, mask)
+    )(*arrived, pltpu.with_memory_space_constraint(pointers, pltpu.HBM), *prepared[:3], weights, skin, mask)
     forcing, own = outs[:2]
     received = [send(a, p) for a, p in zip(outs[2:], moves["homeward"])]
     ocean_out, warm = pl.pallas_call(
@@ -616,7 +635,7 @@
         ],
         compiler_params=params,
         name="finish",
-    )(*received, own, *prepared[1:], ocean, depth, mask, forcing)
+    )(*received, own, *prepared[3:], ocean, depth, mask, forcing)
     return ocean_out[None], warm.reshape(1, columns)
 
 

time: 32.5 us -> 32.1 us (0.988)
  no operation moved by 1% of the time
where the time goes in v6:
time: 32.1 us; the launch traced here: 31.9 us
  starting transfers between devices  15.7 us (49%)
  Pallas kernels  11.3 us (35%)
  waiting for transfers between devices  4.33 us (13%)
  between operations  0.67 us (2%)
    ppermute x9, starting transfers between devices, send(): lax.ppermute(array, axes, [(a, b) for a, b in enumerate(targets) if b >= 0])  15.7 us
    pallas_call x1, Pallas kernels, shards(): pl.pallas_call(functools.partial(route_kernel, moves['sent'], total), out...  4.8 us
    ppermute x9, waiting for transfers between devices, send(): lax.ppermute(array, axes, [(a, b) for a, b in enumerate(targets) if b >= 0])  4.33 us
    pallas_call x1, Pallas kernels, shards(): pl.pallas_call(functools.partial(finish_kernel, moves['sources'], moves['...  2.79 us
    pallas_call x1, Pallas kernels, shards(): pl.pallas_call(functools.partial(remap_kernel, moves['came'], moves['retu...  2.68 us
    pallas_call x1, Pallas kernels, shards(): pl.pallas_call(functools.partial(prepare_kernel, total), out_shape=[jax.S...  1 us
  transfers between devices with their start and end apart: 9, of which 6 were waited for; matrix products, arithmetic and copies ran while one was open for 0% of the time, Pallas kernels for 3%

profile of v6, /device:TPU:0, one launch (start us, length us, event | category | flops | bytes accessed | tf_op | source)
XLA Modules:
  0.0 31.9 jit_solution(16327779359831644280)
XLA Ops:
  0.6 4.8 %route.1 = (bf16[256,128]{1,0:T(8,128)(2,1)S(1)}, bf16[256,128]{1,0:T(8,128)(2,1)S(1)}, bf16[256,128]{1,0:T(8,128)(2,1)S(1)}, bf16[256,128]{1,0:T(8,128)(2,1)S(1...) custom-call(bf16[8,16384]{1,0:T(8,128)(2,1)} %bitcast.13, ...), custom_call_target="tpu_custom_call" | custom-call | tf_op jit(solution)/shard_map/route/pallas_call | solution.py:557
  5.4 3.1 %collective-permute-start = (bf16[256,128]{1,0:T(8,128)(2,1)S(1)}, bf16[256,128]{1,0:T(8,128)(2,1)S(1)}, u32[]{:S(2)}, u32[]{:S(2)}) collective-permute-start(bf16[256,128]{1,0:T(8,128)(2,1)S(1)} %get-tuple-element.34), channel_id=1, source_target_pairs={{0,4},{2,6},{4,8},{6,2},{8,12},{10,14},{12,0},{14,10},{1,5},{3,7},... | collective-permute-start | bytes 196616 | tf_op jit(solution)/shard_map/ppermute | solution.py:578
  8.5 3.4 %collective-permute-start.1 = (bf16[256,128]{1,0:T(8,128)(2,1)S(1)}, bf16[256,128]{1,0:T(8,128)(2,1)S(1)}, u32[]{:S(2)}, u32[]{:S(2)}) collective-permute-start(bf16[256,128]{1,0:T(8,128)(2,1)S(1)} %get-tuple-element.35), channel_id=1, source_target_pairs={{0,14},{2,4},{4,2},{6,10},{8,6},{10,12},{12,8},{14,0},{1,15},{3,5}... | collective-permute-start | bytes 196616 | tf_op jit(solution)/shard_map/ppermute | solution.py:578
  11.9 0.6 %collective-permute-start.2 = (bf16[256,128]{1,0:T(8,128)(2,1)S(1)}, bf16[256,128]{1,0:T(8,128)(2,1)S(1)}, u32[]{:S(2)}, u32[]{:S(2)}) collective-permute-start(bf16[256,128]{1,0:T(8,128)(2,1)S(1)} %get-tuple-element.36), channel_id=1, source_target_pairs={{0,12},{2,14},{4,0},{6,8},{8,4},{10,6},{12,10},{14,2},{1,13},{3,15... | collective-permute-start | bytes 196616 | tf_op jit(solution)/shard_map/ppermute | solution.py:578
  12.6 1.2 %collective-permute-start.3 = (bf16[256,128]{1,0:T(8,128)(2,1)S(1)}, bf16[256,128]{1,0:T(8,128)(2,1)S(1)}, u32[]{:S(2)}, u32[]{:S(2)}) collective-permute-start(bf16[256,128]{1,0:T(8,128)(2,1)S(1)} %get-tuple-element.37), channel_id=1, source_target_pairs={{0,2},{2,0},{4,6},{6,4},{8,10},{10,8},{12,14},{14,12},{1,3},{3,1},... | collective-permute-start | bytes 196616 | tf_op jit(solution)/shard_map/ppermute | solution.py:578
  13.8 1.0 %prepare.1 = (bf16[320,128]{1,0:T(8,128)(2,1)S(1)}, bf16[2,80,128]{2,1,0:T(8,128)(2,1)S(1)}, bf16[2,64,128]{2,1,0:T(8,128)(2,1)S(1)}, s32[128,128]{1,0:T(8,128)S...) custom-call(s32[128,128]{1,0:T(8,128)S(1)} %get-tuple-element.38.des, ...), custom_call_target="tpu_custom_call" | custom-call | flops 62914560 | bytes 524288 | tf_op jit(solution)/shard_map/prepare/pallas_call | solution.py:581
  14.8 0.0 collective-permute-done.rest_1_
  14.8 1.6 %collective-permute-done.1.rest_2_ = bf16[256,128]{1,0:T(8,128)(2,1)S(1)} collective-permute-done((bf16[256,128]{1,0:T(8,128)(2,1)S(1)}, bf16[256,128]{1,0:T(8,128)(2,1)S(1)}, u32[]{:S(2)}, u32[]{:S(2)}) %collective-permute-start.1) | collective-permute-done | bytes 65568 | tf_op jit(solution)/shard_map/ppermute | solution.py:578
  16.4 0.0 collective-permute-done.2.rest_3_
  16.4 0.6 %collective-permute-done.3.rest_4_ = bf16[256,128]{1,0:T(8,128)(2,1)S(1)} collective-permute-done((bf16[256,128]{1,0:T(8,128)(2,1)S(1)}, bf16[256,128]{1,0:T(8,128)(2,1)S(1)}, u32[]{:S(2)}, u32[]{:S(2)}) %collective-permute-start.3) | collective-permute-done | bytes 65568 | tf_op jit(solution)/shard_map/ppermute | solution.py:578
  16.9 2.7 %remap.1 = (f32[3,64,128]{2,1,0:T(8,128)S(1)}, bf16[64,128]{1,0:T(8,128)(2,1)S(1)}, bf16[192,128]{1,0:T(8,128)(2,1)S(1)}, bf16[192,128]{1,0:T(8,128)(2,1)S(1)}, ...) custom-call(bf16[256,128]{1,0:T(8,128)(2,1)S(1)} %get-tuple-element.33.rest_0_, ...), custom_call_target="tpu_custom_call" | custom-call | tf_op jit(solution)/shard_map/remap/pallas_call | solution.py:599
  19.6 1.5 %collective-permute-start.4 = (bf16[192,128]{1,0:T(8,128)(2,1)S(1)}, bf16[192,128]{1,0:T(8,128)(2,1)S(1)}, u32[]{:S(2)}, u32[]{:S(2)}) collective-permute-start(bf16[192,128]{1,0:T(8,128)(2,1)S(1)} %get-tuple-element.48), channel_id=1, source_target_pairs={{0,6},{2,12},{4,10},{6,0},{8,14},{10,4},{12,2},{14,8},{1,7},{3,13}... | collective-permute-start | bytes 147464 | tf_op jit(solution)/shard_map/ppermute | solution.py:578
  21.1 0.5 %collective-permute-start.5 = (bf16[192,128]{1,0:T(8,128)(2,1)S(1)}, bf16[192,128]{1,0:T(8,128)(2,1)S(1)}, u32[]{:S(2)}, u32[]{:S(2)}) collective-permute-start(bf16[192,128]{1,0:T(8,128)(2,1)S(1)} %get-tuple-element.49), channel_id=1, source_target_pairs={{0,4},{2,6},{4,8},{6,2},{8,12},{10,14},{12,0},{14,10},{1,5},{3,7},... | collective-permute-start | bytes 147464 | tf_op jit(solution)/shard_map/ppermute | solution.py:578
  21.6 3.1 %collective-permute-start.6 = (bf16[192,128]{1,0:T(8,128)(2,1)S(1)}, bf16[192,128]{1,0:T(8,128)(2,1)S(1)}, u32[]{:S(2)}, u32[]{:S(2)}) collective-permute-start(bf16[192,128]{1,0:T(8,128)(2,1)S(1)} %get-tuple-element.50), channel_id=1, source_target_pairs={{0,14},{2,4},{4,2},{6,8},{8,6},{10,12},{12,10},{14,0},{1,15},{3,5}... | collective-permute-start | bytes 147464 | tf_op jit(solution)/shard_map/ppermute | solution.py:578
  24.8 0.2 collective-permute-start.7
  25.0 1.9 %collective-permute-start.8 = (bf16[192,128]{1,0:T(8,128)(2,1)S(1)}, bf16[192,128]{1,0:T(8,128)(2,1)S(1)}, u32[]{:S(2)}, u32[]{:S(2)}) collective-permute-start(bf16[192,128]{1,0:T(8,128)(2,1)S(1)} %get-tuple-element.52), channel_id=1, source_target_pairs={{0,2},{2,0},{4,6},{6,4},{8,10},{10,8},{12,14},{14,12},{1,3},{3,1},... | collective-permute-start | bytes 147464 | tf_op jit(solution)/shard_map/ppermute | solution.py:578
  26.9 0.0 collective-permute-done.4.rest_0_
  26.9 0.4 %collective-permute-done.5.rest_1_ = bf16[192,128]{1,0:T(8,128)(2,1)S(1)} collective-permute-done((bf16[192,128]{1,0:T(8,128)(2,1)S(1)}, bf16[192,128]{1,0:T(8,128)(2,1)S(1)}, u32[]{:S(2)}, u32[]{:S(2)}) %collective-permute-start.5) | collective-permute-done | bytes 49184 | tf_op jit(solution)/shard_map/ppermute | solution.py:578
  27.3 1.1 %collective-permute-done.6.rest_2_ = bf16[192,128]{1,0:T(8,128)(2,1)S(1)} collective-permute-done((bf16[192,128]{1,0:T(8,128)(2,1)S(1)}, bf16[192,128]{1,0:T(8,128)(2,1)S(1)}, u32[]{:S(2)}, u32[]{:S(2)}) %collective-permute-start.6) | collective-permute-done | bytes 49184 | tf_op jit(solution)/shard_map/ppermute | solution.py:578
  28.4 0.5 %collective-permute-done.7.rest_3_ = bf16[192,128]{1,0:T(8,128)(2,1)S(1)} collective-permute-done((bf16[192,128]{1,0:T(8,128)(2,1)S(1)}, bf16[192,128]{1,0:T(8,128)(2,1)S(1)}, u32[]{:S(2)}, u32[]{:S(2)}) %collective-permute-start.7) | collective-permute-done | bytes 49184 | tf_op jit(solution)/shard_map/ppermute | solution.py:578
  28.9 0.2 collective-permute-done.8.rest_4_
  29.1 2.8 %finish.1 = (f32[3,64,128]{2,1,0:T(8,128)}, f32[128,128]{1,0:T(8,128)}) custom-call(bf16[192,128]{1,0:T(8,128)(2,1)S(1)} %collective-permute-done.4.rest_0_, bf16[192,128]{1,0:T(8,128)(2,1)S(1)} %collective-permute-done.5.rest_1_, bf16[192,128]{1,0:T(8,128)(2,1)S(1)} %collective-permute-done.6.rest_2_, bf16[192,128]{1,0:T(8,128)(2,1)S(1)} %collective-permute-done.7.rest_3_, ...), custom_call_target="tpu_custom_call" | custom-call | tf_op jit(solution)/shard_map/finish/pallas_call | solution.py:622
Async XLA Ops:
  5.4 9.4 %collective-permute-start = (bf16[256,128]{1,0:T(8,128)(2,1)S(1)}, bf16[256,128]{1,0:T(8,128)(2,1)S(1)}, u32[]{:S(2)}, u32[]{:S(2)}) collective-permute-start(bf16[256,128]{1,0:T(8,128)(2,1)S(1)} %get-tuple-element.34), channel_id=1, source_target_pairs={{0,4},{2,6},{4,8},{6,2},{8,12},{10,14},{12,0},{14,10},{1,5},{3,7},... | collective-permute-start | bytes 196616 | tf_op jit(solution)/shard_map/ppermute | solution.py:578
  8.5 7.9 %collective-permute-start.1 = (bf16[256,128]{1,0:T(8,128)(2,1)S(1)}, bf16[256,128]{1,0:T(8,128)(2,1)S(1)}, u32[]{:S(2)}, u32[]{:S(2)}) collective-permute-start(bf16[256,128]{1,0:T(8,128)(2,1)S(1)} %get-tuple-element.35), channel_id=1, source_target_pairs={{0,14},{2,4},{4,2},{6,10},{8,6},{10,12},{12,8},{14,0},{1,15},{3,5}... | collective-permute-start | bytes 196616 | tf_op jit(solution)/shard_map/ppermute | solution.py:578
  11.9 4.5 %collective-permute-start.2 = (bf16[256,128]{1,0:T(8,128)(2,1)S(1)}, bf16[256,128]{1,0:T(8,128)(2,1)S(1)}, u32[]{:S(2)}, u32[]{:S(2)}) collective-permute-start(bf16[256,128]{1,0:T(8,128)(2,1)S(1)} %get-tuple-element.36), channel_id=1, source_target_pairs={{0,12},{2,14},{4,0},{6,8},{8,4},{10,6},{12,10},{14,2},{1,13},{3,15... | collective-permute-start | bytes 196616 | tf_op jit(solution)/shard_map/ppermute | solution.py:578
  12.6 4.4 %collective-permute-start.3 = (bf16[256,128]{1,0:T(8,128)(2,1)S(1)}, bf16[256,128]{1,0:T(8,128)(2,1)S(1)}, u32[]{:S(2)}, u32[]{:S(2)}) collective-permute-start(bf16[256,128]{1,0:T(8,128)(2,1)S(1)} %get-tuple-element.37), channel_id=1, source_target_pairs={{0,2},{2,0},{4,6},{6,4},{8,10},{10,8},{12,14},{14,12},{1,3},{3,1},... | collective-permute-start | bytes 196616 | tf_op jit(solution)/shard_map/ppermute | solution.py:578
  19.6 7.3 %collective-permute-start.4 = (bf16[192,128]{1,0:T(8,128)(2,1)S(1)}, bf16[192,128]{1,0:T(8,128)(2,1)S(1)}, u32[]{:S(2)}, u32[]{:S(2)}) collective-permute-start(bf16[192,128]{1,0:T(8,128)(2,1)S(1)} %get-tuple-element.48), channel_id=1, source_target_pairs={{0,6},{2,12},{4,10},{6,0},{8,14},{10,4},{12,2},{14,8},{1,7},{3,13}... | collective-permute-start | bytes 147464 | tf_op jit(solution)/shard_map/ppermute | solution.py:578
  21.1 6.2 %collective-permute-start.5 = (bf16[192,128]{1,0:T(8,128)(2,1)S(1)}, bf16[192,128]{1,0:T(8,128)(2,1)S(1)}, u32[]{:S(2)}, u32[]{:S(2)}) collective-permute-start(bf16[192,128]{1,0:T(8,128)(2,1)S(1)} %get-tuple-element.49), channel_id=1, source_target_pairs={{0,4},{2,6},{4,8},{6,2},{8,12},{10,14},{12,0},{14,10},{1,5},{3,7},... | collective-permute-start | bytes 147464 | tf_op jit(solution)/shard_map/ppermute | solution.py:578
  21.6 6.8 %collective-permute-start.6 = (bf16[192,128]{1,0:T(8,128)(2,1)S(1)}, bf16[192,128]{1,0:T(8,128)(2,1)S(1)}, u32[]{:S(2)}, u32[]{:S(2)}) collective-permute-start(bf16[192,128]{1,0:T(8,128)(2,1)S(1)} %get-tuple-element.50), channel_id=1, source_target_pairs={{0,14},{2,4},{4,2},{6,8},{8,6},{10,12},{12,10},{14,0},{1,15},{3,5}... | collective-permute-start | bytes 147464 | tf_op jit(solution)/shard_map/ppermute | solution.py:578
  24.8 4.1 %collective-permute-start.7 = (bf16[192,128]{1,0:T(8,128)(2,1)S(1)}, bf16[192,128]{1,0:T(8,128)(2,1)S(1)}, u32[]{:S(2)}, u32[]{:S(2)}) collective-permute-start(bf16[192,128]{1,0:T(8,128)(2,1)S(1)} %get-tuple-element.51), channel_id=1, source_target_pairs={{0,12},{2,14},{4,0},{6,10},{8,4},{10,6},{12,8},{14,2},{1,13},{3,15... | collective-permute-start | bytes 147464 | tf_op jit(solution)/shard_map/ppermute | solution.py:578
  25.0 4.1 %collective-permute-start.8 = (bf16[192,128]{1,0:T(8,128)(2,1)S(1)}, bf16[192,128]{1,0:T(8,128)(2,1)S(1)}, u32[]{:S(2)}, u32[]{:S(2)}) collective-permute-start(bf16[192,128]{1,0:T(8,128)(2,1)S(1)} %get-tuple-element.52), channel_id=1, source_target_pairs={{0,2},{2,0},{4,6},{6,4},{8,10},{10,8},{12,14},{14,12},{1,3},{3,1},... | collective-permute-start | bytes 147464 | tf_op jit(solution)/shard_map/ppermute | solution.py:578

commit v7 on v6

--- a/solution.py
+++ b/solution.py
@@ -329,7 +329,8 @@
     index = index_ref[...]
     code = code_ref[...]
     warm = jnp.zeros((blocks, LANES), F32)
-    for o in range(NEIGHBOR_TILES):
+
+    def warmth(o, warm):
         if o == MIDDLE:
             value = own_ref[...]
         else:
@@ -338,8 +339,7 @@
         upper = jnp.bitwise_and(code, 8 << o) != 0
         lines = jnp.where(upper, lines[:blocks], lines[blocks:])
         picked = jnp.take_along_axis(lines, index, axis=1)
-        warm = jnp.where(jnp.bitwise_and(code, 7) == o, picked, warm)
-    warm_ref[...] = warm
+        return jnp.where(jnp.bitwise_and(code, 7) == o, picked, warm)
 
     tall = depth_ref.shape[0]
     full = tall + 2 * HALO
@@ -426,6 +426,8 @@
             )
             first, last = below_first, full - below_first
         slope_x = across(eta)
+        if step <= NEIGHBOR_TILES:
+            warm = warmth(step - 1, warm)
         new_east = [
             east[i] + turning[i] * north[i] + stress_x[i] - half_d[i] * slope_x[i] for i in both
         ]
@@ -433,6 +435,7 @@
             north[i] - turning[i] * east[i] + stress_y[i] - half_d[i] * slope_y[i] for i in both
         ]
         east = new_east
+    warm_ref[...] = warm
     for i, a in enumerate((eta, east, north)):
         out_ref[i] = a[0][HALO - first : HALO - first + tall]
 

time: 32.1 us -> 31.8 us (level)
  no operation moved by 1% of the time
where the time goes in v7:
time: 31.8 us; the launch traced here: 31.7 us
  starting transfers between devices  15.6 us (49%)
  Pallas kernels  11 us (35%)
  waiting for transfers between devices  4.34 us (14%)
  between operations  0.67 us (2%)
    ppermute x9, starting transfers between devices, send(): lax.ppermute(array, axes, [(a, b) for a, b in enumerate(targets) if b >= 0])  15.6 us
    pallas_call x1, Pallas kernels, shards(): pl.pallas_call(functools.partial(route_kernel, moves['sent'], total), out...  4.8 us
    ppermute x9, waiting for transfers between devices, send(): lax.ppermute(array, axes, [(a, b) for a, b in enumerate(targets) if b >= 0])  4.34 us
    pallas_call x1, Pallas kernels, shards(): pl.pallas_call(functools.partial(remap_kernel, moves['came'], moves['retu...  2.68 us
    pallas_call x1, Pallas kernels, shards(): pl.pallas_call(functools.partial(finish_kernel, moves['sources'], moves['...  2.56 us
    pallas_call x1, Pallas kernels, shards(): pl.pallas_call(functools.partial(prepare_kernel, total), out_shape=[jax.S...  1 us
  transfers between devices with their start and end apart: 9, of which 6 were waited for; matrix products, arithmetic and copies ran while one was open for 0% of the time, Pallas kernels for 3%

profile of v7, /device:TPU:0, one launch (start us, length us, event | category | flops | bytes accessed | tf_op | source)
XLA Modules:
  0.0 31.7 jit_solution(2959286299225059347)
XLA Ops:
  0.6 4.8 %route.1 = (bf16[256,128]{1,0:T(8,128)(2,1)S(1)}, bf16[256,128]{1,0:T(8,128)(2,1)S(1)}, bf16[256,128]{1,0:T(8,128)(2,1)S(1)}, bf16[256,128]{1,0:T(8,128)(2,1)S(1...) custom-call(bf16[8,16384]{1,0:T(8,128)(2,1)} %bitcast.13, ...), custom_call_target="tpu_custom_call" | custom-call | tf_op jit(solution)/shard_map/route/pallas_call | solution.py:560
  5.4 3.1 %collective-permute-start = (bf16[256,128]{1,0:T(8,128)(2,1)S(1)}, bf16[256,128]{1,0:T(8,128)(2,1)S(1)}, u32[]{:S(2)}, u32[]{:S(2)}) collective-permute-start(bf16[256,128]{1,0:T(8,128)(2,1)S(1)} %get-tuple-element.34), channel_id=1, source_target_pairs={{0,4},{2,6},{4,8},{6,2},{8,12},{10,14},{12,0},{14,10},{1,5},{3,7},... | collective-permute-start | bytes 196616 | tf_op jit(solution)/shard_map/ppermute | solution.py:581
  8.5 3.4 %collective-permute-start.1 = (bf16[256,128]{1,0:T(8,128)(2,1)S(1)}, bf16[256,128]{1,0:T(8,128)(2,1)S(1)}, u32[]{:S(2)}, u32[]{:S(2)}) collective-permute-start(bf16[256,128]{1,0:T(8,128)(2,1)S(1)} %get-tuple-element.35), channel_id=1, source_target_pairs={{0,14},{2,4},{4,2},{6,10},{8,6},{10,12},{12,8},{14,0},{1,15},{3,5}... | collective-permute-start | bytes 196616 | tf_op jit(solution)/shard_map/ppermute | solution.py:581
  11.9 0.6 %collective-permute-start.2 = (bf16[256,128]{1,0:T(8,128)(2,1)S(1)}, bf16[256,128]{1,0:T(8,128)(2,1)S(1)}, u32[]{:S(2)}, u32[]{:S(2)}) collective-permute-start(bf16[256,128]{1,0:T(8,128)(2,1)S(1)} %get-tuple-element.36), channel_id=1, source_target_pairs={{0,12},{2,14},{4,0},{6,8},{8,4},{10,6},{12,10},{14,2},{1,13},{3,15... | collective-permute-start | bytes 196616 | tf_op jit(solution)/shard_map/ppermute | solution.py:581
  12.6 1.2 %collective-permute-start.3 = (bf16[256,128]{1,0:T(8,128)(2,1)S(1)}, bf16[256,128]{1,0:T(8,128)(2,1)S(1)}, u32[]{:S(2)}, u32[]{:S(2)}) collective-permute-start(bf16[256,128]{1,0:T(8,128)(2,1)S(1)} %get-tuple-element.37), channel_id=1, source_target_pairs={{0,2},{2,0},{4,6},{6,4},{8,10},{10,8},{12,14},{14,12},{1,3},{3,1},... | collective-permute-start | bytes 196616 | tf_op jit(solution)/shard_map/ppermute | solution.py:581
  13.8 1.0 %prepare.1 = (bf16[320,128]{1,0:T(8,128)(2,1)S(1)}, bf16[2,80,128]{2,1,0:T(8,128)(2,1)S(1)}, bf16[2,64,128]{2,1,0:T(8,128)(2,1)S(1)}, s32[128,128]{1,0:T(8,128)S...) custom-call(s32[128,128]{1,0:T(8,128)S(1)} %get-tuple-element.38.des, ...), custom_call_target="tpu_custom_call" | custom-call | flops 62914560 | bytes 524288 | tf_op jit(solution)/shard_map/prepare/pallas_call | solution.py:584
  14.8 0.0 collective-permute-done.rest_1_
  14.8 1.6 %collective-permute-done.1.rest_2_ = bf16[256,128]{1,0:T(8,128)(2,1)S(1)} collective-permute-done((bf16[256,128]{1,0:T(8,128)(2,1)S(1)}, bf16[256,128]{1,0:T(8,128)(2,1)S(1)}, u32[]{:S(2)}, u32[]{:S(2)}) %collective-permute-start.1) | collective-permute-done | bytes 65568 | tf_op jit(solution)/shard_map/ppermute | solution.py:581
  16.4 0.0 collective-permute-done.2.rest_3_
  16.4 0.6 %collective-permute-done.3.rest_4_ = bf16[256,128]{1,0:T(8,128)(2,1)S(1)} collective-permute-done((bf16[256,128]{1,0:T(8,128)(2,1)S(1)}, bf16[256,128]{1,0:T(8,128)(2,1)S(1)}, u32[]{:S(2)}, u32[]{:S(2)}) %collective-permute-start.3) | collective-permute-done | bytes 65568 | tf_op jit(solution)/shard_map/ppermute | solution.py:581
  16.9 2.7 %remap.1 = (f32[3,64,128]{2,1,0:T(8,128)S(1)}, bf16[64,128]{1,0:T(8,128)(2,1)S(1)}, bf16[192,128]{1,0:T(8,128)(2,1)S(1)}, bf16[192,128]{1,0:T(8,128)(2,1)S(1)}, ...) custom-call(bf16[256,128]{1,0:T(8,128)(2,1)S(1)} %get-tuple-element.33.rest_0_, ...), custom_call_target="tpu_custom_call" | custom-call | tf_op jit(solution)/shard_map/remap/pallas_call | solution.py:602
  19.6 1.5 %collective-permute-start.4 = (bf16[192,128]{1,0:T(8,128)(2,1)S(1)}, bf16[192,128]{1,0:T(8,128)(2,1)S(1)}, u32[]{:S(2)}, u32[]{:S(2)}) collective-permute-start(bf16[192,128]{1,0:T(8,128)(2,1)S(1)} %get-tuple-element.48), channel_id=1, source_target_pairs={{0,6},{2,12},{4,10},{6,0},{8,14},{10,4},{12,2},{14,8},{1,7},{3,13}... | collective-permute-start | bytes 147464 | tf_op jit(solution)/shard_map/ppermute | solution.py:581
  21.1 0.5 %collective-permute-start.5 = (bf16[192,128]{1,0:T(8,128)(2,1)S(1)}, bf16[192,128]{1,0:T(8,128)(2,1)S(1)}, u32[]{:S(2)}, u32[]{:S(2)}) collective-permute-start(bf16[192,128]{1,0:T(8,128)(2,1)S(1)} %get-tuple-element.49), channel_id=1, source_target_pairs={{0,4},{2,6},{4,8},{6,2},{8,12},{10,14},{12,0},{14,10},{1,5},{3,7},... | collective-permute-start | bytes 147464 | tf_op jit(solution)/shard_map/ppermute | solution.py:581
  21.6 3.2 %collective-permute-start.6 = (bf16[192,128]{1,0:T(8,128)(2,1)S(1)}, bf16[192,128]{1,0:T(8,128)(2,1)S(1)}, u32[]{:S(2)}, u32[]{:S(2)}) collective-permute-start(bf16[192,128]{1,0:T(8,128)(2,1)S(1)} %get-tuple-element.50), channel_id=1, source_target_pairs={{0,14},{2,4},{4,2},{6,8},{8,6},{10,12},{12,10},{14,0},{1,15},{3,5}... | collective-permute-start | bytes 147464 | tf_op jit(solution)/shard_map/ppermute | solution.py:581
  24.8 0.3 collective-permute-start.7
  25.0 1.9 %collective-permute-start.8 = (bf16[192,128]{1,0:T(8,128)(2,1)S(1)}, bf16[192,128]{1,0:T(8,128)(2,1)S(1)}, u32[]{:S(2)}, u32[]{:S(2)}) collective-permute-start(bf16[192,128]{1,0:T(8,128)(2,1)S(1)} %get-tuple-element.52), channel_id=1, source_target_pairs={{0,2},{2,0},{4,6},{6,4},{8,10},{10,8},{12,14},{14,12},{1,3},{3,1},... | collective-permute-start | bytes 147464 | tf_op jit(solution)/shard_map/ppermute | solution.py:581
  26.9 0.0 collective-permute-done.4.rest_0_
  26.9 0.4 %collective-permute-done.5.rest_1_ = bf16[192,128]{1,0:T(8,128)(2,1)S(1)} collective-permute-done((bf16[192,128]{1,0:T(8,128)(2,1)S(1)}, bf16[192,128]{1,0:T(8,128)(2,1)S(1)}, u32[]{:S(2)}, u32[]{:S(2)}) %collective-permute-start.5) | collective-permute-done | bytes 49184 | tf_op jit(solution)/shard_map/ppermute | solution.py:581
  27.3 1.1 %collective-permute-done.6.rest_2_ = bf16[192,128]{1,0:T(8,128)(2,1)S(1)} collective-permute-done((bf16[192,128]{1,0:T(8,128)(2,1)S(1)}, bf16[192,128]{1,0:T(8,128)(2,1)S(1)}, u32[]{:S(2)}, u32[]{:S(2)}) %collective-permute-start.6) | collective-permute-done | bytes 49184 | tf_op jit(solution)/shard_map/ppermute | solution.py:581
  28.4 0.5 %collective-permute-done.7.rest_3_ = bf16[192,128]{1,0:T(8,128)(2,1)S(1)} collective-permute-done((bf16[192,128]{1,0:T(8,128)(2,1)S(1)}, bf16[192,128]{1,0:T(8,128)(2,1)S(1)}, u32[]{:S(2)}, u32[]{:S(2)}) %collective-permute-start.7) | collective-permute-done | bytes 49184 | tf_op jit(solution)/shard_map/ppermute | solution.py:581
  28.9 0.3 collective-permute-done.8.rest_4_
  29.1 2.6 %finish.1 = (f32[3,64,128]{2,1,0:T(8,128)}, f32[128,128]{1,0:T(8,128)}) custom-call(bf16[192,128]{1,0:T(8,128)(2,1)S(1)} %collective-permute-done.4.rest_0_, bf16[192,128]{1,0:T(8,128)(2,1)S(1)} %collective-permute-done.5.rest_1_, bf16[192,128]{1,0:T(8,128)(2,1)S(1)} %collective-permute-done.6.rest_2_, bf16[192,128]{1,0:T(8,128)(2,1)S(1)} %collective-permute-done.7.rest_3_, ...), custom_call_target="tpu_custom_call" | custom-call | tf_op jit(solution)/shard_map/finish/pallas_call | solution.py:625
Async XLA Ops:
  5.4 9.4 %collective-permute-start = (bf16[256,128]{1,0:T(8,128)(2,1)S(1)}, bf16[256,128]{1,0:T(8,128)(2,1)S(1)}, u32[]{:S(2)}, u32[]{:S(2)}) collective-permute-start(bf16[256,128]{1,0:T(8,128)(2,1)S(1)} %get-tuple-element.34), channel_id=1, source_target_pairs={{0,4},{2,6},{4,8},{6,2},{8,12},{10,14},{12,0},{14,10},{1,5},{3,7},... | collective-permute-start | bytes 196616 | tf_op jit(solution)/shard_map/ppermute | solution.py:581
  8.5 7.9 %collective-permute-start.1 = (bf16[256,128]{1,0:T(8,128)(2,1)S(1)}, bf16[256,128]{1,0:T(8,128)(2,1)S(1)}, u32[]{:S(2)}, u32[]{:S(2)}) collective-permute-start(bf16[256,128]{1,0:T(8,128)(2,1)S(1)} %get-tuple-element.35), channel_id=1, source_target_pairs={{0,14},{2,4},{4,2},{6,10},{8,6},{10,12},{12,8},{14,0},{1,15},{3,5}... | collective-permute-start | bytes 196616 | tf_op jit(solution)/shard_map/ppermute | solution.py:581
  11.9 4.5 %collective-permute-start.2 = (bf16[256,128]{1,0:T(8,128)(2,1)S(1)}, bf16[256,128]{1,0:T(8,128)(2,1)S(1)}, u32[]{:S(2)}, u32[]{:S(2)}) collective-permute-start(bf16[256,128]{1,0:T(8,128)(2,1)S(1)} %get-tuple-element.36), channel_id=1, source_target_pairs={{0,12},{2,14},{4,0},{6,8},{8,4},{10,6},{12,10},{14,2},{1,13},{3,15... | collective-permute-start | bytes 196616 | tf_op jit(solution)/shard_map/ppermute | solution.py:581
  12.6 4.4 %collective-permute-start.3 = (bf16[256,128]{1,0:T(8,128)(2,1)S(1)}, bf16[256,128]{1,0:T(8,128)(2,1)S(1)}, u32[]{:S(2)}, u32[]{:S(2)}) collective-permute-start(bf16[256,128]{1,0:T(8,128)(2,1)S(1)} %get-tuple-element.37), channel_id=1, source_target_pairs={{0,2},{2,0},{4,6},{6,4},{8,10},{10,8},{12,14},{14,12},{1,3},{3,1},... | collective-permute-start | bytes 196616 | tf_op jit(solution)/shard_map/ppermute | solution.py:581
  19.6 7.3 %collective-permute-start.4 = (bf16[192,128]{1,0:T(8,128)(2,1)S(1)}, bf16[192,128]{1,0:T(8,128)(2,1)S(1)}, u32[]{:S(2)}, u32[]{:S(2)}) collective-permute-start(bf16[192,128]{1,0:T(8,128)(2,1)S(1)} %get-tuple-element.48), channel_id=1, source_target_pairs={{0,6},{2,12},{4,10},{6,0},{8,14},{10,4},{12,2},{14,8},{1,7},{3,13}... | collective-permute-start | bytes 147464 | tf_op jit(solution)/shard_map/ppermute | solution.py:581
  21.1 6.2 %collective-permute-start.5 = (bf16[192,128]{1,0:T(8,128)(2,1)S(1)}, bf16[192,128]{1,0:T(8,128)(2,1)S(1)}, u32[]{:S(2)}, u32[]{:S(2)}) collective-permute-start(bf16[192,128]{1,0:T(8,128)(2,1)S(1)} %get-tuple-element.49), channel_id=1, source_target_pairs={{0,4},{2,6},{4,8},{6,2},{8,12},{10,14},{12,0},{14,10},{1,5},{3,7},... | collective-permute-start | bytes 147464 | tf_op jit(solution)/shard_map/ppermute | solution.py:581
  21.6 6.8 %collective-permute-start.6 = (bf16[192,128]{1,0:T(8,128)(2,1)S(1)}, bf16[192,128]{1,0:T(8,128)(2,1)S(1)}, u32[]{:S(2)}, u32[]{:S(2)}) collective-permute-start(bf16[192,128]{1,0:T(8,128)(2,1)S(1)} %get-tuple-element.50), channel_id=1, source_target_pairs={{0,14},{2,4},{4,2},{6,8},{8,6},{10,12},{12,10},{14,0},{1,15},{3,5}... | collective-permute-start | bytes 147464 | tf_op jit(solution)/shard_map/ppermute | solution.py:581
  24.8 4.1 %collective-permute-start.7 = (bf16[192,128]{1,0:T(8,128)(2,1)S(1)}, bf16[192,128]{1,0:T(8,128)(2,1)S(1)}, u32[]{:S(2)}, u32[]{:S(2)}) collective-permute-start(bf16[192,128]{1,0:T(8,128)(2,1)S(1)} %get-tuple-element.51), channel_id=1, source_target_pairs={{0,12},{2,14},{4,0},{6,10},{8,4},{10,6},{12,8},{14,2},{1,13},{3,15... | collective-permute-start | bytes 147464 | tf_op jit(solution)/shard_map/ppermute | solution.py:581
  25.0 4.1 %collective-permute-start.8 = (bf16[192,128]{1,0:T(8,128)(2,1)S(1)}, bf16[192,128]{1,0:T(8,128)(2,1)S(1)}, u32[]{:S(2)}, u32[]{:S(2)}) collective-permute-start(bf16[192,128]{1,0:T(8,128)(2,1)S(1)} %get-tuple-element.52), channel_id=1, source_target_pairs={{0,2},{2,0},{4,6},{6,4},{8,10},{10,8},{12,14},{14,12},{1,3},{3,1},... | collective-permute-start | bytes 147464 | tf_op jit(solution)/shard_map/ppermute | solution.py:581

commit v8 on v7

--- a/solution.py
+++ b/solution.py
@@ -235,11 +235,11 @@
 
 def remap_kernel(came, returns, edges, *rest):
     arrived, rest = rest[: len(came)], rest[len(came) :]
-    ptr_hbm, hot_ref, edge_rows, edge_columns, w_ref, skin_ref, mask_ref = rest[:7]
+    ptr_vmem, hot_ref, edge_rows, edge_columns, w_ref, skin_ref, mask_ref = rest[:7]
     forcing_ref, own_ref = rest[7:9]
     message_refs = rest[9 : 9 + len(returns)]
     slots, mapped, shares, homebound, bank, ptr_ref, sem = rest[9 + len(returns) :]
-    pointers = pltpu.make_async_copy(ptr_hbm, ptr_ref, sem)
+    pointers = pltpu.make_async_copy(ptr_vmem, ptr_ref, sem)
     pointers.start()
     per_step = 8
     size = arrived[0].shape[0]
@@ -606,7 +606,7 @@
             jax.ShapeDtypeStruct((groups, LANES), BF16),
         ]
         + [jax.ShapeDtypeStruct(message, BF16)] * returns,
-        in_specs=[vmem] * sends + [hbm] + [vmem] * 6,
+        in_specs=[vmem] * (sends + 7),
         out_specs=[vmem] * (2 + returns),
         scratch_shapes=[
             pltpu.VMEM((NEIGHBOR_TILES * groups * 4 + 8, LANES), F32),
@@ -619,7 +619,7 @@
         ],
         compiler_params=params,
         name="remap",
-    )(*arrived, pltpu.with_memory_space_constraint(pointers, pltpu.HBM), *prepared[:3], weights, skin, mask)
+    )(*arrived, rows, *prepared[:3], weights, skin, mask)
     forcing, own = outs[:2]
     received = [send(a, p) for a, p in zip(outs[2:], moves["homeward"])]
     ocean_out, warm = pl.pallas_call(

time: 31.8 us -> 31.7 us (level)
  no operation moved by 1% of the time
where the time goes in v8:
time: 31.7 us; the launch traced here: 31.6 us
  starting transfers between devices  15.6 us (49%)
  Pallas kernels  10.9 us (34%)
  waiting for transfers between devices  4.34 us (14%)
  between operations  0.67 us (2%)
    ppermute x9, starting transfers between devices, send(): lax.ppermute(array, axes, [(a, b) for a, b in enumerate(targets) if b >= 0])  15.6 us
    pallas_call x1, Pallas kernels, shards(): pl.pallas_call(functools.partial(route_kernel, moves['sent'], total), out...  4.8 us
    ppermute x9, waiting for transfers between devices, send(): lax.ppermute(array, axes, [(a, b) for a, b in enumerate(targets) if b >= 0])  4.34 us
    pallas_call x1, Pallas kernels, shards(): pl.pallas_call(functools.partial(finish_kernel, moves['sources'], moves['...  2.56 us
    pallas_call x1, Pallas kernels, shards(): pl.pallas_call(functools.partial(remap_kernel, moves['came'], moves['retu...  2.54 us
    pallas_call x1, Pallas kernels, shards(): pl.pallas_call(functools.partial(prepare_kernel, total), out_shape=[jax.S...  1 us
  transfers between devices with their start and end apart: 9, of which 6 were waited for; matrix products, arithmetic and copies ran while one was open for 0% of the time, Pallas kernels for 3%

profile of v8, /device:TPU:0, one launch (start us, length us, event | category | flops | bytes accessed | tf_op | source)
XLA Modules:
  0.0 31.6 jit_solution(13145390495949080044)
XLA Ops:
  0.6 4.8 %route.1 = (bf16[256,128]{1,0:T(8,128)(2,1)S(1)}, bf16[256,128]{1,0:T(8,128)(2,1)S(1)}, bf16[256,128]{1,0:T(8,128)(2,1)S(1)}, bf16[256,128]{1,0:T(8,128)(2,1)S(1...) custom-call(bf16[8,16384]{1,0:T(8,128)(2,1)} %bitcast.13, ...), custom_call_target="tpu_custom_call" | custom-call | tf_op jit(solution)/shard_map/route/pallas_call | solution.py:560
  5.4 3.1 %collective-permute-start = (bf16[256,128]{1,0:T(8,128)(2,1)S(1)}, bf16[256,128]{1,0:T(8,128)(2,1)S(1)}, u32[]{:S(2)}, u32[]{:S(2)}) collective-permute-start(bf16[256,128]{1,0:T(8,128)(2,1)S(1)} %get-tuple-element.34), channel_id=1, source_target_pairs={{0,4},{2,6},{4,8},{6,2},{8,12},{10,14},{12,0},{14,10},{1,5},{3,7},... | collective-permute-start | bytes 196616 | tf_op jit(solution)/shard_map/ppermute | solution.py:581
  8.5 3.4 %collective-permute-start.1 = (bf16[256,128]{1,0:T(8,128)(2,1)S(1)}, bf16[256,128]{1,0:T(8,128)(2,1)S(1)}, u32[]{:S(2)}, u32[]{:S(2)}) collective-permute-start(bf16[256,128]{1,0:T(8,128)(2,1)S(1)} %get-tuple-element.35), channel_id=1, source_target_pairs={{0,14},{2,4},{4,2},{6,10},{8,6},{10,12},{12,8},{14,0},{1,15},{3,5}... | collective-permute-start | bytes 196616 | tf_op jit(solution)/shard_map/ppermute | solution.py:581
  11.9 0.6 %collective-permute-start.2 = (bf16[256,128]{1,0:T(8,128)(2,1)S(1)}, bf16[256,128]{1,0:T(8,128)(2,1)S(1)}, u32[]{:S(2)}, u32[]{:S(2)}) collective-permute-start(bf16[256,128]{1,0:T(8,128)(2,1)S(1)} %get-tuple-element.36), channel_id=1, source_target_pairs={{0,12},{2,14},{4,0},{6,8},{8,4},{10,6},{12,10},{14,2},{1,13},{3,15... | collective-permute-start | bytes 196616 | tf_op jit(solution)/shard_map/ppermute | solution.py:581
  12.6 1.2 %collective-permute-start.3 = (bf16[256,128]{1,0:T(8,128)(2,1)S(1)}, bf16[256,128]{1,0:T(8,128)(2,1)S(1)}, u32[]{:S(2)}, u32[]{:S(2)}) collective-permute-start(bf16[256,128]{1,0:T(8,128)(2,1)S(1)} %get-tuple-element.37), channel_id=1, source_target_pairs={{0,2},{2,0},{4,6},{6,4},{8,10},{10,8},{12,14},{14,12},{1,3},{3,1},... | collective-permute-start | bytes 196616 | tf_op jit(solution)/shard_map/ppermute | solution.py:581
  13.8 1.0 %prepare.1 = (bf16[320,128]{1,0:T(8,128)(2,1)S(1)}, bf16[2,80,128]{2,1,0:T(8,128)(2,1)S(1)}, bf16[2,64,128]{2,1,0:T(8,128)(2,1)S(1)}, s32[128,128]{1,0:T(8,128)S...) custom-call(s32[128,128]{1,0:T(8,128)S(1)} %get-tuple-element.39.des, ...), custom_call_target="tpu_custom_call" | custom-call | flops 62914560 | bytes 524288 | tf_op jit(solution)/shard_map/prepare/pallas_call | solution.py:584
  14.8 0.0 collective-permute-done.rest_1_
  14.8 1.6 %collective-permute-done.1.rest_2_ = bf16[256,128]{1,0:T(8,128)(2,1)S(1)} collective-permute-done((bf16[256,128]{1,0:T(8,128)(2,1)S(1)}, bf16[256,128]{1,0:T(8,128)(2,1)S(1)}, u32[]{:S(2)}, u32[]{:S(2)}) %collective-permute-start.1) | collective-permute-done | bytes 65568 | tf_op jit(solution)/shard_map/ppermute | solution.py:581
  16.4 0.0 collective-permute-done.2.rest_3_
  16.4 0.6 %collective-permute-done.3.rest_4_ = bf16[256,128]{1,0:T(8,128)(2,1)S(1)} collective-permute-done((bf16[256,128]{1,0:T(8,128)(2,1)S(1)}, bf16[256,128]{1,0:T(8,128)(2,1)S(1)}, u32[]{:S(2)}, u32[]{:S(2)}) %collective-permute-start.3) | collective-permute-done | bytes 65568 | tf_op jit(solution)/shard_map/ppermute | solution.py:581
  16.9 2.5 %remap.1 = (f32[3,64,128]{2,1,0:T(8,128)S(1)}, bf16[64,128]{1,0:T(8,128)(2,1)S(1)}, bf16[192,128]{1,0:T(8,128)(2,1)S(1)}, bf16[192,128]{1,0:T(8,128)(2,1)S(1)}, ...) custom-call(bf16[256,128]{1,0:T(8,128)(2,1)S(1)} %get-tuple-element.33.rest_0_, ...), custom_call_target="tpu_custom_call" | custom-call | tf_op jit(solution)/shard_map/remap/pallas_call | solution.py:602
  19.5 1.5 %collective-permute-start.4 = (bf16[192,128]{1,0:T(8,128)(2,1)S(1)}, bf16[192,128]{1,0:T(8,128)(2,1)S(1)}, u32[]{:S(2)}, u32[]{:S(2)}) collective-permute-start(bf16[192,128]{1,0:T(8,128)(2,1)S(1)} %get-tuple-element.48), channel_id=1, source_target_pairs={{0,6},{2,12},{4,10},{6,0},{8,14},{10,4},{12,2},{14,8},{1,7},{3,13}... | collective-permute-start | bytes 147464 | tf_op jit(solution)/shard_map/ppermute | solution.py:581
  21.0 0.5 %collective-permute-start.5 = (bf16[192,128]{1,0:T(8,128)(2,1)S(1)}, bf16[192,128]{1,0:T(8,128)(2,1)S(1)}, u32[]{:S(2)}, u32[]{:S(2)}) collective-permute-start(bf16[192,128]{1,0:T(8,128)(2,1)S(1)} %get-tuple-element.49), channel_id=1, source_target_pairs={{0,4},{2,6},{4,8},{6,2},{8,12},{10,14},{12,0},{14,10},{1,5},{3,7},... | collective-permute-start | bytes 147464 | tf_op jit(solution)/shard_map/ppermute | solution.py:581
  21.5 3.2 %collective-permute-start.6 = (bf16[192,128]{1,0:T(8,128)(2,1)S(1)}, bf16[192,128]{1,0:T(8,128)(2,1)S(1)}, u32[]{:S(2)}, u32[]{:S(2)}) collective-permute-start(bf16[192,128]{1,0:T(8,128)(2,1)S(1)} %get-tuple-element.50), channel_id=1, source_target_pairs={{0,14},{2,4},{4,2},{6,8},{8,6},{10,12},{12,10},{14,0},{1,15},{3,5}... | collective-permute-start | bytes 147464 | tf_op jit(solution)/shard_map/ppermute | solution.py:581
  24.7 0.2 collective-permute-start.7
  24.9 1.9 %collective-permute-start.8 = (bf16[192,128]{1,0:T(8,128)(2,1)S(1)}, bf16[192,128]{1,0:T(8,128)(2,1)S(1)}, u32[]{:S(2)}, u32[]{:S(2)}) collective-permute-start(bf16[192,128]{1,0:T(8,128)(2,1)S(1)} %get-tuple-element.52), channel_id=1, source_target_pairs={{0,2},{2,0},{4,6},{6,4},{8,10},{10,8},{12,14},{14,12},{1,3},{3,1},... | collective-permute-start | bytes 147464 | tf_op jit(solution)/shard_map/ppermute | solution.py:581
  26.8 0.0 collective-permute-done.4.rest_0_
  26.8 0.4 %collective-permute-done.5.rest_1_ = bf16[192,128]{1,0:T(8,128)(2,1)S(1)} collective-permute-done((bf16[192,128]{1,0:T(8,128)(2,1)S(1)}, bf16[192,128]{1,0:T(8,128)(2,1)S(1)}, u32[]{:S(2)}, u32[]{:S(2)}) %collective-permute-start.5) | collective-permute-done | bytes 49184 | tf_op jit(solution)/shard_map/ppermute | solution.py:581
  27.2 1.1 %collective-permute-done.6.rest_2_ = bf16[192,128]{1,0:T(8,128)(2,1)S(1)} collective-permute-done((bf16[192,128]{1,0:T(8,128)(2,1)S(1)}, bf16[192,128]{1,0:T(8,128)(2,1)S(1)}, u32[]{:S(2)}, u32[]{:S(2)}) %collective-permute-start.6) | collective-permute-done | bytes 49184 | tf_op jit(solution)/shard_map/ppermute | solution.py:581
  28.3 0.5 %collective-permute-done.7.rest_3_ = bf16[192,128]{1,0:T(8,128)(2,1)S(1)} collective-permute-done((bf16[192,128]{1,0:T(8,128)(2,1)S(1)}, bf16[192,128]{1,0:T(8,128)(2,1)S(1)}, u32[]{:S(2)}, u32[]{:S(2)}) %collective-permute-start.7) | collective-permute-done | bytes 49184 | tf_op jit(solution)/shard_map/ppermute | solution.py:581
  28.7 0.2 collective-permute-done.8.rest_4_
  29.0 2.6 %finish.1 = (f32[3,64,128]{2,1,0:T(8,128)}, f32[128,128]{1,0:T(8,128)}) custom-call(bf16[192,128]{1,0:T(8,128)(2,1)S(1)} %collective-permute-done.4.rest_0_, bf16[192,128]{1,0:T(8,128)(2,1)S(1)} %collective-permute-done.5.rest_1_, bf16[192,128]{1,0:T(8,128)(2,1)S(1)} %collective-permute-done.6.rest_2_, bf16[192,128]{1,0:T(8,128)(2,1)S(1)} %collective-permute-done.7.rest_3_, ...), custom_call_target="tpu_custom_call" | custom-call | tf_op jit(solution)/shard_map/finish/pallas_call | solution.py:625
Async XLA Ops:
  5.4 9.4 %collective-permute-start = (bf16[256,128]{1,0:T(8,128)(2,1)S(1)}, bf16[256,128]{1,0:T(8,128)(2,1)S(1)}, u32[]{:S(2)}, u32[]{:S(2)}) collective-permute-start(bf16[256,128]{1,0:T(8,128)(2,1)S(1)} %get-tuple-element.34), channel_id=1, source_target_pairs={{0,4},{2,6},{4,8},{6,2},{8,12},{10,14},{12,0},{14,10},{1,5},{3,7},... | collective-permute-start | bytes 196616 | tf_op jit(solution)/shard_map/ppermute | solution.py:581
  8.5 7.9 %collective-permute-start.1 = (bf16[256,128]{1,0:T(8,128)(2,1)S(1)}, bf16[256,128]{1,0:T(8,128)(2,1)S(1)}, u32[]{:S(2)}, u32[]{:S(2)}) collective-permute-start(bf16[256,128]{1,0:T(8,128)(2,1)S(1)} %get-tuple-element.35), channel_id=1, source_target_pairs={{0,14},{2,4},{4,2},{6,10},{8,6},{10,12},{12,8},{14,0},{1,15},{3,5}... | collective-permute-start | bytes 196616 | tf_op jit(solution)/shard_map/ppermute | solution.py:581
  11.9 4.5 %collective-permute-start.2 = (bf16[256,128]{1,0:T(8,128)(2,1)S(1)}, bf16[256,128]{1,0:T(8,128)(2,1)S(1)}, u32[]{:S(2)}, u32[]{:S(2)}) collective-permute-start(bf16[256,128]{1,0:T(8,128)(2,1)S(1)} %get-tuple-element.36), channel_id=1, source_target_pairs={{0,12},{2,14},{4,0},{6,8},{8,4},{10,6},{12,10},{14,2},{1,13},{3,15... | collective-permute-start | bytes 196616 | tf_op jit(solution)/shard_map/ppermute | solution.py:581
  12.6 4.4 %collective-permute-start.3 = (bf16[256,128]{1,0:T(8,128)(2,1)S(1)}, bf16[256,128]{1,0:T(8,128)(2,1)S(1)}, u32[]{:S(2)}, u32[]{:S(2)}) collective-permute-start(bf16[256,128]{1,0:T(8,128)(2,1)S(1)} %get-tuple-element.37), channel_id=1, source_target_pairs={{0,2},{2,0},{4,6},{6,4},{8,10},{10,8},{12,14},{14,12},{1,3},{3,1},... | collective-permute-start | bytes 196616 | tf_op jit(solution)/shard_map/ppermute | solution.py:581
  19.5 7.3 %collective-permute-start.4 = (bf16[192,128]{1,0:T(8,128)(2,1)S(1)}, bf16[192,128]{1,0:T(8,128)(2,1)S(1)}, u32[]{:S(2)}, u32[]{:S(2)}) collective-permute-start(bf16[192,128]{1,0:T(8,128)(2,1)S(1)} %get-tuple-element.48), channel_id=1, source_target_pairs={{0,6},{2,12},{4,10},{6,0},{8,14},{10,4},{12,2},{14,8},{1,7},{3,13}... | collective-permute-start | bytes 147464 | tf_op jit(solution)/shard_map/ppermute | solution.py:581
  21.0 6.2 %collective-permute-start.5 = (bf16[192,128]{1,0:T(8,128)(2,1)S(1)}, bf16[192,128]{1,0:T(8,128)(2,1)S(1)}, u32[]{:S(2)}, u32[]{:S(2)}) collective-permute-start(bf16[192,128]{1,0:T(8,128)(2,1)S(1)} %get-tuple-element.49), channel_id=1, source_target_pairs={{0,4},{2,6},{4,8},{6,2},{8,12},{10,14},{12,0},{14,10},{1,5},{3,7},... | collective-permute-start | bytes 147464 | tf_op jit(solution)/shard_map/ppermute | solution.py:581
  21.5 6.8 %collective-permute-start.6 = (bf16[192,128]{1,0:T(8,128)(2,1)S(1)}, bf16[192,128]{1,0:T(8,128)(2,1)S(1)}, u32[]{:S(2)}, u32[]{:S(2)}) collective-permute-start(bf16[192,128]{1,0:T(8,128)(2,1)S(1)} %get-tuple-element.50), channel_id=1, source_target_pairs={{0,14},{2,4},{4,2},{6,8},{8,6},{10,12},{12,10},{14,0},{1,15},{3,5}... | collective-permute-start | bytes 147464 | tf_op jit(solution)/shard_map/ppermute | solution.py:581
  24.7 4.1 %collective-permute-start.7 = (bf16[192,128]{1,0:T(8,128)(2,1)S(1)}, bf16[192,128]{1,0:T(8,128)(2,1)S(1)}, u32[]{:S(2)}, u32[]{:S(2)}) collective-permute-start(bf16[192,128]{1,0:T(8,128)(2,1)S(1)} %get-tuple-element.51), channel_id=1, source_target_pairs={{0,12},{2,14},{4,0},{6,10},{8,4},{10,6},{12,8},{14,2},{1,13},{3,15... | collective-permute-start | bytes 147464 | tf_op jit(solution)/shard_map/ppermute | solution.py:581
  24.9 4.1 %collective-permute-start.8 = (bf16[192,128]{1,0:T(8,128)(2,1)S(1)}, bf16[192,128]{1,0:T(8,128)(2,1)S(1)}, u32[]{:S(2)}, u32[]{:S(2)}) collective-permute-start(bf16[192,128]{1,0:T(8,128)(2,1)S(1)} %get-tuple-element.52), channel_id=1, source_target_pairs={{0,2},{2,0},{4,6},{6,4},{8,10},{10,8},{12,14},{14,12},{1,3},{3,1},... | collective-permute-start | bytes 147464 | tf_op jit(solution)/shard_map/ppermute | solution.py:581

commit v9 on v8

--- a/solution.py
+++ b/solution.py
@@ -247,6 +247,10 @@
         o = pick(offset)
         slots[pl.ds(pl.multiple_of(o * size, size), size), :] = block[...].astype(F32)
     slots[NEIGHBOR_TILES * size :, :] = jnp.zeros((8, LANES), F32)
+    rows = HALO * FIELDS
+    for i in range(2):
+        bank[i * rows : i * rows + edge_rows.shape[1], :] = edge_rows[i]
+    bank[bank.shape[0] - rows :, :] = jnp.zeros((rows, LANES), BF16)
     pointers.wait()
     sub = iota((per_step, LANES), 0)
 
@@ -302,12 +306,10 @@
     still = HALO * (FIELDS - len(fields))
     lane = iota((tall, LANES), 1)
     for i, low in enumerate((False, True)):
-        bank[i * rows : i * rows + still, :] = edge_rows[i]
         bank[i * rows + still : (i + 1) * rows, :] = packed_rows(fields, low).astype(BF16)
         columns = packed_columns(fields, low, FIELDS - len(fields))
         columns = jnp.where(lane < still, edge_columns[i].astype(F32), columns)
         bank[2 * rows + i * tall : 2 * rows + (i + 1) * tall, :] = columns.astype(BF16)
-    bank[2 * rows + 2 * tall :, :] = jnp.zeros((rows, LANES), BF16)
     for offset, edge, out in zip(returns, edges, message_refs):
         first = pl.multiple_of(pick(offset) * groups, 16)
         out[0:groups, :] = homebound[pl.ds(first, groups), :]

time: 31.7 us -> 31.7 us (level)
  no operation moved by 1% of the time
where the time goes in v9:
time: 31.7 us; the launch traced here: 31.5 us
  starting transfers between devices  15.7 us (50%)
  Pallas kernels  10.9 us (34%)
  waiting for transfers between devices  4.34 us (14%)
  between operations  0.67 us (2%)
    ppermute x9, starting transfers between devices, send(): lax.ppermute(array, axes, [(a, b) for a, b in enumerate(targets) if b >= 0])  15.7 us
    pallas_call x1, Pallas kernels, shards(): pl.pallas_call(functools.partial(route_kernel, moves['sent'], total), out...  4.8 us
    ppermute x9, waiting for transfers between devices, send(): lax.ppermute(array, axes, [(a, b) for a, b in enumerate(targets) if b >= 0])  4.34 us
    pallas_call x1, Pallas kernels, shards(): pl.pallas_call(functools.partial(finish_kernel, moves['sources'], moves['...  2.56 us
    pallas_call x1, Pallas kernels, shards(): pl.pallas_call(functools.partial(remap_kernel, moves['came'], moves['retu...  2.53 us
    pallas_call x1, Pallas kernels, shards(): pl.pallas_call(functools.partial(prepare_kernel, total), out_shape=[jax.S...  1 us
  transfers between devices with their start and end apart: 9, of which 6 were waited for; matrix products, arithmetic and copies ran while one was open for 0% of the time, Pallas kernels for 3%

profile of v9, /device:TPU:0, one launch (start us, length us, event | category | flops | bytes accessed | tf_op | source)
XLA Modules:
  0.0 31.5 jit_solution(16787917447300175384)
XLA Ops:
  0.6 4.8 %route.1 = (bf16[256,128]{1,0:T(8,128)(2,1)S(1)}, bf16[256,128]{1,0:T(8,128)(2,1)S(1)}, bf16[256,128]{1,0:T(8,128)(2,1)S(1)}, bf16[256,128]{1,0:T(8,128)(2,1)S(1...) custom-call(bf16[8,16384]{1,0:T(8,128)(2,1)} %bitcast.13, ...), custom_call_target="tpu_custom_call" | custom-call | tf_op jit(solution)/shard_map/route/pallas_call | solution.py:562
  5.4 3.1 %collective-permute-start = (bf16[256,128]{1,0:T(8,128)(2,1)S(1)}, bf16[256,128]{1,0:T(8,128)(2,1)S(1)}, u32[]{:S(2)}, u32[]{:S(2)}) collective-permute-start(bf16[256,128]{1,0:T(8,128)(2,1)S(1)} %get-tuple-element.34), channel_id=1, source_target_pairs={{0,4},{2,6},{4,8},{6,2},{8,12},{10,14},{12,0},{14,10},{1,5},{3,7},... | collective-permute-start | bytes 196616 | tf_op jit(solution)/shard_map/ppermute | solution.py:583
  8.5 3.4 %collective-permute-start.1 = (bf16[256,128]{1,0:T(8,128)(2,1)S(1)}, bf16[256,128]{1,0:T(8,128)(2,1)S(1)}, u32[]{:S(2)}, u32[]{:S(2)}) collective-permute-start(bf16[256,128]{1,0:T(8,128)(2,1)S(1)} %get-tuple-element.35), channel_id=1, source_target_pairs={{0,14},{2,4},{4,2},{6,10},{8,6},{10,12},{12,8},{14,0},{1,15},{3,5}... | collective-permute-start | bytes 196616 | tf_op jit(solution)/shard_map/ppermute | solution.py:583
  11.9 0.6 %collective-permute-start.2 = (bf16[256,128]{1,0:T(8,128)(2,1)S(1)}, bf16[256,128]{1,0:T(8,128)(2,1)S(1)}, u32[]{:S(2)}, u32[]{:S(2)}) collective-permute-start(bf16[256,128]{1,0:T(8,128)(2,1)S(1)} %get-tuple-element.36), channel_id=1, source_target_pairs={{0,12},{2,14},{4,0},{6,8},{8,4},{10,6},{12,10},{14,2},{1,13},{3,15... | collective-permute-start | bytes 196616 | tf_op jit(solution)/shard_map/ppermute | solution.py:583
  12.6 1.2 %collective-permute-start.3 = (bf16[256,128]{1,0:T(8,128)(2,1)S(1)}, bf16[256,128]{1,0:T(8,128)(2,1)S(1)}, u32[]{:S(2)}, u32[]{:S(2)}) collective-permute-start(bf16[256,128]{1,0:T(8,128)(2,1)S(1)} %get-tuple-element.37), channel_id=1, source_target_pairs={{0,2},{2,0},{4,6},{6,4},{8,10},{10,8},{12,14},{14,12},{1,3},{3,1},... | collective-permute-start | bytes 196616 | tf_op jit(solution)/shard_map/ppermute | solution.py:583
  13.8 1.0 %prepare.1 = (bf16[320,128]{1,0:T(8,128)(2,1)S(1)}, bf16[2,80,128]{2,1,0:T(8,128)(2,1)S(1)}, bf16[2,64,128]{2,1,0:T(8,128)(2,1)S(1)}, s32[128,128]{1,0:T(8,128)S...) custom-call(s32[128,128]{1,0:T(8,128)S(1)} %get-tuple-element.39.des, ...), custom_call_target="tpu_custom_call" | custom-call | flops 62914560 | bytes 524288 | tf_op jit(solution)/shard_map/prepare/pallas_call | solution.py:586
  14.8 0.0 collective-permute-done.rest_1_
  14.8 1.6 %collective-permute-done.1.rest_2_ = bf16[256,128]{1,0:T(8,128)(2,1)S(1)} collective-permute-done((bf16[256,128]{1,0:T(8,128)(2,1)S(1)}, bf16[256,128]{1,0:T(8,128)(2,1)S(1)}, u32[]{:S(2)}, u32[]{:S(2)}) %collective-permute-start.1) | collective-permute-done | bytes 65568 | tf_op jit(solution)/shard_map/ppermute | solution.py:583
  16.4 0.0 collective-permute-done.2.rest_3_
  16.4 0.6 %collective-permute-done.3.rest_4_ = bf16[256,128]{1,0:T(8,128)(2,1)S(1)} collective-permute-done((bf16[256,128]{1,0:T(8,128)(2,1)S(1)}, bf16[256,128]{1,0:T(8,128)(2,1)S(1)}, u32[]{:S(2)}, u32[]{:S(2)}) %collective-permute-start.3) | collective-permute-done | bytes 65568 | tf_op jit(solution)/shard_map/ppermute | solution.py:583
  16.9 2.5 %remap.1 = (f32[3,64,128]{2,1,0:T(8,128)S(1)}, bf16[64,128]{1,0:T(8,128)(2,1)S(1)}, bf16[192,128]{1,0:T(8,128)(2,1)S(1)}, bf16[192,128]{1,0:T(8,128)(2,1)S(1)}, ...) custom-call(bf16[256,128]{1,0:T(8,128)(2,1)S(1)} %get-tuple-element.33.rest_0_, ...), custom_call_target="tpu_custom_call" | custom-call | tf_op jit(solution)/shard_map/remap/pallas_call | solution.py:604
  19.5 1.5 %collective-permute-start.4 = (bf16[192,128]{1,0:T(8,128)(2,1)S(1)}, bf16[192,128]{1,0:T(8,128)(2,1)S(1)}, u32[]{:S(2)}, u32[]{:S(2)}) collective-permute-start(bf16[192,128]{1,0:T(8,128)(2,1)S(1)} %get-tuple-element.48), channel_id=1, source_target_pairs={{0,6},{2,12},{4,10},{6,0},{8,14},{10,4},{12,2},{14,8},{1,7},{3,13}... | collective-permute-start | bytes 147464 | tf_op jit(solution)/shard_map/ppermute | solution.py:583
  21.0 0.5 %collective-permute-start.5 = (bf16[192,128]{1,0:T(8,128)(2,1)S(1)}, bf16[192,128]{1,0:T(8,128)(2,1)S(1)}, u32[]{:S(2)}, u32[]{:S(2)}) collective-permute-start(bf16[192,128]{1,0:T(8,128)(2,1)S(1)} %get-tuple-element.49), channel_id=1, source_target_pairs={{0,4},{2,6},{4,8},{6,2},{8,12},{10,14},{12,0},{14,10},{1,5},{3,7},... | collective-permute-start | bytes 147464 | tf_op jit(solution)/shard_map/ppermute | solution.py:583
  21.5 3.1 %collective-permute-start.6 = (bf16[192,128]{1,0:T(8,128)(2,1)S(1)}, bf16[192,128]{1,0:T(8,128)(2,1)S(1)}, u32[]{:S(2)}, u32[]{:S(2)}) collective-permute-start(bf16[192,128]{1,0:T(8,128)(2,1)S(1)} %get-tuple-element.50), channel_id=1, source_target_pairs={{0,14},{2,4},{4,2},{6,8},{8,6},{10,12},{12,10},{14,0},{1,15},{3,5}... | collective-permute-start | bytes 147464 | tf_op jit(solution)/shard_map/ppermute | solution.py:583
  24.6 0.3 collective-permute-start.7
  24.9 1.9 %collective-permute-start.8 = (bf16[192,128]{1,0:T(8,128)(2,1)S(1)}, bf16[192,128]{1,0:T(8,128)(2,1)S(1)}, u32[]{:S(2)}, u32[]{:S(2)}) collective-permute-start(bf16[192,128]{1,0:T(8,128)(2,1)S(1)} %get-tuple-element.52), channel_id=1, source_target_pairs={{0,2},{2,0},{4,6},{6,4},{8,10},{10,8},{12,14},{14,12},{1,3},{3,1},... | collective-permute-start | bytes 147464 | tf_op jit(solution)/shard_map/ppermute | solution.py:583
  26.8 0.0 collective-permute-done.4.rest_0_
  26.8 0.4 %collective-permute-done.5.rest_1_ = bf16[192,128]{1,0:T(8,128)(2,1)S(1)} collective-permute-done((bf16[192,128]{1,0:T(8,128)(2,1)S(1)}, bf16[192,128]{1,0:T(8,128)(2,1)S(1)}, u32[]{:S(2)}, u32[]{:S(2)}) %collective-permute-start.5) | collective-permute-done | bytes 49184 | tf_op jit(solution)/shard_map/ppermute | solution.py:583
  27.2 1.1 %collective-permute-done.6.rest_2_ = bf16[192,128]{1,0:T(8,128)(2,1)S(1)} collective-permute-done((bf16[192,128]{1,0:T(8,128)(2,1)S(1)}, bf16[192,128]{1,0:T(8,128)(2,1)S(1)}, u32[]{:S(2)}, u32[]{:S(2)}) %collective-permute-start.6) | collective-permute-done | bytes 49184 | tf_op jit(solution)/shard_map/ppermute | solution.py:583
  28.3 0.5 %collective-permute-done.7.rest_3_ = bf16[192,128]{1,0:T(8,128)(2,1)S(1)} collective-permute-done((bf16[192,128]{1,0:T(8,128)(2,1)S(1)}, bf16[192,128]{1,0:T(8,128)(2,1)S(1)}, u32[]{:S(2)}, u32[]{:S(2)}) %collective-permute-start.7) | collective-permute-done | bytes 49184 | tf_op jit(solution)/shard_map/ppermute | solution.py:583
  28.7 0.3 collective-permute-done.8.rest_4_
  29.0 2.6 %finish.1 = (f32[3,64,128]{2,1,0:T(8,128)}, f32[128,128]{1,0:T(8,128)}) custom-call(bf16[192,128]{1,0:T(8,128)(2,1)S(1)} %collective-permute-done.4.rest_0_, bf16[192,128]{1,0:T(8,128)(2,1)S(1)} %collective-permute-done.5.rest_1_, bf16[192,128]{1,0:T(8,128)(2,1)S(1)} %collective-permute-done.6.rest_2_, bf16[192,128]{1,0:T(8,128)(2,1)S(1)} %collective-permute-done.7.rest_3_, ...), custom_call_target="tpu_custom_call" | custom-call | tf_op jit(solution)/shard_map/finish/pallas_call | solution.py:627
Async XLA Ops:
  5.4 9.4 %collective-permute-start = (bf16[256,128]{1,0:T(8,128)(2,1)S(1)}, bf16[256,128]{1,0:T(8,128)(2,1)S(1)}, u32[]{:S(2)}, u32[]{:S(2)}) collective-permute-start(bf16[256,128]{1,0:T(8,128)(2,1)S(1)} %get-tuple-element.34), channel_id=1, source_target_pairs={{0,4},{2,6},{4,8},{6,2},{8,12},{10,14},{12,0},{14,10},{1,5},{3,7},... | collective-permute-start | bytes 196616 | tf_op jit(solution)/shard_map/ppermute | solution.py:583
  8.5 7.9 %collective-permute-start.1 = (bf16[256,128]{1,0:T(8,128)(2,1)S(1)}, bf16[256,128]{1,0:T(8,128)(2,1)S(1)}, u32[]{:S(2)}, u32[]{:S(2)}) collective-permute-start(bf16[256,128]{1,0:T(8,128)(2,1)S(1)} %get-tuple-element.35), channel_id=1, source_target_pairs={{0,14},{2,4},{4,2},{6,10},{8,6},{10,12},{12,8},{14,0},{1,15},{3,5}... | collective-permute-start | bytes 196616 | tf_op jit(solution)/shard_map/ppermute | solution.py:583
  11.9 4.5 %collective-permute-start.2 = (bf16[256,128]{1,0:T(8,128)(2,1)S(1)}, bf16[256,128]{1,0:T(8,128)(2,1)S(1)}, u32[]{:S(2)}, u32[]{:S(2)}) collective-permute-start(bf16[256,128]{1,0:T(8,128)(2,1)S(1)} %get-tuple-element.36), channel_id=1, source_target_pairs={{0,12},{2,14},{4,0},{6,8},{8,4},{10,6},{12,10},{14,2},{1,13},{3,15... | collective-permute-start | bytes 196616 | tf_op jit(solution)/shard_map/ppermute | solution.py:583
  12.6 4.4 %collective-permute-start.3 = (bf16[256,128]{1,0:T(8,128)(2,1)S(1)}, bf16[256,128]{1,0:T(8,128)(2,1)S(1)}, u32[]{:S(2)}, u32[]{:S(2)}) collective-permute-start(bf16[256,128]{1,0:T(8,128)(2,1)S(1)} %get-tuple-element.37), channel_id=1, source_target_pairs={{0,2},{2,0},{4,6},{6,4},{8,10},{10,8},{12,14},{14,12},{1,3},{3,1},... | collective-permute-start | bytes 196616 | tf_op jit(solution)/shard_map/ppermute | solution.py:583
  19.5 7.3 %collective-permute-start.4 = (bf16[192,128]{1,0:T(8,128)(2,1)S(1)}, bf16[192,128]{1,0:T(8,128)(2,1)S(1)}, u32[]{:S(2)}, u32[]{:S(2)}) collective-permute-start(bf16[192,128]{1,0:T(8,128)(2,1)S(1)} %get-tuple-element.48), channel_id=1, source_target_pairs={{0,6},{2,12},{4,10},{6,0},{8,14},{10,4},{12,2},{14,8},{1,7},{3,13}... | collective-permute-start | bytes 147464 | tf_op jit(solution)/shard_map/ppermute | solution.py:583
  21.0 6.2 %collective-permute-start.5 = (bf16[192,128]{1,0:T(8,128)(2,1)S(1)}, bf16[192,128]{1,0:T(8,128)(2,1)S(1)}, u32[]{:S(2)}, u32[]{:S(2)}) collective-permute-start(bf16[192,128]{1,0:T(8,128)(2,1)S(1)} %get-tuple-element.49), channel_id=1, source_target_pairs={{0,4},{2,6},{4,8},{6,2},{8,12},{10,14},{12,0},{14,10},{1,5},{3,7},... | collective-permute-start | bytes 147464 | tf_op jit(solution)/shard_map/ppermute | solution.py:583
  21.5 6.8 %collective-permute-start.6 = (bf16[192,128]{1,0:T(8,128)(2,1)S(1)}, bf16[192,128]{1,0:T(8,128)(2,1)S(1)}, u32[]{:S(2)}, u32[]{:S(2)}) collective-permute-start(bf16[192,128]{1,0:T(8,128)(2,1)S(1)} %get-tuple-element.50), channel_id=1, source_target_pairs={{0,14},{2,4},{4,2},{6,8},{8,6},{10,12},{12,10},{14,0},{1,15},{3,5}... | collective-permute-start | bytes 147464 | tf_op jit(solution)/shard_map/ppermute | solution.py:583
  24.6 4.1 %collective-permute-start.7 = (bf16[192,128]{1,0:T(8,128)(2,1)S(1)}, bf16[192,128]{1,0:T(8,128)(2,1)S(1)}, u32[]{:S(2)}, u32[]{:S(2)}) collective-permute-start(bf16[192,128]{1,0:T(8,128)(2,1)S(1)} %get-tuple-element.51), channel_id=1, source_target_pairs={{0,12},{2,14},{4,0},{6,10},{8,4},{10,6},{12,8},{14,2},{1,13},{3,15... | collective-permute-start | bytes 147464 | tf_op jit(solution)/shard_map/ppermute | solution.py:583
  24.9 4.1 %collective-permute-start.8 = (bf16[192,128]{1,0:T(8,128)(2,1)S(1)}, bf16[192,128]{1,0:T(8,128)(2,1)S(1)}, u32[]{:S(2)}, u32[]{:S(2)}) collective-permute-start(bf16[192,128]{1,0:T(8,128)(2,1)S(1)} %get-tuple-element.52), channel_id=1, source_target_pairs={{0,2},{2,0},{4,6},{6,4},{8,10},{10,8},{12,14},{14,12},{1,3},{3,1},... | collective-permute-start | bytes 147464 | tf_op jit(solution)/shard_map/ppermute | solution.py:583
